TPU v7x, 32 devices: a whole 2x2x4 slice. The times are simulated.
32 devices in a mesh: section: 2 (over core), dp: 4 (over z), expert: 4 (over y, x).
Axes of the slice: x: 2, y: 2, z: 4, core: 2. Of those that a mesh axis runs over, the one named last changes fastest.
Arguments:
- inputs: bfloat16 [2, 4, 1024, 768], P(None, 'expert', 'dp'), may hold values from -6 to 6
- cotangent: bfloat16 [2, 4, 1024, 768], P(None, 'expert', 'dp'), may hold values from -6 to 6
- lengths: int32 [8, 3], replicated, may hold values from 1 to 896, 1024 in all within a row
- deal: int32 [8], replicated, may hold values from 0 to 7, each once
- routes: int32 [2, 4, 1024, 2], P(None, 'expert', 'dp'), may hold values from 0 to 3, all different within a row; in each aligned block of 256 rows (0 to 255, 256 to 511, ..., all dimensions but the last counted through in order) at most 192 rows name the same one
- order: int32 [2, 4, 2048], P(None, 'expert', 'dp'), may hold values from 0 to 511, as said below
- gains: bfloat16 [2, 2, 768], P('section', None, 'expert'), may hold values from 0.5 to 1.5
- w_qkv: bfloat16 [2, 768, 2304], P('section', 'expert'), may hold values from -0.21875 to 0.21875
- w_out: bfloat16 [2, 768, 768], P('section', 'expert'), may hold values from -1.75 to 1.75
- w_router: bfloat16 [2, 768, 4], P('section', 'expert'), may hold values from -0.21875 to 0.21875
- w_shared_in: bfloat16 [2, 768, 4096], P('section', 'expert'), may hold values from -0.21875 to 0.21875
- w_shared_down: bfloat16 [2, 2048, 768], P('section', 'expert'), may hold values from -0.125 to 0.125
- w_expert_in: bfloat16 [2, 4, 768, 4096], P('section', 'expert'), may hold values from -0.21875 to 0.21875
- w_expert_down: bfloat16 [2, 4, 2048, 768], P('section', 'expert'), may hold values from -0.125 to 0.125
Outputs:
- section_out: bfloat16 [2, 2, 4, 1024, 768], P('section', None, 'expert', 'dp')
- input_grad: float32 [2, 2, 4, 1024, 768], P('section', None, 'expert', 'dp')
- grad_gains: float32 [2, 2, 768], P('section', None, 'expert')
- grad_qkv: float32 [2, 768, 2304], P('section', 'expert')
- grad_out: float32 [2, 768, 768], P('section', 'expert')
- grad_router: float32 [2, 768, 4], P('section', 'expert')
- grad_shared_in: float32 [2, 768, 4096], P('section', 'expert')
- grad_shared_down: float32 [2, 2048, 768], P('section', 'expert')
- grad_expert_in: float32 [2, 4, 768, 4096], P('section', 'expert')
- grad_expert_down: float32 [2, 4, 2048, 768], P('section', 'expert')
Inputs may be any that keep to these rules, and one draw needn't show every extreme that they name: Row r of lengths holds the lengths of 3 sequences laid end to end in a pack of 1024 tokens; the longest of each row is 896. A permutation; pack j of micro-batch m takes row deal[m * 4 + j] of lengths. `routes`: each token names two different experts; in each aligned block of 256 positions of a pack no expert is named more than 192 times. `order`: each aligned block of 512 entries (one block's pairs, token-major) is a permutation; a lower value is slotted first.
All inputs are finite; a program needn't handle non-finite values.
Results may differ from a plain program's by a relative error of at most 0.028.
Values may be sent and summed in bfloat16 or wider, within the bound.
No kernel may reach another device: no remote copies, remote signals or barrier semaphores. Data moves between devices by JAX's collectives and lax.ppermute only.
A program may use at most 320 MiB of HBM per device.

v0:
```python
import functools
import jax
import jax.numpy as jnp
from jax import lax
from jax.experimental import pallas as pl
from jax.experimental.pallas import tpu as pltpu
from jax.sharding import PartitionSpec as P

HEADS = 12
HEAD = 64
FF = 2048
EPS = 1e-06

SEC, DP, EXP = "section", "dp", "expert"
BF, F32, I32 = jnp.bfloat16, jnp.float32, jnp.int32
SWAP = [(0, 1), (1, 0)]


def mm(a, b, ca=1, cb=0, out=F32):
    r = lax.dot_general(a, b, (((ca,), (cb,)), ((), ())), preferred_element_type=F32)
    return r.astype(out)


def swap_cores(v):
    return lax.ppermute(v, SEC, SWAP)


def a2a(v, axis):
    return lax.all_to_all(v, axis, split_axis=0, concat_axis=0, tiled=True)


def gather(v, axis):
    return lax.all_gather(v, axis, axis=0, tiled=True)


def xor_pairs(count, k):
    return [(i, i ^ k) for i in range(count)]


def gather_blocks(v, members):
    return [v] + [lax.ppermute(v, EXP, xor_pairs(members, k)) for k in range(1, members)]


def scatter_blocks(blocks):
    count = len(blocks)
    return [blocks[0]] + [lax.ppermute(blocks[k], EXP, xor_pairs(count, k)) for k in range(1, count)]


def half_of(v, which, axis=0):
    size = v.shape[axis] // 2
    return lax.dynamic_slice_in_dim(v, which * size, size, axis)


def by_core(core, first, second):
    return jnp.where(core == 0, first, second)


def norm_apply(values, gain):
    scale = lax.rsqrt(jnp.mean(values * values, axis=-1, keepdims=True) + EPS)
    return (values * scale * gain).astype(BF), scale


def norm_backward(grad_hidden, values, scale, gain):
    normed = values * scale
    grad_gain = jnp.sum(grad_hidden * normed, axis=0)
    grad_normed = grad_hidden * gain
    grad_values = scale * (
        grad_normed - normed * jnp.mean(grad_normed * normed, axis=-1, keepdims=True)
    )
    return grad_values, grad_gain


def silu(v):
    return v * jax.nn.sigmoid(v)


def silu_parts(v):
    logistic = jax.nn.sigmoid(v)
    return v * logistic, logistic * (1.0 + v * (1.0 - logistic))


def block_mask(ends_ref, first_row, rows, cols):
    q = first_row + lax.broadcasted_iota(I32, (rows, cols), 0)
    k = lax.broadcasted_iota(I32, (rows, cols), 1)
    start = jnp.zeros((rows, cols), I32)
    for i in range(ends_ref.shape[0]):
        end = ends_ref[i]
        start = jnp.where(q >= end, end, start)
    return (k <= q) & (k >= start)


def head_slices(ref, rows, head, per, parts):
    return [ref[rows, (part * per + head) * HEAD : (part * per + head + 1) * HEAD] for part in parts]


def block_probs(q, k, mask):
    scores = lax.dot_general(q, k, (((1,), (1,)), ((), ())), preferred_element_type=F32)
    scores = jnp.where(mask, scores * (HEAD**-0.5), -1e30)
    raised = jnp.exp(scores - jnp.max(scores, axis=-1, keepdims=True))
    return raised / jnp.sum(raised, axis=-1, keepdims=True)


def attention_forward_kernel(block, per, ends_ref, qkv_ref, out_ref):
    pack = qkv_ref.shape[0]
    for i in range(pack // block):
        rows, reach = slice(i * block, (i + 1) * block), slice(0, (i + 1) * block)
        mask = block_mask(ends_ref, i * block, block, (i + 1) * block)
        for head in range(per):
            (q,) = head_slices(qkv_ref, rows, head, per, (0,))
            k, v = head_slices(qkv_ref, reach, head, per, (1, 2))
            probs = block_probs(q, k, mask).astype(BF)
            mixed = jnp.dot(probs, v, preferred_element_type=F32)
            out_ref[rows, head * HEAD : (head + 1) * HEAD] = mixed.astype(BF)


def attention_backward_kernel(block, per, ends_ref, qkv_ref, grad_ref, out_ref, dk_ref, dv_ref):
    pack = qkv_ref.shape[0]
    dk_ref[...] = jnp.zeros_like(dk_ref)
    dv_ref[...] = jnp.zeros_like(dv_ref)
    for i in range(pack // block):
        rows, reach = slice(i * block, (i + 1) * block), slice(0, (i + 1) * block)
        mask = block_mask(ends_ref, i * block, block, (i + 1) * block)
        for head in range(per):
            (q,) = head_slices(qkv_ref, rows, head, per, (0,))
            k, v = head_slices(qkv_ref, reach, head, per, (1, 2))
            grad = grad_ref[rows, head * HEAD : (head + 1) * HEAD]
            probs = block_probs(q, k, mask)
            dprobs = lax.dot_general(grad, v, (((1,), (1,)), ((), ())), preferred_element_type=F32)
            delta = jnp.sum(probs * dprobs, axis=-1, keepdims=True)
            dscores = (probs * (dprobs - delta)).astype(BF)
            dq = jnp.dot(dscores, k, preferred_element_type=F32) * (HEAD**-0.5)
            out_ref[rows, head * HEAD : (head + 1) * HEAD] = dq.astype(BF)
            over_queries = (((0,), (0,)), ((), ()))
            dk_ref[head, reach, :] += lax.dot_general(
                dscores, q, over_queries, preferred_element_type=F32
            )
            dv_ref[head, reach, :] += lax.dot_general(
                probs.astype(BF), grad, over_queries, preferred_element_type=F32
            )
    for head in range(per):
        at = (per + head) * HEAD
        out_ref[:, at : at + HEAD] = (dk_ref[head] * (HEAD**-0.5)).astype(BF)
        at = (2 * per + head) * HEAD
        out_ref[:, at : at + HEAD] = dv_ref[head].astype(BF)


def vmem():
    return pl.BlockSpec(memory_space=pltpu.VMEM)


def attention_forward(ends, qkv, block):
    pack, columns = qkv.shape
    per = columns // (3 * HEAD)
    return pl.pallas_call(
        functools.partial(attention_forward_kernel, block, per),
        out_shape=jax.ShapeDtypeStruct((pack, per * HEAD), BF),
        in_specs=[pl.BlockSpec(memory_space=pltpu.SMEM), vmem()],
        out_specs=vmem(),
        compiler_params=pltpu.CompilerParams(vmem_limit_bytes=32 << 20),
        cost_estimate=pl.CostEstimate(
            flops=4 * per * pack * pack * HEAD, bytes_accessed=8 * pack * columns // 3, transcendentals=per * pack * pack
        ),
    )(ends, qkv)


def attention_backward(ends, qkv, grad, block):
    pack, columns = qkv.shape
    per = columns // (3 * HEAD)
    return pl.pallas_call(
        functools.partial(attention_backward_kernel, block, per),
        out_shape=jax.ShapeDtypeStruct((pack, columns), BF),
        in_specs=[pl.BlockSpec(memory_space=pltpu.SMEM), vmem(), vmem()],
        out_specs=vmem(),
        scratch_shapes=[pltpu.VMEM((per, pack, HEAD), F32)] * 2,
        compiler_params=pltpu.CompilerParams(vmem_limit_bytes=32 << 20),
        cost_estimate=pl.CostEstimate(
            flops=10 * per * pack * pack * HEAD, bytes_accessed=16 * pack * columns // 3, transcendentals=per * pack * pack
        ),
    )(ends, qkv, grad)


def section_weights(core, members, parts):
    gains, w_qkv, w_out, w_router, w_shared_in, w_shared_down, w_expert_in, w_expert_down = parts

    def both(mine):
        other = swap_cores(mine)
        return by_core(core, mine, other), by_core(core, other, mine)

    me = lax.axis_index(EXP)

    def shares(shard):
        mine, theirs = half_of(shard, core), half_of(shard, 1 - core)
        other = swap_cores(theirs)
        return by_core(core, mine, other), by_core(core, other, mine)

    def both_halves(full):
        blocks, rows, columns = full.shape
        other = swap_cores(full)
        halves = [by_core(core, full, other), by_core(core, other, full)]
        return jnp.stack(halves, axis=1).reshape(blocks * 2 * rows, columns)

    def permuted(part):
        blocks = jnp.stack(gather_blocks(part, members))
        return jnp.concatenate(
            [lax.dynamic_slice_in_dim(blocks, me ^ j, 1, 0) for j in range(members)]
        )

    rows, width = w_out.shape
    experts = w_router.shape[1]
    extra = experts + 2
    pad = -(-extra // 128) * 128 - extra
    small = jnp.concatenate([w_router, gains.T, jnp.zeros((rows, pad), BF)], axis=1)
    qkv_0, qkv_1 = shares(w_qkv)
    rest_0, rest_1 = shares(jnp.concatenate([w_out, small], axis=1))
    qkv_0 = both_halves(permuted(qkv_0))
    rest_0, _ = lax.optimization_barrier((rest_0, qkv_0))
    rest_0 = both_halves(permuted(rest_0))
    later, _ = lax.optimization_barrier((jnp.concatenate([qkv_1, rest_1], axis=1), qkv_0))
    dense_1 = both_halves(lax.all_gather(later, EXP))
    qkv = (qkv_0, dense_1[:, : 3 * width])
    rest = (rest_0, dense_1[:, 3 * width :])
    quarter = FF // members
    split = w_shared_in.reshape(rows, 2, members, quarter).transpose(2, 0, 1, 3)
    split = split.reshape(members, rows, 2 * quarter)
    shared_in = both(a2a(split, EXP).reshape(members * rows, 2 * quarter))
    shared_down = both(w_shared_down)
    expert_in = both(w_expert_in)
    expert_down = both(w_expert_down)
    return [
        (
            rest[s][:, width + experts : width + experts + 2].T.astype(F32),
            qkv[s],
            rest[s][:, :width],
            rest[s][:, width : width + experts],
            shared_in[s],
            shared_down[s],
            expert_in[s],
            expert_down[s],
        )
        for s in range(2)
    ]


def to_heads(v, lanes, parts):
    tokens, columns = v.shape
    per = columns // (parts * lanes)
    split = v.reshape(tokens, parts, lanes, per).transpose(2, 0, 1, 3).reshape(lanes, tokens, parts * per)
    return a2a(split, DP).reshape(lanes * tokens, parts * per)


def to_tokens(v, lanes, parts):
    pack, columns = v.shape
    tokens, per = pack // lanes, columns // parts
    got = a2a(v.reshape(lanes, tokens, columns), DP).reshape(lanes, tokens, parts, per)
    return got.transpose(1, 2, 0, 3).reshape(tokens, lanes * columns)


def layer_forward(current, context, weights):
    ends, chosen_all, slots, lanes, members, block = context
    gain, w_qkv, w_out, w_router, w_sin, w_sdown, w_ein, w_edown = weights
    tokens, width = current.shape
    hidden_one, scale_one = norm_apply(current, gain[0])
    qkv_heads = to_heads(mm(hidden_one, w_qkv, out=BF), lanes, 3)
    mixed = to_tokens(attention_forward(ends, qkv_heads, block), lanes, 1)
    middle = current + mm(mixed, w_out)
    hidden_two, scale_two = norm_apply(middle, gain[1])
    hidden_all = jnp.concatenate(gather_blocks(hidden_two, members))
    logits = mm(hidden_all, w_router)
    raised = jnp.exp(logits - jnp.max(logits, axis=-1, keepdims=True))
    router = raised / jnp.sum(raised, axis=-1, keepdims=True)
    both_picked = jnp.sum(router * chosen_all, axis=-1, keepdims=True)
    me = lax.axis_index(EXP)
    gate_here = lax.dynamic_slice_in_dim(router, me, 1, 1) / both_picked
    rows = mm(slots, hidden_all, out=BF)
    pre, act = branch(rows, w_ein, FF)
    result = mm(act, w_edown, out=BF)
    quarter = w_sdown.shape[0]
    shared_pre, shared_act = branch(hidden_all, w_sin, quarter)
    returned = mm(slots, result, 0, 0)
    partial = (gate_here * returned + mm(shared_act, w_sdown)).astype(BF)
    parts = scatter_blocks([partial[k * tokens : (k + 1) * tokens] for k in range(members)])
    output = middle + functools.reduce(jnp.add, [part.astype(F32) for part in parts])
    saved = (
        current, scale_one, hidden_one, qkv_heads, mixed, middle, scale_two, hidden_two, hidden_all,
        router, both_picked, gate_here, rows, pre, act, returned.astype(BF), shared_pre, shared_act,
    )
    return output, saved


def branch(rows, w_in, units):
    gate, up = mm(rows, w_in[:, :units], out=BF), mm(rows, w_in[:, units:], out=BF)
    return (gate, up), (silu(gate.astype(F32)) * up.astype(F32)).astype(BF)


def silu_grads(pre, grad_act):
    up = pre[1].astype(F32)
    value, slope = silu_parts(pre[0].astype(F32))
    return jnp.concatenate([grad_act * up * slope, grad_act * value], axis=1).astype(BF)


def layer_backward(grad_low, saved, context, weights):
    ends, chosen_all, slots, lanes, members, block = context
    gain, w_qkv, w_out, w_router, w_sin, w_sdown, w_ein, w_edown = weights
    (
        current, scale_one, hidden_one, qkv_heads, mixed, middle, scale_two, hidden_two, hidden_all,
        router_all, picked_all, gate_here, rows, pre, act, returned, shared_pre, shared_act,
    ) = saved
    tokens, width = current.shape
    core, me = lax.axis_index(SEC), lax.axis_index(EXP)
    grad_out = grad_low.astype(F32)
    grad_all = jnp.concatenate(gather_blocks(grad_low, members))
    wide = grad_all.astype(F32)
    dy = mm(slots, (gate_here * wide).astype(BF), out=BF)
    dgate = jnp.sum(wide * returned.astype(F32), axis=-1)
    dpre = silu_grads(pre, mm(dy, w_edown, 1, 1))
    drows = mm(dpre, w_ein, 1, 1, out=BF)
    dshared = silu_grads(shared_pre, mm(grad_all, w_sdown, 1, 1))
    partial = (mm(slots, drows, 0, 0) + mm(dshared, w_sin, 1, 1)).astype(BF)
    high = dgate.astype(BF)
    low = (dgate - high.astype(F32)).astype(BF)
    lines = -(-2 * tokens // (16 * width)) * 16
    blocks = []
    for k in range(members):
        own = slice(k * tokens, (k + 1) * tokens)
        pair = jnp.pad(jnp.concatenate([high[own], low[own]]), (0, lines * width - 2 * tokens))
        blocks.append(jnp.concatenate([partial[own], pair.reshape(lines, width)]))
    parts = scatter_blocks(blocks)
    dh2 = functools.reduce(jnp.add, [part[:tokens].astype(F32) for part in parts])
    gates = jnp.stack([part[tokens:].reshape(-1)[: 2 * tokens].astype(F32) for part in parts])
    gates = gates[:, :tokens] + gates[:, tokens:]
    column = jnp.arange(members, dtype=I32)[None, :]
    dgates = sum(
        jnp.where(column == (me ^ k), gates[k][:, None], 0.0) for k in range(members)
    )
    router, chosen, picked = router_all[:tokens], chosen_all[:tokens], picked_all[:tokens]
    inner = jnp.sum(dgates * router * chosen, axis=-1, keepdims=True) / picked
    dprob = chosen * (dgates - inner) / picked
    dlogits = (router * (dprob - jnp.sum(router * dprob, axis=-1, keepdims=True))).astype(BF)
    dh2 = dh2 + mm(dlogits, w_router, 1, 1)
    dmiddle_norm, dgain_two = norm_backward(dh2, middle, scale_two, gain[1])
    dmiddle = grad_out + dmiddle_norm
    dattn = dmiddle.astype(BF)
    dmixed = to_heads(mm(dattn, w_out, 1, 1, out=BF), lanes, 1)
    dqkv = to_tokens(attention_backward(ends, qkv_heads, dmixed, block), lanes, 3)
    dh1 = mm(dqkv, w_qkv, 1, 1)
    dinput_norm, dgain_one = norm_backward(dh1, current, scale_one, gain[0])
    grad_input = dmiddle + dinput_norm

    def halves(rows_of, grads):
        send = mm(half_of(rows_of, 1 - core, 1), grads, 0, 0, out=BF)
        keep = mm(half_of(rows_of, core, 1), grads, 0, 0)
        return (keep + swap_cores(send).astype(F32)).astype(BF)

    def halves_by_member(rows_of, grads):
        split = rows_of.reshape(rows_of.shape[0], members, 2, -1)

        def side(which):
            return lax.dynamic_index_in_dim(split, which, 2, False).reshape(rows_of.shape[0], -1)

        send = mm(side(1 - core), grads, 0, 0, out=BF)
        keep = mm(side(core), grads, 0, 0)
        return (keep + swap_cores(send).astype(F32)).astype(BF).reshape(members, -1, grads.shape[1])

    def small_halves(grad):
        split = grad.reshape(members, 2, -1, grad.shape[1])
        send = lax.dynamic_index_in_dim(split, 1 - core, 1, False).astype(BF)
        keep = lax.dynamic_index_in_dim(split, core, 1, False)
        return (keep + swap_cores(send).astype(F32)).astype(BF)

    def summed(parts):
        return jnp.sum(a2a(parts, EXP).astype(F32), axis=0).astype(BF)

    g_down = halves(act, dy)
    g_in = halves(rows, dpre)
    g_sdown = halves(shared_act, grad_all)
    g_sin = a2a(halves_by_member(hidden_all, dshared), EXP)
    extra = w_router.shape[1] + 2
    pad = -(-extra // 128) * 128 - extra
    small = jnp.concatenate(
        [
            mm(hidden_two, dlogits, 0, 0),
            jnp.stack([dgain_one, dgain_two], axis=1),
            jnp.zeros((width, pad), F32),
        ],
        axis=1,
    )
    g_out = halves_by_member(mixed, dattn)
    g_dense = summed(
        jnp.concatenate([halves_by_member(hidden_one, dqkv), g_out, small_halves(small)], axis=2)
    )
    return grad_input, (g_down, g_in, g_sdown, g_sin, g_dense)


def over_lanes(chunks):
    lane = lax.axis_index(DP)
    middle = (lane == 1) | (lane == 2)

    def add(a, b):
        return (a.astype(F32) + b.astype(F32)).astype(BF)

    arrived, result = [], []
    for k, chunk in enumerate(chunks):
        if k >= 2:
            chunk, _ = lax.optimization_barrier((chunk, arrived[k - 2]))
        arrived.append(lax.ppermute(chunk, DP, [(0, 1), (3, 2)]))
        part = add(chunk, arrived[k])
        total = add(part, lax.ppermute(part, DP, [(1, 2), (2, 1)]))
        result.append(jnp.where(middle, total, lax.ppermute(total, DP, [(1, 0), (2, 3)])))
    return result


def lane_sums(groups):
    done, last = [], None
    for group in groups:
        if last is not None:
            group, _ = lax.optimization_barrier((group, last))
        sums = lax.psum(tuple(group), DP)
        last = sums[0]
        done.append(tuple(sums))
    return done[0] + done[1], done[2] + done[3]


def local(
    inputs, cotangent, lengths, deal, routes, order, gains, w_qkv, w_out, w_router, w_shared_in, w_shared_down,
    w_expert_in, w_expert_down,
):
    core, me, lane = lax.axis_index(SEC), lax.axis_index(EXP), lax.axis_index(DP)
    members, lanes = lax.axis_size(EXP), lax.axis_size(DP)
    batches, _, tokens, width = inputs.shape
    experts = w_router.shape[2]
    assert batches == lax.axis_size(SEC) == 2 and w_expert_in.shape[1] == 1 and experts == members
    weights = section_weights(
        core,
        members,
        (
            gains[0], w_qkv[0], w_out[0], w_router[0], w_shared_in[0], w_shared_down[0],
            w_expert_in[0, 0], w_expert_down[0, 0],
        ),
    )
    row = lax.dynamic_index_in_dim(deal, core * members + me, 0, False)
    ends = jnp.cumsum(lax.dynamic_index_in_dim(lengths, row, 0, False))[:-1].astype(I32)
    pairs = lax.dynamic_index_in_dim(routes[:, 0], core, 0, False).reshape(-1)
    places = lax.dynamic_index_in_dim(order[:, 0], core, 0, False)
    same = pairs[:, None] == pairs[None, :]
    rank = jnp.sum((same & (places[None, :] < places[:, None])).astype(I32), axis=1)
    code = jnp.stack(gather_blocks(pairs * (2 * tokens) + rank, members))
    owner = me ^ jnp.arange(members, dtype=I32)
    pairs_all, rank_all = code // (2 * tokens), code % (2 * tokens)
    onehot = (pairs_all[:, :, None] == jnp.arange(experts, dtype=I32)).astype(I32)
    counts = jnp.sum(onehot, axis=1)
    lower = (owner[None, :] < owner[:, None]).astype(I32)
    before = jnp.sum(lower[:, :, None] * counts[None], axis=1)
    place = jnp.sum(onehot * before[:, None, :], axis=2) + rank_all
    capacity = 2 * tokens * members // experts
    slot = jnp.where((pairs_all == me) & (place < capacity), place, -1)
    slot = jnp.max(slot.reshape(members * tokens, 2), axis=1)
    slots = (jnp.arange(capacity, dtype=I32)[:, None] == slot[None, :]).astype(BF)
    chosen_all = jnp.sum(onehot.reshape(members * tokens, 2, experts), axis=1).astype(F32)
    context = (ends, chosen_all, slots, lanes, members, tokens)

    first_low = lax.dynamic_index_in_dim(inputs[:, 0], core, 0, False)
    grad_low = lax.dynamic_index_in_dim(cotangent[:, 0], core, 0, False)
    out_0, saved_0 = layer_forward(first_low.astype(F32), context, weights[0])
    low_0 = out_0.astype(BF)
    out_1, saved_1 = layer_forward(low_0.astype(F32), context, weights[1])
    low_1 = out_1.astype(BF)
    grad_1, terms_1 = layer_backward(grad_low, saved_1, context, weights[1])
    grad_0, terms_0 = layer_backward(grad_1.astype(BF), saved_0, context, weights[0])
    sum_1, sum_0 = lane_sums([terms_1[:2], terms_1[2:], terms_0[:2], terms_0[2:]])

    def to_section(of_0, of_1):
        mine = by_core(core, of_0, of_1)
        other = swap_cores(by_core(core, of_1, of_0))
        both = jnp.stack([by_core(core, mine, other), by_core(core, other, mine)])
        return both[None, :, None]

    def whole(half_0, half_1):
        got_1 = lax.ppermute(half_1, SEC, [(0, 1)])
        got_0 = lax.ppermute(half_0, SEC, [(1, 0)])
        return by_core(core, half_0, got_1).astype(F32), by_core(core, got_0, half_1).astype(F32)

    down, ein, sdown, sin, dense = [whole(a, b) for a, b in zip(sum_0, sum_1)]
    quarter = FF // members
    sin = jnp.concatenate(
        [
            h.reshape(members, -1, 2, quarter).transpose(1, 2, 0, 3).reshape(-1, 2 * FF) for h in sin
        ]
    )
    dense = jnp.concatenate(dense)
    at = 4 * width
    return (
        to_section(low_0, low_1),
        to_section(grad_0, grad_1),
        dense[:, at + experts : at + experts + 2].T[None],
        dense[None, :, : 3 * width],
        dense[None, :, 3 * width : at],
        dense[None, :, at : at + experts],
        sin[None],
        jnp.concatenate(sdown)[None],
        jnp.concatenate(ein)[None, None],
        jnp.concatenate(down)[None, None],
    )


def solution(mesh):
    tokens = P(None, EXP, DP, None)
    dense = P(SEC, EXP, None)
    expert = P(SEC, EXP, None, None)
    both = P(SEC, None, EXP, DP, None)
    gains = P(SEC, None, EXP)
    return jax.shard_map(
        local,
        mesh=mesh,
        in_specs=(tokens, tokens, P(), P(), tokens, P(None, EXP, DP), gains)
        + (dense,) * 5
        + (expert,) * 2,
        out_specs=(both, both, gains) + (dense,) * 5 + (expert,) * 2,
        check_vma=False,
    )
```

profile of v0, /device:TPU:1, one launch (start us, length us, event | category | flops | bytes accessed | tf_op | source)
XLA Modules:
  0.0 1226.0 jit_solution(10217761911797520373)
XLA Ops:
  15.6 10.0 collective-permute-done.4
  25.6 9.8 collective-permute-done.3
  66.7 4.7 all-to-all-start
  80.1 19.6 %all-to-all-done = bf16[4,256,576]{1,2,0:T(8,128)(2,1)} async-done(((bf16[4,256,576]{1,2,0:T(8,128)(2,1)}), bf16[4,256,576]{1,2,0:T(8,128)(2,1)}, u32[]{:S(2)}, u32[]{:S(2)}) %all-to-all-start) | async-done | bytes 1179680 | tf_op jit(solution)/shard_map/all_to_all | solution.py:29
  99.6 4.5 all-to-all-start.2
  110.4 12.3 %collective-permute-done.15 = s32[512]{0:T(512)S(1)} collective-permute-done((s32[512]{0:T(512)S(1)}, s32[512]{0:T(512)S(1)}, u32[]{:S(2)}, u32[]{:S(2)}) %collective-permute-start.15) | collective-permute-done | bytes 2080 | tf_op jit(solution)/shard_map/ppermute | solution.py:41
  128.9 6.7 shard_map.213
  156.4 4.4 collective-permute-start.19
  164.0 5.6 collective-permute-start.17
  169.6 6.9 collective-permute-done.11
  183.6 7.3 broadcast_select_fusion
  200.7 7.1 fusion.1
  207.8 8.7 fusion.67
  222.9 8.4 collective-permute-done.20
  231.3 8.5 collective-permute-done.22
  251.9 43.3 %all_to_all.65 = bf16[4,256,576]{1,2,0:T(8,128)(2,1)} all-to-all(bf16[4,256,576]{1,2,0:T(8,128)(2,1)S(1)} %bitcast.392), channel_id=1, replica_groups=mesh['section'=2,'dp'=4,'expert'=4] {'dp'}, dimensions={0} | all-to-all | bytes 2359296 | tf_op jit(solution)/shard_map/all_to_all | solution.py:29
  296.9 6.7 shard_map.214
  304.6 13.8 %all_to_all.66 = bf16[4,256,192]{1,2,0:T(8,128)(2,1)S(1)} all-to-all(bf16[4,256,192]{1,2,0:T(8,128)(2,1)} %copy.152), channel_id=1, replica_groups=mesh['section'=2,'dp'=4,'expert'=4] {'dp'}, dimensions={0} | all-to-all | bytes 786432 | tf_op jit(solution)/shard_map/all_to_all | solution.py:29
  324.9 5.1 collective-permute-done.26
  330.3 13.3 %collective-permute-done.25 = bf16[256,768]{1,0:T(8,128)(2,1)S(1)} collective-permute-done((bf16[256,768]{1,0:T(8,128)(2,1)S(1)}, bf16[256,768]{1,0:T(8,128)(2,1)S(1)}, u32[]{:S(2)}, u32[]{:S(2)}) %collective-permute-start.25) | collective-permute-done | bytes 393248 | tf_op jit(solution)/shard_map/ppermute | solution.py:41
  360.0 8.3 fusion.6
  368.3 11.1 fusion.63
  379.5 5.0 fusion.50
  388.5 8.0 fusion.18
  426.6 11.2 all_to_all.67
  439.0 12.0 shard_map.215
  454.5 4.6 all-to-all-start.6
  480.0 8.0 collective-permute-start.51
  505.3 9.5 collective-permute-done.38
  518.3 8.4 fusion.3
  526.8 11.2 fusion.61
  554.2 10.4 collective-permute-done.41
  573.5 4.8 all-to-all-start.7
  590.9 12.4 %shard_map.216 = bf16[1024,576]{1,0:T(8,128)(2,1)S(1)} custom-call(s32[2]{0:T(128)S(1)} %slice_bitcast_fusion.1.ends_ref, bf16[1024,576]{1,0:T(8,128)(2,1)S(1)} %bitcast.352, bf16[1024,192]{1,0:T(8,128)(2,1)S(1)} %bitcast.357), custom_call_target="tpu_custom_call" | custom-call | flops 2013265920 | bytes 3145728 | tf_op jit(solution)/shard_map/pallas_call | solution.py:169
  617.1 5.8 convolution_convert_fusion.1
  640.8 4.8 fusion.134
  654.1 4.6 all-to-all-start.12
  673.7 14.1 %all-to-all-done.12 = bf16[4,96,3200]{2,1,0:T(8,128)(2,1)} async-done(((bf16[4,96,3200]{2,1,0:T(8,128)(2,1)}), bf16[4,96,3200]{2,1,0:T(8,128)(2,1)}, u32[]{:S(2)}, u32[]{:S(2)}) %all-to-all-start.12) | async-done | bytes 2457632 | tf_op jit(solution)/shard_map/all_to_all | solution.py:29
  703.3 27.1 %all-reduce.12.cloned.1.call-done = bf16[1024,768]{1,0:T(8,128)(2,1)} async-done(((bf16[1024,768]{1,0:T(8,128)(2,1)}), bf16[1024,768]{1,0:T(8,128)(2,1)}) %all-reduce.12.cloned.1.call-update) | async-done | bytes 1572880 | tf_op jit(solution)/shard_map/psum | solution.py:417
  730.4 6.8 add_convert_fusion.1
  737.3 31.2 %all-reduce.14.cloned.1.call-done = bf16[256,768]{1,0:T(8,128)(2,1)} async-done(((bf16[256,768]{1,0:T(8,128)(2,1)}), bf16[256,768]{1,0:T(8,128)(2,1)}) %all-reduce.14.cloned.1.call-update) | async-done | bytes 393232 | tf_op jit(solution)/shard_map/psum | solution.py:417
  781.1 7.0 add_convert_fusion
  792.1 48.5 %all-reduce.16.cloned.1.call-done = bf16[1024,768]{1,0:T(8,128)(2,1)} async-done(((bf16[1024,768]{1,0:T(8,128)(2,1)}), bf16[1024,768]{1,0:T(8,128)(2,1)}) %all-reduce.16.cloned.1.call-update) | async-done | bytes 1572880 | tf_op jit(solution)/shard_map/psum | solution.py:417
  846.5 5.9 collective-permute-done.27
  852.4 9.4 collective-permute-done.29
  862.2 4.3 collective-permute-start.30
  876.9 299.3 %all-reduce.18.cloned.1.call-done = (bf16[96,3200]{1,0:T(8,128)(2,1)}, bf16[96,3200]{1,0:T(8,128)(2,1)}, bf16[4,96,1024]{2,1,0:T(8,128)(2,1)}, bf16[4,96,1024]{2...) async-done(((bf16[96,3200]{1,0:T(8,128)(2,1)}, bf16[96,3200]{1,0:T(8,128)(2,1)}, bf16[4,96,1024]{2,1,0:T(8,128)(2,1)}, ...) | async-done | bytes 9486352 | tf_op jit(solution)/shard_map/psum | solution.py:417
  1212.7 6.5 fusion
  (779 shorter events, 399.7 us)
Async XLA Ops:
  15.3 20.1 %collective-permute-start.3 = (bf16[96,2304]{1,0:T(8,128)(2,1)S(1)}, bf16[96,2304]{1,0:T(8,128)(2,1)S(1)}, u32[]{:S(2)}, u32[]{:S(2)}) collective-permute-start(bf16[96,2304]{1,0:T(8,128)(2,1)S(1)} %get-tuple-element.154), channel_id=1, source_target_pairs={{0,2},{1,3},{2,0},{3,1},{4,6},{5,7},{6,4},{7,5},{8,10},{9,11},{10,... | collective-permute-start | bytes 1327112 | tf_op jit(solution)/shard_map/ppermute | solution.py:41
  15.6 19.9 %collective-permute-start.2 = (bf16[96,2304]{1,0:T(8,128)(2,1)S(1)}, bf16[96,2304]{1,0:T(8,128)(2,1)S(1)}, u32[]{:S(2)}, u32[]{:S(2)}) collective-permute-start(bf16[96,2304]{1,0:T(8,128)(2,1)S(1)} %get-tuple-element.154), channel_id=1, source_target_pairs={{0,1},{1,0},{2,3},{3,2},{4,5},{5,4},{6,7},{7,6},{8,9},{9,8},{10,11... | collective-permute-start | bytes 1327112 | tf_op jit(solution)/shard_map/ppermute | solution.py:41
  66.7 32.9 %all-to-all-start = ((bf16[4,256,576]{1,2,0:T(8,128)(2,1)}), bf16[4,256,576]{1,2,0:T(8,128)(2,1)}, u32[]{:S(2)}, u32[]{:S(2)}) async-start(bf16[4,256,576]{1,2,0:T(8,128)(2,1)} %bitcast.28), calls=%async_computation | async-start | bytes 2359296 | tf_op jit(solution)/shard_map/all_to_all | solution.py:29
  71.4 112.0 %collective-permute-start.16 = (bf16[768,4096]{1,0:T(8,128)(2,1)}, bf16[768,4096]{1,0:T(8,128)(2,1)}, u32[]{:S(2)}, u32[]{:S(2)}) collective-permute-start(bf16[768,4096]{1,0:T(8,128)(2,1)} %bitcast.382), channel_id=1, source_target_pairs={{0,16},{16,0},{1,17},{17,1},{2,18},{18,2},{3,19},{19,3},{4,20},{20... | collective-permute-start | bytes 18874376 | tf_op jit(solution)/shard_map/ppermute | solution.py:25
  99.6 36.9 %all-to-all-start.2 = ((bf16[4,192,1024]{2,1,0:T(8,128)(2,1)}), bf16[4,192,1024]{2,1,0:T(8,128)(2,1)}, u32[]{:S(2)}, u32[]{:S(2)}) async-start(bf16[4,192,1024]{2,1,0:T(8,128)(2,1)} %reshape.659), calls=%async_computation.2 | async-start | bytes 3145728 | tf_op jit(solution)/shard_map/all_to_all | solution.py:29
  104.2 18.5 %collective-permute-start.15 = (s32[512]{0:T(512)S(1)}, s32[512]{0:T(512)S(1)}, u32[]{:S(2)}, u32[]{:S(2)}) collective-permute-start(s32[512]{0:T(512)S(1)} %multiply_add_fusion.2), channel_id=1, source_target_pairs={{0,3},{1,2},{2,1},{3,0},{4,7},{5,6},{6,5},{7,4},{8,11},{9,10},{10,... | collective-permute-start | bytes 6152 | tf_op jit(solution)/shard_map/ppermute | solution.py:41
  140.8 59.2 %all-gather.3.cloned.1.call-start = ((), (), s32[]{:S(2)}) async-start(), calls=%async_computation.16 | async-start | bytes 3072000 | tf_op jit(solution)/shard_map/all_gather | solution.py:219
  153.2 23.3 %collective-permute-start.11 = (bf16[256,768]{1,0:T(8,128)(2,1)}, bf16[256,768]{1,0:T(8,128)(2,1)}, u32[]{:S(2)}, u32[]{:S(2)}) collective-permute-start(bf16[256,768]{1,0:T(8,128)(2,1)} %multiply_convert_fusion.6), channel_id=1, source_target_pairs={{0,2},{1,3},{2,0},{3,1},{4,6},{5,7},{6,4},{7,5},{8,10},{9,11},{10,... | collective-permute-start | bytes 1179656 | tf_op jit(solution)/shard_map/ppermute | solution.py:41
  154.3 22.2 %collective-permute-start.10 = (bf16[256,768]{1,0:T(8,128)(2,1)}, bf16[256,768]{1,0:T(8,128)(2,1)}, u32[]{:S(2)}, u32[]{:S(2)}) collective-permute-start(bf16[256,768]{1,0:T(8,128)(2,1)} %multiply_convert_fusion.6), channel_id=1, source_target_pairs={{0,1},{1,0},{2,3},{3,2},{4,5},{5,4},{6,7},{7,6},{8,9},{9,8},{10,11... | collective-permute-start | bytes 1179656 | tf_op jit(solution)/shard_map/ppermute | solution.py:41
  156.4 60.1 %collective-permute-start.19 = (bf16[512,768]{1,0:T(8,128)(2,1)}, bf16[512,768]{1,0:T(8,128)(2,1)}, u32[]{:S(2)}, u32[]{:S(2)}) collective-permute-start(bf16[512,768]{1,0:T(8,128)(2,1)} %bitcast.395), channel_id=1, source_target_pairs={{0,16},{16,0},{1,17},{17,1},{2,18},{18,2},{3,19},{19,3},{4,20},{20... | collective-permute-start | bytes 2359304 | tf_op jit(solution)/shard_map/ppermute | solution.py:25
  164.0 43.8 %collective-permute-start.17 = (bf16[2048,768]{1,0:T(8,128)(2,1)}, bf16[2048,768]{1,0:T(8,128)(2,1)}, u32[]{:S(2)}, u32[]{:S(2)}) collective-permute-start(bf16[2048,768]{1,0:T(8,128)(2,1)} %bitcast.46), channel_id=1, source_target_pairs={{0,16},{16,0},{1,17},{17,1},{2,18},{18,2},{3,19},{19,3},{4,20},{20... | collective-permute-start | bytes 9437192 | tf_op jit(solution)/shard_map/ppermute | solution.py:25
  200.0 42.2 %collective-permute-start.23 = (bf16[4,96,3200]{2,1,0:T(8,128)(2,1)}, bf16[4,96,3200]{2,1,0:T(8,128)(2,1)}, u32[]{:S(2)}, u32[]{:S(2)}) collective-permute-start(bf16[4,96,3200]{2,1,0:T(8,128)(2,1)} %bitcast.399), channel_id=1, source_target_pairs={{0,16},{16,0},{1,17},{17,1},{2,18},{18,2},{3,19},{19,3},{4,20},{20... | collective-permute-start | bytes 7372808 | tf_op jit(solution)/shard_map/ppermute | solution.py:25
  221.4 18.4 %collective-permute-start.22 = (bf16[256,768]{1,0:T(8,128)(2,1)S(1)}, bf16[256,768]{1,0:T(8,128)(2,1)S(1)}, u32[]{:S(2)}, u32[]{:S(2)}) collective-permute-start(bf16[256,768]{1,0:T(8,128)(2,1)S(1)} %get-tuple-element.149), channel_id=1, source_target_pairs={{0,3},{1,2},{2,1},{3,0},{4,7},{5,6},{6,5},{7,4},{8,11},{9,10},{10,... | collective-permute-start | bytes 1179656 | tf_op jit(solution)/shard_map/ppermute | solution.py:46
  222.6 19.3 %collective-permute-start.21 = (bf16[256,768]{1,0:T(8,128)(2,1)S(1)}, bf16[256,768]{1,0:T(8,128)(2,1)S(1)}, u32[]{:S(2)}, u32[]{:S(2)}) collective-permute-start(bf16[256,768]{1,0:T(8,128)(2,1)S(1)} %get-tuple-element.150), channel_id=1, source_target_pairs={{0,2},{1,3},{2,0},{3,1},{4,6},{5,7},{6,4},{7,5},{8,10},{9,11},{10,... | collective-permute-start | bytes 1179656 | tf_op jit(solution)/shard_map/ppermute | solution.py:46
  321.9 21.8 %collective-permute-start.25 = (bf16[256,768]{1,0:T(8,128)(2,1)S(1)}, bf16[256,768]{1,0:T(8,128)(2,1)S(1)}, u32[]{:S(2)}, u32[]{:S(2)}) collective-permute-start(bf16[256,768]{1,0:T(8,128)(2,1)S(1)} %multiply_convert_fusion.5), channel_id=1, source_target_pairs={{0,2},{1,3},{2,0},{3,1},{4,6},{5,7},{6,4},{7,5},{8,10},{9,11},{10,... | collective-permute-start | bytes 1179656 | tf_op jit(solution)/shard_map/ppermute | solution.py:41
  322.1 21.5 %collective-permute-start.24 = (bf16[256,768]{1,0:T(8,128)(2,1)S(1)}, bf16[256,768]{1,0:T(8,128)(2,1)S(1)}, u32[]{:S(2)}, u32[]{:S(2)}) collective-permute-start(bf16[256,768]{1,0:T(8,128)(2,1)S(1)} %multiply_convert_fusion.5), channel_id=1, source_target_pairs={{0,1},{1,0},{2,3},{3,2},{4,5},{5,4},{6,7},{7,6},{8,9},{9,8},{10,11... | collective-permute-start | bytes 1179656 | tf_op jit(solution)/shard_map/ppermute | solution.py:41
  323.4 31.3 %collective-permute-start.33 = (bf16[256,768]{1,0:T(8,128)(2,1)S(1)}, bf16[256,768]{1,0:T(8,128)(2,1)S(1)}, u32[]{:S(2)}, u32[]{:S(2)}) collective-permute-start(bf16[256,768]{1,0:T(8,128)(2,1)S(1)} %dynamic-slice_bitcast_fusion.1), channel_id=1, source_target_pairs={{0,3},{1,2},{2,1},{3,0},{4,7},{5,6},{6,5},{7,4},{8,11},{9,10},{10,... | collective-permute-start | bytes 1179656 | tf_op jit(solution)/shard_map/ppermute | solution.py:41
  324.6 33.3 %collective-permute-start.32 = (bf16[256,768]{1,0:T(8,128)(2,1)S(1)}, bf16[256,768]{1,0:T(8,128)(2,1)S(1)}, u32[]{:S(2)}, u32[]{:S(2)}) collective-permute-start(bf16[256,768]{1,0:T(8,128)(2,1)S(1)} %dynamic-slice_bitcast_fusion.1), channel_id=1, source_target_pairs={{0,2},{1,3},{2,0},{3,1},{4,6},{5,7},{6,4},{7,5},{8,10},{9,11},{10,... | collective-permute-start | bytes 1179656 | tf_op jit(solution)/shard_map/ppermute | solution.py:41
  330.0 27.9 %collective-permute-start.31 = (bf16[256,768]{1,0:T(8,128)(2,1)S(1)}, bf16[256,768]{1,0:T(8,128)(2,1)S(1)}, u32[]{:S(2)}, u32[]{:S(2)}) collective-permute-start(bf16[256,768]{1,0:T(8,128)(2,1)S(1)} %dynamic-slice_bitcast_fusion.1), channel_id=1, source_target_pairs={{0,1},{1,0},{2,3},{3,2},{4,5},{5,4},{6,7},{7,6},{8,9},{9,8},{10,11... | collective-permute-start | bytes 1179656 | tf_op jit(solution)/shard_map/ppermute | solution.py:41
  454.5 33.5 %all-to-all-start.6 = ((bf16[4,256,576]{1,2,0:T(8,128)(2,1)}), bf16[4,256,576]{1,2,0:T(8,128)(2,1)}, u32[]{:S(2)}, u32[]{:S(2)}) async-start(bf16[4,256,576]{1,2,0:T(8,128)(2,1)} %copy.157), calls=%async_computation.6 | async-start | bytes 2359296 | tf_op jit(solution)/shard_map/all_to_all | solution.py:29
  480.0 98.4 %collective-permute-start.51 = (bf16[256,768]{1,0:T(8,128)(2,1)}, bf16[256,768]{1,0:T(8,128)(2,1)}, u32[]{:S(2)}, u32[]{:S(2)}) collective-permute-start(bf16[256,768]{1,0:T(8,128)(2,1)} %convolution_convert_fusion.20), channel_id=1, source_target_pairs={{0,16},{16,0},{1,17},{17,1},{2,18},{18,2},{3,19},{19,3},{4,20},{20... | collective-permute-start | bytes 1179656 | tf_op jit(solution)/shard_map/ppermute | solution.py:25
  495.6 19.2 %collective-permute-start.38 = (bf16[256,768]{1,0:T(8,128)(2,1)S(1)}, bf16[256,768]{1,0:T(8,128)(2,1)S(1)}, u32[]{:S(2)}, u32[]{:S(2)}) collective-permute-start(bf16[256,768]{1,0:T(8,128)(2,1)S(1)} %get-tuple-element.95), channel_id=1, source_target_pairs={{0,2},{1,3},{2,0},{3,1},{4,6},{5,7},{6,4},{7,5},{8,10},{9,11},{10,... | collective-permute-start | bytes 1179656 | tf_op jit(solution)/shard_map/ppermute | solution.py:41
  496.8 18.0 %collective-permute-start.37 = (bf16[256,768]{1,0:T(8,128)(2,1)S(1)}, bf16[256,768]{1,0:T(8,128)(2,1)S(1)}, u32[]{:S(2)}, u32[]{:S(2)}) collective-permute-start(bf16[256,768]{1,0:T(8,128)(2,1)S(1)} %get-tuple-element.95), channel_id=1, source_target_pairs={{0,1},{1,0},{2,3},{3,2},{4,5},{5,4},{6,7},{7,6},{8,9},{9,8},{10,11... | collective-permute-start | bytes 1179656 | tf_op jit(solution)/shard_map/ppermute | solution.py:41
  501.4 108.6 %collective-permute-start.52 = (bf16[384,1024]{1,0:T(8,128)(2,1)}, bf16[384,1024]{1,0:T(8,128)(2,1)}, u32[]{:S(2)}, u32[]{:S(2)}) collective-permute-start(bf16[384,1024]{1,0:T(8,128)(2,1)} %convolution_convert_fusion.16), channel_id=1, source_target_pairs={{0,16},{16,0},{1,17},{17,1},{2,18},{18,2},{3,19},{19,3},{4,20},{20... | collective-permute-start | bytes 2359304 | tf_op jit(solution)/shard_map/ppermute | solution.py:25
  544.0 20.6 %collective-permute-start.41 = (bf16[272,768]{1,0:T(8,128)(2,1)S(1)}, bf16[272,768]{1,0:T(8,128)(2,1)S(1)}, u32[]{:S(2)}, u32[]{:S(2)}) collective-permute-start(bf16[272,768]{1,0:T(8,128)(2,1)S(1)} %pad_maximum_fusion.46), channel_id=1, source_target_pairs={{0,2},{1,3},{2,0},{3,1},{4,6},{5,7},{6,4},{7,5},{8,10},{9,11},{10,... | collective-permute-start | bytes 1253384 | tf_op jit(solution)/shard_map/ppermute | solution.py:46
  546.0 19.4 %collective-permute-start.42 = (bf16[272,768]{1,0:T(8,128)(2,1)}, bf16[272,768]{1,0:T(8,128)(2,1)}, u32[]{:S(2)}, u32[]{:S(2)}) collective-permute-start(bf16[272,768]{1,0:T(8,128)(2,1)} %pad_maximum_fusion.47), channel_id=1, source_target_pairs={{0,3},{1,2},{2,1},{3,0},{4,7},{5,6},{6,5},{7,4},{8,11},{9,10},{10,... | collective-permute-start | bytes 1253384 | tf_op jit(solution)/shard_map/ppermute | solution.py:46
  548.0 18.9 %collective-permute-start.40 = (bf16[272,768]{1,0:T(8,128)(2,1)}, bf16[272,768]{1,0:T(8,128)(2,1)}, u32[]{:S(2)}, u32[]{:S(2)}) collective-permute-start(bf16[272,768]{1,0:T(8,128)(2,1)} %pad_maximum_fusion.45), channel_id=1, source_target_pairs={{0,1},{1,0},{2,3},{3,2},{4,5},{5,4},{6,7},{7,6},{8,9},{9,8},{10,11... | collective-permute-start | bytes 1253384 | tf_op jit(solution)/shard_map/ppermute | solution.py:46
  564.6 94.3 %collective-permute-start.56 = (bf16[1024,768]{1,0:T(8,128)(2,1)}, bf16[1024,768]{1,0:T(8,128)(2,1)}, u32[]{:S(2)}, u32[]{:S(2)}) collective-permute-start(bf16[1024,768]{1,0:T(8,128)(2,1)} %convolution_convert_fusion.6), channel_id=1, source_target_pairs={{0,16},{16,0},{1,17},{17,1},{2,18},{18,2},{3,19},{19,3},{4,20},{20... | collective-permute-start | bytes 4718600 | tf_op jit(solution)/shard_map/ppermute | solution.py:25
  565.4 215.7 %collective-permute-start.63 = (bf16[384,4096]{1,0:T(8,128)(2,1)}, bf16[384,4096]{1,0:T(8,128)(2,1)}, u32[]{:S(2)}, u32[]{:S(2)}) collective-permute-start(bf16[384,4096]{1,0:T(8,128)(2,1)} %convolution_convert_fusion), channel_id=1, source_target_pairs={{0,16},{16,0},{1,17},{17,1},{2,18},{18,2},{3,19},{19,3},{4,20},{20... | collective-permute-start | bytes 9437192 | tf_op jit(solution)/shard_map/ppermute | solution.py:25
  582.5 31.2 %collective-permute-start.54 = (bf16[384,768]{1,0:T(8,128)(2,1)}, bf16[384,768]{1,0:T(8,128)(2,1)}, u32[]{:S(2)}, u32[]{:S(2)}) collective-permute-start(bf16[384,768]{1,0:T(8,128)(2,1)} %convolution_convert_fusion.18), channel_id=1, source_target_pairs={{0,16},{16,0},{1,17},{17,1},{2,18},{18,2},{3,19},{19,3},{4,20},{20... | collective-permute-start | bytes 1769480 | tf_op jit(solution)/shard_map/ppermute | solution.py:25
  586.1 45.0 %collective-permute-start.53 = (bf16[384,2304]{1,0:T(8,128)(2,1)}, bf16[384,2304]{1,0:T(8,128)(2,1)}, u32[]{:S(2)}, u32[]{:S(2)}) collective-permute-start(bf16[384,2304]{1,0:T(8,128)(2,1)} %convolution_convert_fusion.2), channel_id=1, source_target_pairs={{0,16},{16,0},{1,17},{17,1},{2,18},{18,2},{3,19},{19,3},{4,20},{20... | collective-permute-start | bytes 5308424 | tf_op jit(solution)/shard_map/ppermute | solution.py:25
  604.8 31.7 %all-to-all-start.8 = ((bf16[4,256,576]{1,2,0:T(8,128)(2,1)}), bf16[4,256,576]{1,2,0:T(8,128)(2,1)S(1)}, u32[]{:S(2)}, u32[]{:S(2)}) async-start(bf16[4,256,576]{1,2,0:T(8,128)(2,1)} %copy.162), calls=%async_computation.8 | async-start | bytes 2359296 | tf_op jit(solution)/shard_map/all_to_all | solution.py:29
  622.9 107.5 %collective-permute-start.50 = (bf16[384,4096]{1,0:T(8,128)(2,1)}, bf16[384,4096]{1,0:T(8,128)(2,1)}, u32[]{:S(2)}, u32[]{:S(2)}) collective-permute-start(bf16[384,4096]{1,0:T(8,128)(2,1)} %convolution_convert_fusion.1), channel_id=1, source_target_pairs={{0,16},{16,0},{1,17},{17,1},{2,18},{18,2},{3,19},{19,3},{4,20},{20... | collective-permute-start | bytes 9437192 | tf_op jit(solution)/shard_map/ppermute | solution.py:25
  631.0 35.9 %collective-permute-start.47 = (bf16[384,768]{1,0:T(8,128)(2,1)}, bf16[384,768]{1,0:T(8,128)(2,1)}, u32[]{:S(2)}, u32[]{:S(2)}) collective-permute-start(bf16[384,768]{1,0:T(8,128)(2,1)} %convolution_convert_fusion.19), channel_id=1, source_target_pairs={{0,16},{16,0},{1,17},{17,1},{2,18},{18,2},{3,19},{19,3},{4,20},{20... | collective-permute-start | bytes 1769480 | tf_op jit(solution)/shard_map/ppermute | solution.py:25
  636.5 17.7 %all-to-all-start.11 = ((bf16[4,96,1024]{2,1,0:T(8,128)(2,1)}), bf16[4,96,1024]{2,1,0:T(8,128)(2,1)}, u32[]{:S(2)}, u32[]{:S(2)}) async-start(bf16[4,96,1024]{2,1,0:T(8,128)(2,1)} %bitcast.410), calls=%async_computation.11 | async-start | bytes 1572864 | tf_op jit(solution)/shard_map/all_to_all | solution.py:29
  652.5 17.5 %collective-permute-start.46 = (bf16[384,2304]{1,0:T(8,128)(2,1)}, bf16[384,2304]{1,0:T(8,128)(2,1)}, u32[]{:S(2)}, u32[]{:S(2)}) collective-permute-start(bf16[384,2304]{1,0:T(8,128)(2,1)} %convolution_convert_fusion.3), channel_id=1, source_target_pairs={{0,16},{16,0},{1,17},{17,1},{2,18},{18,2},{3,19},{19,3},{4,20},{20... | collective-permute-start | bytes 5308424 | tf_op jit(solution)/shard_map/ppermute | solution.py:25
  654.1 33.7 %all-to-all-start.12 = ((bf16[4,96,3200]{2,1,0:T(8,128)(2,1)}), bf16[4,96,3200]{2,1,0:T(8,128)(2,1)}, u32[]{:S(2)}, u32[]{:S(2)}) async-start(bf16[4,96,3200]{2,1,0:T(8,128)(2,1)} %pad_maximum_fusion.5), calls=%async_computation.12 | async-start | bytes 4915200 | tf_op jit(solution)/shard_map/all_to_all | solution.py:29
  658.8 71.5 %all-reduce.12.cloned.1.call-start = ((), (), s32[]{:S(2)}) async-start(), calls=%async_computation.13 | async-start | bytes 3145728 | tf_op jit(solution)/shard_map/psum | solution.py:417
  666.4 30.2 %collective-permute-start.49 = (bf16[1024,768]{1,0:T(8,128)(2,1)}, bf16[1024,768]{1,0:T(8,128)(2,1)}, u32[]{:S(2)}, u32[]{:S(2)}) collective-permute-start(bf16[1024,768]{1,0:T(8,128)(2,1)} %convolution_convert_fusion.7), channel_id=1, source_target_pairs={{0,16},{16,0},{1,17},{17,1},{2,18},{18,2},{3,19},{19,3},{4,20},{20... | collective-permute-start | bytes 4718600 | tf_op jit(solution)/shard_map/ppermute | solution.py:25
  687.8 89.0 %all-to-all-start.10 = ((bf16[4,96,3200]{2,1,0:T(8,128)(2,1)}), bf16[4,96,3200]{2,1,0:T(8,128)(2,1)S(1)}, u32[]{:S(2)}, u32[]{:S(2)}) async-start(bf16[4,96,3200]{2,1,0:T(8,128)(2,1)} %pad_maximum_fusion.4), calls=%async_computation.10 | async-start | bytes 4915200 | tf_op jit(solution)/shard_map/all_to_all | solution.py:29
  691.5 77.0 %all-reduce.14.cloned.1.call-start = ((), (), s32[]{:S(2)}) async-start(), calls=%async_computation.14 | async-start | bytes 786432 | tf_op jit(solution)/shard_map/psum | solution.py:417
  695.5 78.2 %collective-permute-start.45 = (bf16[384,1024]{1,0:T(8,128)(2,1)}, bf16[384,1024]{1,0:T(8,128)(2,1)}, u32[]{:S(2)}, u32[]{:S(2)}) collective-permute-start(bf16[384,1024]{1,0:T(8,128)(2,1)} %convolution_convert_fusion.17), channel_id=1, source_target_pairs={{0,16},{16,0},{1,17},{17,1},{2,18},{18,2},{3,19},{19,3},{4,20},{20... | collective-permute-start | bytes 2359304 | tf_op jit(solution)/shard_map/ppermute | solution.py:25
  730.4 110.2 %all-reduce.16.cloned.1.call-start = ((), (), s32[]{:S(2)}) async-start(), calls=%async_computation.15 | async-start | bytes 3145728 | tf_op jit(solution)/shard_map/psum | solution.py:417
  771.5 16.6 %collective-permute-start.44 = (bf16[256,768]{1,0:T(8,128)(2,1)}, bf16[256,768]{1,0:T(8,128)(2,1)}, u32[]{:S(2)}, u32[]{:S(2)}) collective-permute-start(bf16[256,768]{1,0:T(8,128)(2,1)} %convolution_convert_fusion.21), channel_id=1, source_target_pairs={{0,16},{16,0},{1,17},{17,1},{2,18},{18,2},{3,19},{19,3},{4,20},{20... | collective-permute-start | bytes 1179656 | tf_op jit(solution)/shard_map/ppermute | solution.py:25
  781.0 395.1 %all-reduce.18.cloned.1.call-start = ((), (), s32[]{:S(2)}) async-start(), calls=%async_computation.17 | async-start | bytes 18972672 | tf_op jit(solution)/shard_map/psum | solution.py:417
  845.0 16.9 %collective-permute-start.29 = (bf16[256,768]{1,0:T(8,128)(2,1)S(1)}, bf16[256,768]{1,0:T(8,128)(2,1)S(1)}, u32[]{:S(2)}, u32[]{:S(2)}) collective-permute-start(bf16[256,768]{1,0:T(8,128)(2,1)S(1)} %get-tuple-element.146), channel_id=1, source_target_pairs={{0,3},{1,2},{2,1},{3,0},{4,7},{5,6},{6,5},{7,4},{8,11},{9,10},{10,... | collective-permute-start | bytes 1179656 | tf_op jit(solution)/shard_map/ppermute | solution.py:46
  875.0 312.8 %collective-permute-start.61 = (bf16[256,768]{1,0:T(8,128)(2,1)S(1)}, bf16[256,768]{1,0:T(8,128)(2,1)}, u32[]{:S(2)}, u32[]{:S(2)}) collective-permute-start(bf16[256,768]{1,0:T(8,128)(2,1)S(1)} %copy-done.79), channel_id=1, source_target_pairs={{0,16},{1,17},{2,18},{3,19},{4,20},{5,21},{6,22},{7,23},{8,24},{9,... | collective-permute-start | bytes 1179656 | tf_op jit(solution)/shard_map/ppermute | solution.py:478
  1190.2 18.1 %collective-permute-start.65 = (bf16[384,4096]{1,0:T(8,128)(2,1)}, bf16[384,4096]{1,0:T(8,128)(2,1)}, u32[]{:S(2)}, u32[]{:S(2)}) collective-permute-start(bf16[384,4096]{1,0:T(8,128)(2,1)} %get-tuple-element.87), channel_id=1, source_target_pairs={{16,0},{17,1},{18,2},{19,3},{20,4},{21,5},{22,6},{23,7},{24,8},{25... | collective-permute-start | bytes 9437192 | tf_op jit(solution)/shard_map/ppermute | solution.py:479
  (206 other events, 2992.9 us)
Sparse Core Ops, SparseCore 0:
  156.5 43.4 all-gather.2
  663.0 67.3 all-reduce.11
  732.7 35.6 all-reduce.13
  771.4 69.1 all-reduce.15
  845.4 330.7 all-reduce.17
where the time goes:
time: 1240 us; the launch traced here: 1230 us
  waiting for transfers between devices  593 us (48%)
  matrix products  208 us (17%)
  starting transfers between devices  133 us (11%)
  local copies, waits for them, and re-layouts  86.9 us (7%)
  other arithmetic  80.1 us (6%)
  blocking collectives  68.3 us (6%)
  Pallas kernels  37.9 us (3%)
  between operations  19 us (2%)
    psum x4, waiting for transfers between devices, lane_sums(): sums = lax.psum(tuple(group), DP)  406 us
    dot_general x62, matrix products, mm(): lax.dot_general(a, b, (((ca,), (cb,)), ((), ())), preferred_element_type=...  208 us
    ppermute x21, waiting for transfers between devices, gather_blocks(): lax.ppermute(v, EXP, xor_pairs(members, k))  81.1 us
    all_to_all x3, blocking collectives, a2a(): return lax.all_to_all(v, axis, split_axis=0, concat_axis=0, tiled=True)  68.3 us
    ppermute x12, waiting for transfers between devices, scatter_blocks(): lax.ppermute(blocks[k], EXP, xor_pairs(count, k))  55.9 us
    all_to_all x10, starting transfers between devices, a2a(): return lax.all_to_all(v, axis, split_axis=0, concat_axis=0, tiled=True)  43.3 us
    all_to_all x10, waiting for transfers between devices, a2a(): return lax.all_to_all(v, axis, split_axis=0, concat_axis=0, tiled=True)  40.8 us
    ppermute x25, starting transfers between devices, swap_cores(): return lax.ppermute(v, SEC, SWAP)  38.5 us
  transfers between devices with their start and end apart: 83, of which 37 were waited for; matrix products, arithmetic and copies ran while one was open for 22% of the time, Pallas kernels for 2%

commit v1 on v0

v1 whole, which is shorter than its diff:
```python
import functools
import jax
import jax.numpy as jnp
from jax import lax
from jax.experimental import pallas as pl
from jax.experimental.pallas import tpu as pltpu
from jax.sharding import PartitionSpec as P

HEADS = 12
HEAD = 64
FF = 2048
EPS = 1e-06

SEC, DP, EXP = "section", "dp", "expert"
BF, F32, I32 = jnp.bfloat16, jnp.float32, jnp.int32
SWAP = [(0, 1), (1, 0)]


def mm(a, b, ca=1, cb=0, out=F32):
    r = lax.dot_general(a, b, (((ca,), (cb,)), ((), ())), preferred_element_type=F32)
    return r.astype(out)


def swap_cores(v):
    return lax.ppermute(v, SEC, SWAP)


def a2a(v, axis):
    return lax.all_to_all(v, axis, split_axis=0, concat_axis=0, tiled=True)


def gather(v, axis):
    return lax.all_gather(v, axis, axis=0, tiled=True)


def xor_pairs(count, k):
    return [(i, i ^ k) for i in range(count)]


def gather_blocks(v, members):
    return [v] + [lax.ppermute(v, EXP, xor_pairs(members, k)) for k in range(1, members)]


def scatter_blocks(blocks):
    count = len(blocks)
    return [blocks[0]] + [lax.ppermute(blocks[k], EXP, xor_pairs(count, k)) for k in range(1, count)]


def half_of(v, which, axis=0):
    size = v.shape[axis] // 2
    return lax.dynamic_slice_in_dim(v, which * size, size, axis)


def by_core(core, first, second):
    return jnp.where(core == 0, first, second)


def norm_apply(values, gain):
    scale = lax.rsqrt(jnp.mean(values * values, axis=-1, keepdims=True) + EPS)
    return (values * scale * gain).astype(BF), scale


def norm_backward(grad_hidden, values, scale, gain):
    normed = values * scale
    grad_gain = jnp.sum(grad_hidden * normed, axis=0)
    grad_normed = grad_hidden * gain
    grad_values = scale * (
        grad_normed - normed * jnp.mean(grad_normed * normed, axis=-1, keepdims=True)
    )
    return grad_values, grad_gain


def silu(v):
    return v * jax.nn.sigmoid(v)


def silu_parts(v):
    logistic = jax.nn.sigmoid(v)
    return v * logistic, logistic * (1.0 + v * (1.0 - logistic))


def block_mask(ends_ref, first_row, rows, cols):
    q = first_row + lax.broadcasted_iota(I32, (rows, cols), 0)
    k = lax.broadcasted_iota(I32, (rows, cols), 1)
    start = jnp.zeros((rows, cols), I32)
    for i in range(ends_ref.shape[0]):
        end = ends_ref[i]
        start = jnp.where(q >= end, end, start)
    return (k <= q) & (k >= start)


def head_slices(ref, rows, head, per, parts):
    return [ref[rows, (part * per + head) * HEAD : (part * per + head + 1) * HEAD] for part in parts]


def block_probs(q, k, mask):
    scores = lax.dot_general(q, k, (((1,), (1,)), ((), ())), preferred_element_type=F32)
    scores = jnp.where(mask, scores * (HEAD**-0.5), -1e30)
    raised = jnp.exp(scores - jnp.max(scores, axis=-1, keepdims=True))
    return raised / jnp.sum(raised, axis=-1, keepdims=True)


def attention_forward_kernel(block, per, ends_ref, qkv_ref, out_ref):
    pack = qkv_ref.shape[0]
    for i in range(pack // block):
        rows, reach = slice(i * block, (i + 1) * block), slice(0, (i + 1) * block)
        mask = block_mask(ends_ref, i * block, block, (i + 1) * block)
        for head in range(per):
            (q,) = head_slices(qkv_ref, rows, head, per, (0,))
            k, v = head_slices(qkv_ref, reach, head, per, (1, 2))
            probs = block_probs(q, k, mask).astype(BF)
            mixed = jnp.dot(probs, v, preferred_element_type=F32)
            out_ref[rows, head * HEAD : (head + 1) * HEAD] = mixed.astype(BF)


def attention_backward_kernel(block, per, ends_ref, qkv_ref, grad_ref, out_ref, dk_ref, dv_ref):
    pack = qkv_ref.shape[0]
    dk_ref[...] = jnp.zeros_like(dk_ref)
    dv_ref[...] = jnp.zeros_like(dv_ref)
    for i in range(pack // block):
        rows, reach = slice(i * block, (i + 1) * block), slice(0, (i + 1) * block)
        mask = block_mask(ends_ref, i * block, block, (i + 1) * block)
        for head in range(per):
            (q,) = head_slices(qkv_ref, rows, head, per, (0,))
            k, v = head_slices(qkv_ref, reach, head, per, (1, 2))
            grad = grad_ref[rows, head * HEAD : (head + 1) * HEAD]
            probs = block_probs(q, k, mask)
            dprobs = lax.dot_general(grad, v, (((1,), (1,)), ((), ())), preferred_element_type=F32)
            delta = jnp.sum(probs * dprobs, axis=-1, keepdims=True)
            dscores = (probs * (dprobs - delta)).astype(BF)
            dq = jnp.dot(dscores, k, preferred_element_type=F32) * (HEAD**-0.5)
            out_ref[rows, head * HEAD : (head + 1) * HEAD] = dq.astype(BF)
            over_queries = (((0,), (0,)), ((), ()))
            dk_ref[head, reach, :] += lax.dot_general(
                dscores, q, over_queries, preferred_element_type=F32
            )
            dv_ref[head, reach, :] += lax.dot_general(
                probs.astype(BF), grad, over_queries, preferred_element_type=F32
            )
    for head in range(per):
        at = (per + head) * HEAD
        out_ref[:, at : at + HEAD] = (dk_ref[head] * (HEAD**-0.5)).astype(BF)
        at = (2 * per + head) * HEAD
        out_ref[:, at : at + HEAD] = dv_ref[head].astype(BF)


def vmem():
    return pl.BlockSpec(memory_space=pltpu.VMEM)


def attention_forward(ends, qkv, block):
    pack, columns = qkv.shape
    per = columns // (3 * HEAD)
    return pl.pallas_call(
        functools.partial(attention_forward_kernel, block, per),
        out_shape=jax.ShapeDtypeStruct((pack, per * HEAD), BF),
        in_specs=[pl.BlockSpec(memory_space=pltpu.SMEM), vmem()],
        out_specs=vmem(),
        compiler_params=pltpu.CompilerParams(vmem_limit_bytes=32 << 20),
        cost_estimate=pl.CostEstimate(
            flops=4 * per * pack * pack * HEAD, bytes_accessed=8 * pack * columns // 3, transcendentals=per * pack * pack
        ),
    )(ends, qkv)


def attention_backward(ends, qkv, grad, block):
    pack, columns = qkv.shape
    per = columns // (3 * HEAD)
    return pl.pallas_call(
        functools.partial(attention_backward_kernel, block, per),
        out_shape=jax.ShapeDtypeStruct((pack, columns), BF),
        in_specs=[pl.BlockSpec(memory_space=pltpu.SMEM), vmem(), vmem()],
        out_specs=vmem(),
        scratch_shapes=[pltpu.VMEM((per, pack, HEAD), F32)] * 2,
        compiler_params=pltpu.CompilerParams(vmem_limit_bytes=32 << 20),
        cost_estimate=pl.CostEstimate(
            flops=10 * per * pack * pack * HEAD, bytes_accessed=16 * pack * columns // 3, transcendentals=per * pack * pack
        ),
    )(ends, qkv, grad)


SPOT = 64
TAIL = 16
TILE = 512
WINDOW_STEP = (1, 2)
TAIL_STEP = (1, 2)
CHUNKS = (1, 2, 1, 1, 1)


def nt(a, b):
    return lax.dot_general(a, b, (((1,), (1,)), ((), ())), preferred_element_type=F32)


def nn(a, b):
    return jnp.dot(a, b, preferred_element_type=F32)


def slot_rows(slot_ref, k, first, count):
    row = slot_ref[k : k + 1, :]
    place = first + lax.broadcasted_iota(I32, (count, row.shape[1]), 0)
    return (place == row).astype(F32).astype(BF)


def slot_columns(info, capacity):
    column = info[:, SPOT : SPOT + 1]
    place = lax.broadcasted_iota(I32, (info.shape[0], capacity), 1).astype(F32)
    return (place == column).astype(F32).astype(BF)


def dispatch(slot_ref, block_refs, first, count):
    total = None
    for k, ref in enumerate(block_refs):
        part = nn(slot_rows(slot_ref, k, first, count), ref[...])
        total = part if total is None else total + part
    return total.astype(BF)


def from_either(which_ref, sources, body):
    @pl.when(which_ref[1] == 1)
    def _():
        body(*sources[0])

    @pl.when(which_ref[1] == 0)
    def _():
        body(*sources[1])


def moe_forward_kernel(members, experts, *refs):
    which_ref, slot_ref, info_ref, router_ref = refs[:4]
    h_refs, refs = refs[4 : 4 + members], refs[4 + members :]
    sources, (wsi_ref, wsd_ref), refs = (refs[:3], refs[3:6]), refs[6:8], refs[3:]
    rows_ref, g_ref, u_ref, a_ref, meta_ref, ret_ref, sg_ref, su_ref, sa_ref = refs[5:14]
    part_refs, (acc_ref, y_ref) = refs[14 : 14 + members], refs[14 + members :]
    step, last = pl.program_id(0), pl.num_programs(0) - 1
    capacity, tokens = rows_ref.shape[0], h_refs[0].shape[0]
    tiles = [slice(r, r + tokens) for r in range(0, capacity, tokens)]

    @pl.when(step == 0)
    def _():
        for r in tiles:
            rows_ref[r, :] = dispatch(slot_ref, h_refs, r.start, tokens)
            acc_ref[r, :] = jnp.zeros((tokens, acc_ref.shape[1]), F32)

    def units(wg_ref, wu_ref, wd_ref):
        for r in tiles:
            x = rows_ref[r, :]
            gate, up = nn(x, wg_ref[...]), nn(x, wu_ref[...])
            act = (gate * jax.nn.sigmoid(gate) * up).astype(BF)
            g_ref[r, :], u_ref[r, :], a_ref[r, :] = gate.astype(BF), up.astype(BF), act
            acc_ref[r, :] += nn(act, wd_ref[...])

    from_either(which_ref, sources, units)

    @pl.when(step == last)
    def _():
        for r in tiles:
            y_ref[r, :] = acc_ref[r, :].astype(BF)
        quarter = wsd_ref.shape[0]
        for k in range(members):
            t = slice(k * tokens, (k + 1) * tokens)
            h, info = h_refs[k][...], info_ref[t, :]
            lane = lax.broadcasted_iota(I32, info.shape, 1)
            logits = jnp.where(lane < experts, nn(h, router_ref[...]), -1e30)
            raised = jnp.exp(logits - jnp.max(logits, axis=-1, keepdims=True))
            probs = raised / jnp.sum(raised, axis=-1, keepdims=True)
            chosen = jnp.where(lane < experts, info, 0.0)
            picked = jnp.sum(probs * chosen, axis=-1, keepdims=True)
            here = jnp.sum(jnp.where(lane == which_ref[0], probs, 0.0), axis=-1, keepdims=True)
            weight = here / picked
            meta_ref[t, :] = jnp.where(lane == SPOT, weight, probs)
            gate, up = nn(h, wsi_ref[:, :quarter]), nn(h, wsi_ref[:, quarter:])
            act = (gate * jax.nn.sigmoid(gate) * up).astype(BF)
            sg_ref[t, :], su_ref[t, :], sa_ref[t, :] = gate.astype(BF), up.astype(BF), act
            back = nn(slot_columns(info, capacity), y_ref[...])
            ret_ref[t, :] = back.astype(BF)
            part_refs[k][...] = (weight * back + nn(act, wsd_ref[...])).astype(BF)


def act_grads(gate_low, up_low, grad_act):
    gate, up = gate_low.astype(F32), up_low.astype(F32)
    value, slope = silu_parts(gate)
    return (grad_act * up * slope).astype(BF), (grad_act * value).astype(BF)


def moe_backward_kernel(members, *refs):
    which_ref, slot_ref, info_ref, meta_ref = refs[:4]
    grad_refs, refs = refs[4 : 4 + members], refs[4 + members :]
    ret_ref, sources, refs = refs[0], (refs[1:4], refs[4:7]), refs[7:]
    g_ref, u_ref, sg_ref, su_ref, wsi_ref, wsd_ref = refs[:6]
    dy_ref, dg_ref, du_ref, dsg_ref, dsu_ref = refs[6:11]
    part_refs, (gated_ref, acc_ref) = refs[11 : 11 + members], refs[11 + members :]
    step, last = pl.program_id(0), pl.num_programs(0) - 1
    capacity, width = dy_ref.shape
    tokens = grad_refs[0].shape[0]
    tiles = [slice(r, r + tokens) for r in range(0, capacity, tokens)]

    @pl.when(step == 0)
    def _():
        for k in range(members):
            t = slice(k * tokens, (k + 1) * tokens)
            grad = grad_refs[k][...].astype(F32)
            weight = meta_ref[t, SPOT : SPOT + 1]
            gated_ref[k, :, :] = (weight * grad).astype(BF)
            product = grad * ret_ref[t, :].astype(F32)
            high = product.astype(BF)
            low = (product - high.astype(F32)).astype(BF)
            ones = jnp.ones((TAIL, width), BF)
            total = nt(ones, high) + nt(ones, low)
            high = total.astype(BF).astype(F32)
            row = lax.broadcasted_iota(I32, total.shape, 0)
            tail = jnp.where(row == 0, high, jnp.where(row == 1, total - high, 0.0))
            part_refs[k][tokens : tokens + TAIL, :] = jnp.zeros((TAIL, width), BF)
            part_refs[k][tokens : tokens + TAIL, :tokens] = tail.astype(BF)
        for r in tiles:
            dy_ref[r, :] = dispatch(slot_ref, [gated_ref.at[k] for k in range(members)], r.start, tokens)
            acc_ref[r, :] = jnp.zeros((tokens, width), F32)

    def units(wg_ref, wu_ref, wd_ref):
        for r in tiles:
            dg, du = act_grads(g_ref[r, :], u_ref[r, :], nt(dy_ref[r, :], wd_ref[...]))
            dg_ref[r, :], du_ref[r, :] = dg, du
            acc_ref[r, :] += nt(dg, wg_ref[...]) + nt(du, wu_ref[...])

    from_either(which_ref, sources, units)

    @pl.when(step == last)
    def _():
        rows = acc_ref[...].astype(BF)
        quarter = wsd_ref.shape[0]
        for k in range(members):
            t = slice(k * tokens, (k + 1) * tokens)
            dsg, dsu = act_grads(sg_ref[t, :], su_ref[t, :], nt(grad_refs[k][...], wsd_ref[...]))
            dsg_ref[t, :], dsu_ref[t, :] = dsg, dsu
            back = nt(dsg, wsi_ref[:, :quarter]) + nt(dsu, wsi_ref[:, quarter:])
            back = back + nn(slot_columns(info_ref[t, :], capacity), rows)
            part_refs[k][:tokens, :] = back.astype(BF)


def whole_block(*shape):
    return pl.BlockSpec(shape, lambda i, which: (0,) * len(shape), pipeline_mode=pl.Buffered(1))


def expert_specs(width):
    steps = FF // TILE

    def tiles(own):
        def at(i, which):
            return i * (which[1] if own else 1 - which[1])

        return [
            pl.BlockSpec((width, TILE), lambda i, which: (0, at(i, which))),
            pl.BlockSpec((width, TILE), lambda i, which: (0, steps + at(i, which))),
            pl.BlockSpec((TILE, width), lambda i, which: (at(i, which), 0)),
        ]

    return tiles(True) + tiles(False)


def expert_args(experts):
    return [w for w_in, w_down in experts for w in (w_in, w_in, w_down)]


def moe_call(kernel, shapes, in_specs, out_tiled, scratch, args, work):
    whole = [whole_block(*shape) for shape, _ in shapes]
    tiled = pl.BlockSpec((shapes[0][0][0], TILE), lambda i, which: (0, i))
    return pl.pallas_call(
        kernel,
        out_shape=[jax.ShapeDtypeStruct(*shape) for shape in shapes],
        grid_spec=pltpu.PrefetchScalarGridSpec(
            num_scalar_prefetch=1,
            grid=(FF // TILE,),
            in_specs=in_specs,
            out_specs=whole[:1] + [tiled] * out_tiled + whole[1 + out_tiled :],
            scratch_shapes=scratch,
        ),
        compiler_params=pltpu.CompilerParams(vmem_limit_bytes=56 << 20),
        cost_estimate=pl.CostEstimate(flops=work, bytes_accessed=30 << 20, transcendentals=1 << 20),
    )(*args)


def moe_work(width, capacity, everyone, quarter):
    return 2 * width * (capacity * (3 * FF + 2 * everyone) + 3 * everyone * quarter)


def moe_forward(which, slot, info, w_small, blocks, experts, w_sin, w_sdown, capacity, count):
    members, (tokens, width), quarter = len(blocks), blocks[0].shape, w_sdown.shape[0]
    everyone = members * tokens
    shapes = [((capacity, width), BF)] + [((capacity, FF), BF)] * 3
    shapes += [((everyone, 128), F32), ((everyone, width), BF)] + [((everyone, quarter), BF)] * 3
    shapes += [((tokens, width), BF)] * members
    in_specs = [whole_block(members, tokens), whole_block(everyone, 128), whole_block(width, 128)]
    in_specs += [whole_block(tokens, width)] * members + expert_specs(width)
    in_specs += [whole_block(width, 2 * quarter), whole_block(quarter, width)]
    return moe_call(
        functools.partial(moe_forward_kernel, members, count),
        shapes,
        in_specs,
        3,
        [pltpu.VMEM((capacity, width), F32), pltpu.VMEM((capacity, width), BF)],
        (which, slot, info, w_small, *blocks, *expert_args(experts), w_sin, w_sdown),
        moe_work(width, capacity, everyone, quarter),
    )


def moe_backward(which, slot, info, meta, blocks, ret, experts, gate, up, sg, su, w_sin, w_sdown):
    members, (tokens, width), quarter = len(blocks), blocks[0].shape, w_sdown.shape[0]
    everyone, capacity = members * tokens, gate.shape[0]
    shapes = [((capacity, width), BF)] + [((capacity, FF), BF)] * 2
    shapes += [((everyone, quarter), BF)] * 2 + [((tokens + TAIL, width), BF)] * members
    in_specs = [whole_block(members, tokens), whole_block(everyone, 128), whole_block(everyone, 128)]
    in_specs += [whole_block(tokens, width)] * members + [whole_block(everyone, width)] + expert_specs(width)
    in_specs += [pl.BlockSpec((capacity, TILE), lambda i, which: (0, i))] * 2
    in_specs += [whole_block(everyone, quarter)] * 2
    in_specs += [whole_block(width, 2 * quarter), whole_block(quarter, width)]
    return moe_call(
        functools.partial(moe_backward_kernel, members),
        shapes,
        in_specs,
        2,
        [pltpu.VMEM((members, tokens, width), BF), pltpu.VMEM((capacity, width), F32)],
        (which, slot, info, meta, *blocks, ret, *expert_args(experts), gate, up, sg, su, w_sin, w_sdown),
        moe_work(width, capacity, everyone, quarter),
    )


def after(values, *others):
    return lax.optimization_barrier((values, others))[0]


class Weights:
    def __init__(self, core, members, gains, w_qkv, w_out, w_router, *rest):
        self.core, self.members, self.width = core, members, w_out.shape[1]
        self.experts = w_router.shape[1]
        rows, extra = w_qkv.shape[0], self.experts + 2
        small = jnp.concatenate([w_router, gains.T, jnp.zeros((rows, 128 - extra), BF)], axis=1)
        self.first_shares = self.shares(jnp.concatenate([w_qkv, small], axis=1))
        self.out_shares = self.shares(w_out)
        self.w_sin, self.w_sdown, self.w_ein, self.w_edown = rest

    def both(self, mine):
        other = swap_cores(mine)
        return by_core(self.core, mine, other), by_core(self.core, other, mine)

    def shares(self, shard):
        mine, theirs = half_of(shard, self.core), half_of(shard, 1 - self.core)
        other = swap_cores(theirs)
        return by_core(self.core, mine, other), by_core(self.core, other, mine)

    def both_halves(self, full):
        blocks, rows, columns = full.shape
        other = swap_cores(full)
        halves = [by_core(self.core, full, other), by_core(self.core, other, full)]
        return jnp.stack(halves, axis=1).reshape(blocks * 2 * rows, columns)

    def permuted(self, part):
        me, blocks = lax.axis_index(EXP), jnp.stack(gather_blocks(part, self.members))
        return jnp.concatenate(
            [lax.dynamic_slice_in_dim(blocks, me ^ j, 1, 0) for j in range(self.members)]
        )

    def split_first(self, first):
        at = 3 * self.width
        small = first[:, at : at + 128]
        return first[:, :at], small, small[:, self.experts : self.experts + 2].T.astype(F32)

    def shared_in(self, w_sin):
        me, quarter = lax.axis_index(EXP), FF // self.members
        blocks = []
        for k in range(self.members):
            at = (me ^ k) * quarter
            parts = [lax.dynamic_slice_in_dim(w_sin, start + at, quarter, 1) for start in (0, FF)]
            blocks.append(jnp.concatenate(parts, axis=1))
        blocks = jnp.stack(scatter_blocks(blocks))
        return jnp.concatenate([lax.dynamic_index_in_dim(blocks, me ^ j, 0, False) for j in range(self.members)])


def add_low(a, b):
    return (a.astype(F32) + b.astype(F32)).astype(BF)


class LineSums:
    def __init__(self):
        lane = lax.axis_index(DP)
        self.middle = (lane == 1) | (lane == 2)
        self.now, self.waiting, self.flights, self.done = 0, [], [], {}

    def add(self, section, name, chunks):
        self.waiting += [((section, name, i), chunk) for i, chunk in enumerate(chunks)]

    def busy(self):
        return self.waiting or self.flights

    def step(self, main, count=WINDOW_STEP[0], steps=WINDOW_STEP[1]):
        self.now += 1
        landed = [flight for flight in self.flights if flight[0] <= self.now]
        self.flights = [flight for flight in self.flights if flight[0] > self.now]
        fresh, self.waiting = self.waiting[:count], self.waiting[count:]
        tied = (main, [flight[3:] for flight in landed], [item[1] for item in fresh])
        main, states, chunks = lax.optimization_barrier(tied)

        def launch(stage, key, value, axis, pairs, wait):
            got = lax.ppermute(value, axis, pairs)
            self.flights.append((self.now + wait, stage, key, value, got))

        for (_, stage, key, *_), (value, got) in zip(landed, states):
            if stage == 0:
                launch(1, key, add_low(value, got), DP, [(1, 2), (2, 1)], steps)
            elif stage == 1:
                launch(2, key, add_low(value, got), DP, [(1, 0), (2, 3)], steps)
            elif stage == 2:
                pair = (1, 0) if key[0] == 0 else (0, 1)
                launch(3, key, jnp.where(self.middle, value, got), SEC, [pair], 1)
            else:
                self.done[key] = (value, got)
        for (key, _), chunk in zip(fresh, chunks):
            launch(0, key, chunk, DP, [(0, 1), (3, 2)], steps)
        return main

    def result(self, section, name):
        keys = sorted(key for key in self.done if key[:2] == (section, name))
        return [self.done[key] for key in keys]


def cut(v, count):
    rows = v.shape[0] // count
    return [v[i * rows : (i + 1) * rows] for i in range(count)]


def to_heads(v, lanes, parts):
    tokens, columns = v.shape
    per = columns // (parts * lanes)
    split = v.reshape(tokens, parts, lanes, per).transpose(2, 0, 1, 3).reshape(lanes, tokens, parts * per)
    return a2a(split, DP).reshape(lanes * tokens, parts * per)


def to_tokens(v, lanes, parts):
    pack, columns = v.shape
    tokens, per = pack // lanes, columns // parts
    got = a2a(v.reshape(lanes, tokens, columns), DP).reshape(lanes, tokens, parts, per)
    return got.transpose(1, 2, 0, 3).reshape(tokens, lanes * columns)


def add_blocks(first, blocks):
    return functools.reduce(jnp.add, [block.astype(F32) for block in blocks], first)


def layer_mlp(middle, context, weights, beside=None):
    gain, w_small, w_sin, w_sdown, experts, which = weights
    me, slot, info, capacity, count = context
    members = slot.shape[0]
    hidden, scale = norm_apply(middle, gain)
    blocks = gather_blocks(hidden, members)
    out = moe_forward(which, slot, info, w_small, blocks, experts, w_sin, w_sdown, capacity, count)
    if beside is not None:
        out = beside(out)
    parts = scatter_blocks(out[9:])
    return add_blocks(middle, parts), (scale, hidden, blocks, *out[:9])


def mlp_backward(grad_blocks, middle, saved, context, weights, sums, ready):
    gain, w_small, w_sin, w_sdown, expert_weights, which = weights
    me, slot, info, capacity, experts = context
    scale, hidden, blocks, rows, gate, up, act, meta, ret, sg, su, sact = saved
    members, (tokens, width) = len(blocks), middle.shape
    out = moe_backward(
        which, slot, info, meta, grad_blocks, ret, expert_weights, gate, up, sg, su, w_sin, w_sdown
    )
    out = sums.step(out)
    dy, dg, du, dsg, dsu = out[:5]
    parts = scatter_blocks(out[5:])
    ready((rows, act, dy, dg, du), (blocks, sact, grad_blocks, dsg, dsu))
    parts = sums.step(parts)
    dh2 = add_blocks(jnp.zeros(middle.shape, F32), [part[:tokens] for part in parts])
    tails = [part[tokens : tokens + 2, :tokens].astype(F32) for part in parts]
    column = jnp.arange(experts, dtype=I32)[None, :]
    dgates = sum(
        jnp.where(column == (me ^ k), (tail[0] + tail[1])[:, None], 0.0) for k, tail in enumerate(tails)
    )
    router, chosen = meta[:tokens, :experts], info[:tokens, :experts]
    picked = jnp.sum(router * chosen, axis=-1, keepdims=True)
    inner = jnp.sum(dgates * router * chosen, axis=-1, keepdims=True) / picked
    dprob = chosen * (dgates - inner) / picked
    dlogits = (router * (dprob - jnp.sum(router * dprob, axis=-1, keepdims=True))).astype(BF)
    dh2 = dh2 + mm(dlogits, w_small[:, :experts], 1, 1)
    dmiddle_norm, dgain = norm_backward(dh2, middle, scale, gain)
    dmiddle = grad_blocks[0].astype(F32) + dmiddle_norm
    return dmiddle, dgain, dlogits


def halves(rows_of, grads, core):
    send = mm(half_of(rows_of, 1 - core, 1), grads, 0, 0, out=BF)
    keep = mm(half_of(rows_of, core, 1), grads, 0, 0)
    return (keep + swap_cores(send).astype(F32)).astype(BF)


def halves_by_member(rows_of, grads, core, members):
    split = rows_of.reshape(rows_of.shape[0], members, 2, -1)

    def side(which):
        return lax.dynamic_index_in_dim(split, which, 2, False).reshape(rows_of.shape[0], -1)

    send = mm(side(1 - core), grads, 0, 0, out=BF)
    keep = mm(side(core), grads, 0, 0)
    return (keep + swap_cores(send).astype(F32)).astype(BF).reshape(members, -1, grads.shape[1])


def expert_grads(terms, core):
    rows, act, dy, dg, du = terms
    g_in = jnp.concatenate([halves(rows, dg, core), halves(rows, du, core)], axis=1)
    return halves(act, dy, core), g_in


def shared_grads(terms, core):
    blocks, sact, grad_blocks, dsg, dsu = terms
    members = len(blocks)
    hidden_all, grad_all = jnp.concatenate(blocks), jnp.concatenate(grad_blocks)
    g_in = halves_by_member(hidden_all, jnp.concatenate([dsg, dsu], axis=1), core, members)
    return halves(sact, grad_all, core), a2a(g_in, EXP)


def dense_grads(terms, core, members):
    hidden_one, dqkv, mixed, dattn, hidden_two, dlogits, dgains = terms
    width, experts = hidden_one.shape[1], dlogits.shape[1]
    small = jnp.concatenate(
        [mm(hidden_two, dlogits, 0, 0), jnp.stack(dgains, axis=1), jnp.zeros((width, 126 - experts), F32)],
        axis=1,
    )
    split = small.reshape(members, 2, -1, 128)
    send = lax.dynamic_index_in_dim(split, 1 - core, 1, False).astype(BF)
    keep = lax.dynamic_index_in_dim(split, core, 1, False)
    small = (keep + swap_cores(send).astype(F32)).astype(BF)
    g_out = halves_by_member(mixed, dattn, core, members)
    g_qkv = halves_by_member(hidden_one, dqkv, core, members)
    parts = a2a(jnp.concatenate([g_qkv, g_out, small], axis=2), EXP)
    return jnp.sum(parts.astype(F32), axis=0).astype(BF)


def local(
    inputs, cotangent, lengths, deal, routes, order, gains, w_qkv, w_out, w_router, w_shared_in, w_shared_down,
    w_expert_in, w_expert_down,
):
    core, me = lax.axis_index(SEC), lax.axis_index(EXP)
    members, lanes = lax.axis_size(EXP), lax.axis_size(DP)
    batches, _, tokens, width = inputs.shape
    experts = w_router.shape[2]
    assert batches == lax.axis_size(SEC) == 2 and w_expert_in.shape[1] == 1 and experts == members
    w = Weights(
        core, members, gains[0], w_qkv[0], w_out[0], w_router[0], w_shared_in[0], w_shared_down[0],
        w_expert_in[0, 0], w_expert_down[0, 0],
    )
    first_low = lax.dynamic_index_in_dim(inputs[:, 0], core, 0, False)
    grad_low = lax.dynamic_index_in_dim(cotangent[:, 0], core, 0, False)
    row = lax.dynamic_index_in_dim(deal, core * members + me, 0, False)
    ends = jnp.cumsum(lax.dynamic_index_in_dim(lengths, row, 0, False))[:-1].astype(I32)
    qkv_0, w_small_0, gains_0 = w.split_first(w.both_halves(w.permuted(w.first_shares[0])))
    current_0 = first_low.astype(F32)
    hidden_0, scale_0 = norm_apply(current_0, gains_0[0])
    projected = mm(hidden_0, qkv_0, out=BF)
    pairs = lax.dynamic_index_in_dim(routes[:, 0], core, 0, False).reshape(-1)
    places = lax.dynamic_index_in_dim(order[:, 0], core, 0, False)
    same = pairs[:, None] == pairs[None, :]
    rank = jnp.sum((same & (places[None, :] < places[:, None])).astype(I32), axis=1)
    code = jnp.stack(gather_blocks(after(pairs * (2 * tokens) + rank, projected), members))
    owner = me ^ jnp.arange(members, dtype=I32)
    pairs_all, rank_all = code // (2 * tokens), code % (2 * tokens)
    onehot = (pairs_all[:, :, None] == jnp.arange(experts, dtype=I32)).astype(I32)
    counts = jnp.sum(onehot, axis=1)
    lower = (owner[None, :] < owner[:, None]).astype(I32)
    before = jnp.sum(lower[:, :, None] * counts[None], axis=1)
    place = jnp.sum(onehot * before[:, None, :], axis=2) + rank_all
    capacity = 2 * tokens * members // experts
    slot = jnp.where((pairs_all == me) & (place < capacity), place, -1)
    slot = jnp.max(slot.reshape(members, tokens, 2), axis=2)
    column = jnp.arange(128, dtype=I32)[None, :]
    named = pairs_all.reshape(members * tokens, 2)
    chosen = (named[:, :1] == column) | (named[:, 1:] == column)
    info = jnp.where(column == SPOT, slot.reshape(-1, 1).astype(F32), chosen.astype(F32))

    w_out_0 = w.both_halves(w.permuted(after(w.out_shares[0], projected)))
    shared_in = w.shared_in(after(w.w_sin, projected))
    shared = (shared_in, w.w_sdown)
    shared = (shared, (swap_cores(shared_in), swap_cores(w.w_sdown)))
    expert_weights = ((w.w_ein, w.w_edown), (swap_cores(w.w_ein), swap_cores(w.w_edown)))
    which = [jnp.stack([me, (core == s).astype(I32)]) for s in range(2)]
    heads_0 = to_heads(projected, lanes, 3)
    heads_0, slot, info, w_out_0 = lax.optimization_barrier((heads_0, slot, info, w_out_0))
    context = (me, slot, info, capacity, experts)
    later = jnp.concatenate([w.first_shares[1], w.out_shares[1]], axis=1)
    mixed_0, shared = lax.optimization_barrier((attention_forward(ends, heads_0, tokens), shared))
    mixed_0 = to_tokens(mixed_0, lanes, 1)
    shared_first = [by_core(core, mine, other) for mine, other in zip(*shared)]
    mixed_0, shared_first = lax.optimization_barrier((mixed_0, shared_first))
    shared_second = [by_core(core, other, mine) for mine, other in zip(*shared)]
    middle_0 = current_0 + mm(mixed_0, w_out_0)
    gathered = []

    def land(out):
        out, full = lax.optimization_barrier((out, lax.all_gather(after(later, middle_0), EXP)))
        gathered.append(full)
        return out

    mlp_0 = (gains_0[1], w_small_0, *shared_first, expert_weights, which[0])
    out_0, saved_0 = layer_mlp(middle_0, context, mlp_0, land)
    dense_1 = w.both_halves(gathered[0])
    low_0, dense_1, shared_second = lax.optimization_barrier((out_0.astype(BF), dense_1, shared_second))
    qkv_1, w_small_1, gains_1 = w.split_first(dense_1)
    w_out_1 = dense_1[:, 3 * width + 128 :]
    current_1 = low_0.astype(F32)
    hidden_1, scale_1 = norm_apply(current_1, gains_1[0])
    projected = mm(hidden_1, qkv_1, out=BF)
    grad_blocks = gather_blocks(after(grad_low, projected), members)
    heads_1 = to_heads(projected, lanes, 3)
    heads_1, grad_blocks = lax.optimization_barrier((heads_1, grad_blocks))
    mixed_1 = to_tokens(attention_forward(ends, heads_1, tokens), lanes, 1)
    middle_1 = current_1 + mm(mixed_1, w_out_1)
    mlp_1 = (gains_1[1], w_small_1, *shared_second, expert_weights, which[1])
    out_1, saved_1 = layer_mlp(middle_1, context, mlp_1)
    low_1 = out_1.astype(BF)

    sums = LineSums()

    def backward(section, grad_blocks, current, hidden, scale, heads, mixed, middle, saved, gain, w_qkv_s, w_out_s, mlp):
        shared = []

        def ready(terms, shared_terms):
            down, ein = expert_grads(terms, core)
            sums.add(section, 0, cut(down, CHUNKS[0]))
            sums.add(section, 1, cut(ein, CHUNKS[1]))
            shared.append(shared_terms)

        dmiddle, dgain_two, dlogits = mlp_backward(grad_blocks, middle, saved, context, mlp, sums, ready)
        dattn = dmiddle.astype(BF)
        dheads = to_heads(mm(dattn, w_out_s, 1, 1, out=BF), lanes, 1)
        g_sdown, g_sin = shared_grads(shared[0], core)
        sums.add(section, 2, [g_sdown])
        sums.add(section, 3, [g_sin.reshape(-1, g_sin.shape[2])])
        dheads = sums.step(dheads)
        dheads = sums.step(attention_backward(ends, heads, dheads, tokens))
        dqkv = sums.step(to_tokens(dheads, lanes, 3))
        dinput, dgain_one = norm_backward(mm(dqkv, w_qkv_s, 1, 1), current, scale, gain)
        dense = (hidden, dqkv, mixed, dattn, saved[1], dlogits, (dgain_one, dgain_two))
        sums.add(section, 4, [dense_grads(dense, core, members)])
        return dmiddle + dinput

    grad_1 = backward(
        1, grad_blocks, current_1, hidden_1, scale_1, heads_1, mixed_1, middle_1, saved_1, gains_1[0], qkv_1,
        w_out_1, mlp_1,
    )
    grad_blocks = sums.step(gather_blocks(grad_1.astype(BF), members))
    grad_0 = backward(
        0, grad_blocks, current_0, hidden_0, scale_0, heads_0, mixed_0, middle_0, saved_0, gains_0[0], qkv_0,
        w_out_0, mlp_0,
    )
    quarter = FF // members

    def by_columns(half):
        blocks = half.reshape(members, -1, 2 * quarter)
        return jnp.concatenate(
            [blocks[j][:, at : at + quarter] for at in (0, quarter) for j in range(members)], axis=1
        )

    def whole(name):
        own_0, got_0 = zip(*sums.result(0, name))
        own_1, got_1 = zip(*sums.result(1, name))
        pairs = zip(own_0 + got_0, got_1 + own_1)
        parts = [by_core(core, a, b) for a, b in pairs]
        return jnp.concatenate([by_columns(v) if name == 3 else v for v in parts]).astype(F32)

    def complete(name):
        return all(len(sums.result(section, name)) == CHUNKS[name] for section in range(2))

    results = {}
    while sums.busy():
        results = sums.step(results, *TAIL_STEP)
        results.update({name: whole(name) for name in range(5) if name not in results and complete(name)})

    def to_section(of_0, of_1):
        mine = by_core(core, of_0, of_1)
        other = swap_cores(by_core(core, of_1, of_0))
        both = jnp.stack([by_core(core, mine, other), by_core(core, other, mine)])
        return both[None, :, None]

    down, ein, sdown, sin, dense = [results[name] for name in range(5)]
    at = 4 * width
    return (
        to_section(low_0, low_1),
        to_section(grad_0, grad_1),
        dense[:, at + experts : at + experts + 2].T[None],
        dense[None, :, : 3 * width],
        dense[None, :, 3 * width : at],
        dense[None, :, at : at + experts],
        sin[None],
        sdown[None],
        ein[None, None],
        down[None, None],
    )


def solution(mesh):
    tokens = P(None, EXP, DP, None)
    dense = P(SEC, EXP, None)
    expert = P(SEC, EXP, None, None)
    both = P(SEC, None, EXP, DP, None)
    gains = P(SEC, None, EXP)
    return jax.shard_map(
        local,
        mesh=mesh,
        in_specs=(tokens, tokens, P(), P(), tokens, P(None, EXP, DP), gains)
        + (dense,) * 5
        + (expert,) * 2,
        out_specs=(both, both, gains) + (dense,) * 5 + (expert,) * 2,
        check_vma=False,
    )
```

time: 1240 us -> 1020 us (0.82)
  waiting for transfers between devices: 593 us -> 275 us
  starting transfers between devices: 133 us -> 270 us
  matrix products: 208 us -> 82.9 us
  Pallas kernels: 37.9 us -> 124 us
  other arithmetic: 80.1 us -> 160 us
  blocking collectives: 68.3 us -> 0 us
    psum x4 -> x0, waiting for transfers between devices: 406 us -> none  [lane_sums(): sums = lax.psum(tuple(group), DP)]
    dot_general x62 -> x40, matrix products: 208 us -> 82.9 us  [mm(): lax.dot_general(a, b, (((ca,), (cb,)), ((), ())), preferred_element_type=...]
    ppermute x10 -> x48, starting transfers between devices: 20.5 us -> 142 us  [launch(): got = lax.ppermute(value, axis, pairs)]
    ppermute x10 -> x48, waiting for transfers between devices: 0.03 us -> 101 us  [launch(): got = lax.ppermute(value, axis, pairs)]
    pallas_call x0 -> x4, Pallas kernels: none -> 86.4 us  [moe_call(): pl.pallas_call(kernel, out_shape=[jax.ShapeDtypeStruct(*shape) for shape...]
    all_to_all x3 -> x0, blocking collectives: 68.3 us -> none  [a2a(): return lax.all_to_all(v, axis, split_axis=0, concat_axis=0, tiled=True)]
    convert_element_type x11 -> x46, other arithmetic: 3.54 us -> 69.9 us  [the longest x24 53.9 us: add_low(): return (a.astype(F32) + b.astype(F32)).astype(BF)]
    all_to_all x10 -> x12, waiting for transfers between devices: 40.8 us -> 88.2 us  [a2a(): return lax.all_to_all(v, axis, split_axis=0, concat_axis=0, tiled=True)]
  transfers between devices with their start and end apart: 83 -> 124, of which waited for: 37 -> 30; matrix products, arithmetic and copies ran while one was open for 22% -> 28% of each run, Pallas kernels for 2% -> 10%
where the time goes in v1:
time: 1020 us; the launch traced here: 1010 us
  waiting for transfers between devices  275 us (27%)
  starting transfers between devices  270 us (26%)
  other arithmetic  160 us (16%)
  Pallas kernels  124 us (12%)
  matrix products  82.9 us (8%)
  local copies, waits for them, and re-layouts  81.1 us (8%)
  between operations  18.8 us (2%)
    ppermute x48, starting transfers between devices, launch(): got = lax.ppermute(value, axis, pairs)  142 us
    ppermute x48, waiting for transfers between devices, launch(): got = lax.ppermute(value, axis, pairs)  101 us
    all_to_all x12, waiting for transfers between devices, a2a(): return lax.all_to_all(v, axis, split_axis=0, concat_axis=0, tiled=True)  88.2 us
    pallas_call x4, Pallas kernels, moe_call(): pl.pallas_call(kernel, out_shape=[jax.ShapeDtypeStruct(*shape) for shape...  86.4 us
    dot_general x40, matrix products, mm(): lax.dot_general(a, b, (((ca,), (cb,)), ((), ())), preferred_element_type=...  82.9 us
    convert_element_type x24, other arithmetic, add_low(): return (a.astype(F32) + b.astype(F32)).astype(BF)  53.9 us
    all_to_all x12, starting transfers between devices, a2a(): return lax.all_to_all(v, axis, split_axis=0, concat_axis=0, tiled=True)  52.2 us
    ppermute x21, waiting for transfers between devices, gather_blocks(): lax.ppermute(v, EXP, xor_pairs(members, k))  48.7 us
  transfers between devices with their start and end apart: 124, of which 30 were waited for; matrix products, arithmetic and copies ran while one was open for 28% of the time, Pallas kernels for 10%

profile of v1, /device:TPU:1, one launch (start us, length us, event | category | flops | bytes accessed | tf_op | source)
XLA Modules:
  0.0 1011.1 jit_solution(10519191063149092011)
XLA Ops:
  17.8 8.8 collective-permute-done.3
  26.6 10.3 %collective-permute-done.2 = bf16[96,2432]{1,0:T(8,128)(2,1)S(1)} collective-permute-done((bf16[96,2432]{1,0:T(8,128)(2,1)S(1)}, bf16[96,2432]{1,0:T(8,128)(2,1)S(1)}, u32[]{:S(2)}, u32[]{:S(2)}) %collective-permute-start.2) | collective-permute-done | bytes 466976 | tf_op jit(solution)/shard_map/ppermute | solution.py:41
  58.4 4.9 all-to-all-start
  79.6 9.3 collective-permute-done.14
  103.6 6.6 shard_map.213
  111.3 4.5 all-to-all-start.1
  122.6 4.4 all-to-all-done.1
  143.1 14.5 %collective-permute-done.20.refs_7_ = bf16[256,768]{1,0:T(8,128)(2,1)} collective-permute-done((bf16[256,768]{1,0:T(8,128)(2,1)S(1)}, bf16[256,768]{1,0:T(8,128)(2,1)}, u32[]{:S(2)}, u32[]{:S(2)}) %collective-permute-start.20) | collective-permute-done | bytes 393248 | tf_op jit(solution)/shard_map/ppermute | solution.py:41
  157.6 20.4 %shard_map.214 = (bf16[512,768]{1,0:T(8,128)(2,1)}, bf16[512,2048]{1,0:T(8,128)(2,1)}, bf16[512,2048]{1,0:T(8,128)(2,1)}, bf16[512,2048]{1,0:T(8,128)(2,1)}, f32...) custom-call(s32[2]{0:T(128)} %pad_add_fusion.1.refs_0_, ...), custom_call_target="tpu_custom_call" | custom-call | flops 8858370048 | bytes 31457280 | tf_op jit(solution)/shard_map/pallas_call | solution.py:366
  183.6 9.2 collective-permute-done.25
  192.8 8.5 collective-permute-done.24
  215.1 4.6 all-to-all-start.2
  225.9 22.0 %all-to-all-done.2 = bf16[4,256,576]{1,2,0:T(8,128)(2,1)} async-done(((bf16[4,256,576]{1,2,0:T(8,128)(2,1)}), bf16[4,256,576]{1,2,0:T(8,128)(2,1)}, u32[]{:S(2)}, u32[]{:S(2)}) %all-to-all-start.2) | async-done | bytes 1179680 | tf_op jit(solution)/shard_map/all_to_all | solution.py:29
  249.5 6.6 shard_map.215
  288.9 8.4 collective-permute-done.32.refs_7_
  298.0 20.4 %shard_map.216 = (bf16[512,768]{1,0:T(8,128)(2,1)}, bf16[512,2048]{1,0:T(8,128)(2,1)}, bf16[512,2048]{1,0:T(8,128)(2,1)}, bf16[512,2048]{1,0:T(8,128)(2,1)}, f32...) custom-call(s32[2]{0:T(128)} %pad_add_fusion.2.refs_0_, ...), custom_call_target="tpu_custom_call" | custom-call | flops 8858370048 | bytes 31457280 | tf_op jit(solution)/shard_map/pallas_call | solution.py:366
  321.2 22.8 %shard_map.217 = (bf16[512,768]{1,0:T(8,128)(2,1)}, bf16[512,2048]{1,0:T(8,128)(2,1)}, bf16[512,2048]{1,0:T(8,128)(2,1)}, bf16[1024,512]{1,0:T(8,128)(2,1)}, bf1...) custom-call(s32[2]{0:T(128)} %pad_add_fusion.2.refs_0_, ...), custom_call_target="tpu_custom_call" | custom-call | flops 8858370048 | bytes 31457280 | tf_op jit(solution)/shard_map/pallas_call | solution.py:366
  382.0 9.1 collective-permute-start.36
  391.2 4.5 collective-permute-start.43
  415.1 19.9 %all-to-all-done.4 = bf16[4,256,192]{1,2,0:T(8,128)(2,1)} async-done(((bf16[4,256,192]{1,2,0:T(8,128)(2,1)}), bf16[4,256,192]{1,2,0:T(8,128)(2,1)}, u32[]{:S(2)}, u32[]{:S(2)}) %all-to-all-start.4) | async-done | bytes 393248 | tf_op jit(solution)/shard_map/all_to_all | solution.py:29
  436.2 12.1 %shard_map.218 = bf16[1024,576]{1,0:T(8,128)(2,1)S(1)} custom-call(s32[2]{0:T(128)S(1)} %slice_bitcast_fusion.1.ends_ref, bf16[1024,576]{1,0:T(8,128)(2,1)S(1)} %bitcast.272, bf16[1024,192]{1,0:T(8,128)(2,1)S(1)} %bitcast.277), custom_call_target="tpu_custom_call" | custom-call | flops 2013265920 | bytes 3145728 | tf_op jit(solution)/shard_map/pallas_call | solution.py:169
  451.7 4.5 all-to-all-start.5
  457.6 6.1 collective-permute-start.44
  491.2 17.3 %collective-permute-done.44 = bf16[192,4096]{1,0:T(8,128)(2,1)} collective-permute-done((bf16[192,4096]{1,0:T(8,128)(2,1)}, bf16[192,4096]{1,0:T(8,128)(2,1)}, u32[]{:S(2)}, u32[]{:S(2)}) %collective-permute-start.44) | collective-permute-done | bytes 1572896 | tf_op jit(solution)/shard_map/ppermute | solution.py:502
  528.6 13.6 %collective-permute-done.50 = bf16[192,4096]{1,0:T(8,128)(2,1)} collective-permute-done((bf16[192,4096]{1,0:T(8,128)(2,1)}, bf16[192,4096]{1,0:T(8,128)(2,1)}, u32[]{:S(2)}, u32[]{:S(2)}) %collective-permute-start.50) | collective-permute-done | bytes 1572896 | tf_op jit(solution)/shard_map/ppermute | solution.py:502
  544.0 7.1 collective-permute-start.53
  565.5 5.0 all-to-all-start.7
  575.9 22.8 %shard_map.219 = (bf16[512,768]{1,0:T(8,128)(2,1)}, bf16[512,2048]{1,0:T(8,128)(2,1)}, bf16[512,2048]{1,0:T(8,128)(2,1)}, bf16[1024,512]{1,0:T(8,128)(2,1)}, bf1...) custom-call(s32[2]{0:T(128)} %pad_add_fusion.1.refs_0_, ...), custom_call_target="tpu_custom_call" | custom-call | flops 8858370048 | bytes 31457280 | tf_op jit(solution)/shard_map/pallas_call | solution.py:366
  598.7 5.7 collective-permute-start.62
  634.6 8.2 collective-permute-start.66
  677.1 6.4 collective-permute-start.72
  705.1 11.9 %shard_map.220 = bf16[1024,576]{1,0:T(8,128)(2,1)S(1)} custom-call(s32[2]{0:T(128)S(1)} %slice_bitcast_fusion.1.ends_ref, bf16[1024,576]{1,0:T(8,128)(2,1)S(1)} %bitcast.270, bf16[1024,192]{1,0:T(8,128)(2,1)S(1)} %bitcast.275), custom_call_target="tpu_custom_call" | custom-call | flops 2013265920 | bytes 3145728 | tf_op jit(solution)/shard_map/pallas_call | solution.py:169
  717.0 5.9 collective-permute-start.76
  741.2 30.9 %all-to-all-done.9 = bf16[4,256,576]{1,2,0:T(8,128)(2,1)S(1)} async-done(((bf16[4,256,576]{1,2,0:T(8,128)(2,1)}), bf16[4,256,576]{1,2,0:T(8,128)(2,1)S(1)}, u32[]{:S(2)}, u32[]{:S(2)}) %all-to-all-start.9) | async-done | bytes 1179680 | tf_op jit(solution)/shard_map/all_to_all | solution.py:29
  779.5 6.7 collective-permute-start.85
  817.1 7.4 collective-permute-start.82
  834.9 5.1 all-to-all-done.11
  843.3 7.0 collective-permute-start.97
  855.4 10.0 collective-permute-done.97
  866.7 11.1 %collective-permute-done.95 = bf16[1024,768]{1,0:T(8,128)(2,1)S(1)} collective-permute-done((bf16[1024,768]{1,0:T(8,128)(2,1)}, bf16[1024,768]{1,0:T(8,128)(2,1)S(1)}, u32[]{:S(2)}, u32[]{:S(2)}) %collective-permute-start.95) | collective-permute-done | bytes 1572896 | tf_op jit(solution)/shard_map/ppermute | solution.py:502
  877.9 6.5 collective-permute-start.99
  889.0 13.5 %collective-permute-start.94 = (bf16[96,3200]{1,0:T(8,128)(2,1)S(1)}, bf16[96,3200]{1,0:T(8,128)(2,1)S(1)}, u32[]{:S(2)}, u32[]{:S(2)}) collective-permute-start(bf16[96,3200]{1,0:T(8,128)(2,1)S(1)} %copy-done.44), channel_id=1, source_target_pairs={{0,4},{12,8},{1,5},{13,9},{2,6},{14,10},{3,7},{15,11},{16,20},{28,... | collective-permute-start | bytes 1843208 | tf_op jit(solution)/shard_map/ppermute | solution.py:502
  904.3 11.7 %collective-permute-done.94 = bf16[96,3200]{1,0:T(8,128)(2,1)S(1)} collective-permute-done((bf16[96,3200]{1,0:T(8,128)(2,1)S(1)}, bf16[96,3200]{1,0:T(8,128)(2,1)S(1)}, u32[]{:S(2)}, u32[]{:S(2)}) %collective-permute-start.94) | collective-permute-done | bytes 614432 | tf_op jit(solution)/shard_map/ppermute | solution.py:502
  928.9 16.3 %collective-permute-done.100 = bf16[192,4096]{1,0:T(8,128)(2,1)S(1)} collective-permute-done((bf16[192,4096]{1,0:T(8,128)(2,1)S(1)}, bf16[192,4096]{1,0:T(8,128)(2,1)S(1)}, u32[]{:S(2)}, u32[]{:S(2)}) %collective-permute-start.100) | collective-permute-done | bytes 1572896 | tf_op jit(solution)/shard_map/ppermute | solution.py:502
  945.3 6.5 collective-permute-start.105
  960.2 5.3 maximum_convert_fusion
  965.5 8.5 collective-permute-done.106
  981.3 12.6 %collective-permute-done.108 = bf16[96,3200]{1,0:T(8,128)(2,1)S(1)} collective-permute-done((bf16[96,3200]{1,0:T(8,128)(2,1)S(1)}, bf16[96,3200]{1,0:T(8,128)(2,1)S(1)}, u32[]{:S(2)}, u32[]{:S(2)}) %collective-permute-start.108) | collective-permute-done | bytes 614432 | tf_op jit(solution)/shard_map/ppermute | solution.py:502
  (763 shorter events, 487.2 us)
Async XLA Ops:
  17.7 139.9 %collective-permute-start.21 = (bf16[768,4096]{1,0:T(8,128)(2,1)}, bf16[768,4096]{1,0:T(8,128)(2,1)}, u32[]{:S(2)}, u32[]{:S(2)}) collective-permute-start(bf16[768,4096]{1,0:T(8,128)(2,1)} %bitcast.279), channel_id=1, source_target_pairs={{0,16},{16,0},{1,17},{17,1},{2,18},{18,2},{3,19},{19,3},{4,20},{20... | collective-permute-start | bytes 18874376 | tf_op jit(solution)/shard_map/ppermute | solution.py:25
  58.4 43.5 %all-to-all-start = ((bf16[4,256,576]{1,2,0:T(8,128)(2,1)}), bf16[4,256,576]{1,2,0:T(8,128)(2,1)}, u32[]{:S(2)}, u32[]{:S(2)}) async-start(bf16[4,256,576]{1,2,0:T(8,128)(2,1)} %bitcast.17), calls=%async_computation | async-start | bytes 2359296 | tf_op jit(solution)/shard_map/all_to_all | solution.py:29
  94.4 43.2 %collective-permute-start.22 = (bf16[2048,768]{1,0:T(8,128)(2,1)}, bf16[2048,768]{1,0:T(8,128)(2,1)}, u32[]{:S(2)}, u32[]{:S(2)}) collective-permute-start(bf16[2048,768]{1,0:T(8,128)(2,1)} %bitcast.52.refs_10_.refs_11_), channel_id=1, source_target_pairs={{0,16},{16,0},{1,17},{17,1},{2,18},{18,2},{3,19},{19,3},{4,20},{20... | collective-permute-start | bytes 9437192 | tf_op jit(solution)/shard_map/ppermute | solution.py:25
  115.8 62.5 %all-gather.3.cloned.1.call-start = ((), (), s32[]{:S(2)}) async-start(), calls=%async_computation.12 | async-start | bytes 3072000 | tf_op jit(solution)/shard_map/all_gather | solution.py:698
  215.1 32.7 %all-to-all-start.2 = ((bf16[4,256,576]{1,2,0:T(8,128)(2,1)}), bf16[4,256,576]{1,2,0:T(8,128)(2,1)}, u32[]{:S(2)}, u32[]{:S(2)}) async-start(bf16[4,256,576]{1,2,0:T(8,128)(2,1)} %bitcast.61), calls=%async_computation.2 | async-start | bytes 2359296 | tf_op jit(solution)/shard_map/all_to_all | solution.py:29
  318.5 50.2 %collective-permute-start.35 = (bf16[256,768]{1,0:T(8,128)(2,1)}, bf16[256,768]{1,0:T(8,128)(2,1)}, u32[]{:S(2)}, u32[]{:S(2)}) collective-permute-start(bf16[256,768]{1,0:T(8,128)(2,1)} %get-tuple-element.283), channel_id=1, source_target_pairs={{0,3},{1,2},{2,1},{3,0},{4,7},{5,6},{6,5},{7,4},{8,11},{9,10},{10,... | collective-permute-start | bytes 1179656 | tf_op jit(solution)/shard_map/ppermute | solution.py:46
  319.6 50.5 %collective-permute-start.34 = (bf16[256,768]{1,0:T(8,128)(2,1)}, bf16[256,768]{1,0:T(8,128)(2,1)}, u32[]{:S(2)}, u32[]{:S(2)}) collective-permute-start(bf16[256,768]{1,0:T(8,128)(2,1)} %get-tuple-element.282), channel_id=1, source_target_pairs={{0,2},{1,3},{2,0},{3,1},{4,6},{5,7},{6,4},{7,5},{8,10},{9,11},{10,... | collective-permute-start | bytes 1179656 | tf_op jit(solution)/shard_map/ppermute | solution.py:46
  321.1 49.3 %collective-permute-start.33 = (bf16[256,768]{1,0:T(8,128)(2,1)}, bf16[256,768]{1,0:T(8,128)(2,1)}, u32[]{:S(2)}, u32[]{:S(2)}) collective-permute-start(bf16[256,768]{1,0:T(8,128)(2,1)} %get-tuple-element.281), channel_id=1, source_target_pairs={{0,1},{1,0},{2,3},{3,2},{4,5},{5,4},{6,7},{7,6},{8,9},{9,8},{10,11... | collective-permute-start | bytes 1179656 | tf_op jit(solution)/shard_map/ppermute | solution.py:46
  374.0 33.2 %collective-permute-start.42 = (bf16[384,2048]{1,0:T(8,128)(2,1)}, bf16[384,2048]{1,0:T(8,128)(2,1)}, u32[]{:S(2)}, u32[]{:S(2)}) collective-permute-start(bf16[384,2048]{1,0:T(8,128)(2,1)} %convolution_convert_fusion.6), channel_id=1, source_target_pairs={{0,16},{16,0},{1,17},{17,1},{2,18},{18,2},{3,19},{19,3},{4,20},{20... | collective-permute-start | bytes 4718600 | tf_op jit(solution)/shard_map/ppermute | solution.py:25
  377.8 32.7 %collective-permute-start.41 = (bf16[384,2048]{1,0:T(8,128)(2,1)}, bf16[384,2048]{1,0:T(8,128)(2,1)}, u32[]{:S(2)}, u32[]{:S(2)}) collective-permute-start(bf16[384,2048]{1,0:T(8,128)(2,1)} %convolution_convert_fusion.7), channel_id=1, source_target_pairs={{0,16},{16,0},{1,17},{17,1},{2,18},{18,2},{3,19},{19,3},{4,20},{20... | collective-permute-start | bytes 4718600 | tf_op jit(solution)/shard_map/ppermute | solution.py:25
  381.8 84.9 %collective-permute-start.51 = (bf16[384,1024]{1,0:T(8,128)(2,1)}, bf16[384,1024]{1,0:T(8,128)(2,1)}, u32[]{:S(2)}, u32[]{:S(2)}) collective-permute-start(bf16[384,1024]{1,0:T(8,128)(2,1)} %convolution_convert_fusion.11), channel_id=1, source_target_pairs={{0,16},{16,0},{1,17},{17,1},{2,18},{18,2},{3,19},{19,3},{4,20},{20... | collective-permute-start | bytes 2359304 | tf_op jit(solution)/shard_map/ppermute | solution.py:25
  382.0 74.2 %collective-permute-start.36 = (bf16[256,768]{1,0:T(8,128)(2,1)}, bf16[256,768]{1,0:T(8,128)(2,1)}, u32[]{:S(2)}, u32[]{:S(2)}) collective-permute-start(bf16[256,768]{1,0:T(8,128)(2,1)} %get-tuple-element.566), channel_id=1, source_target_pairs={{0,16},{16,0},{1,17},{17,1},{2,18},{18,2},{3,19},{19,3},{4,20},{20... | collective-permute-start | bytes 1179656 | tf_op jit(solution)/shard_map/ppermute | solution.py:25
  391.2 58.1 %collective-permute-start.43 = (bf16[1024,768]{1,0:T(8,128)(2,1)}, bf16[1024,768]{1,0:T(8,128)(2,1)}, u32[]{:S(2)}, u32[]{:S(2)}) collective-permute-start(bf16[1024,768]{1,0:T(8,128)(2,1)} %add_convert_fusion.17), channel_id=1, source_target_pairs={{0,4},{12,8},{1,5},{13,9},{2,6},{14,10},{3,7},{15,11},{16,20},{28,... | collective-permute-start | bytes 4718600 | tf_op jit(solution)/shard_map/ppermute | solution.py:502
  451.7 33.9 %all-to-all-start.5 = ((bf16[4,256,576]{1,2,0:T(8,128)(2,1)}), bf16[4,256,576]{1,2,0:T(8,128)(2,1)}, u32[]{:S(2)}, u32[]{:S(2)}) async-start(bf16[4,256,576]{1,2,0:T(8,128)(2,1)} %copy.290), calls=%async_computation.5 | async-start | bytes 2359296 | tf_op jit(solution)/shard_map/all_to_all | solution.py:29
  457.6 50.9 %collective-permute-start.44 = (bf16[192,4096]{1,0:T(8,128)(2,1)}, bf16[192,4096]{1,0:T(8,128)(2,1)}, u32[]{:S(2)}, u32[]{:S(2)}) collective-permute-start(bf16[192,4096]{1,0:T(8,128)(2,1)} %get-tuple-element.337), channel_id=1, source_target_pairs={{0,4},{12,8},{1,5},{13,9},{2,6},{14,10},{3,7},{15,11},{16,20},{28,... | collective-permute-start | bytes 4718600 | tf_op jit(solution)/shard_map/ppermute | solution.py:502
  477.8 45.7 %collective-permute-start.49 = (bf16[1024,768]{1,0:T(8,128)(2,1)}, bf16[1024,768]{1,0:T(8,128)(2,1)}, u32[]{:S(2)}, u32[]{:S(2)}) collective-permute-start(bf16[1024,768]{1,0:T(8,128)(2,1)} %add_convert_fusion.14), channel_id=1, source_target_pairs={{4,8},{8,4},{5,9},{9,5},{6,10},{10,6},{7,11},{11,7},{20,24},{24,20... | collective-permute-start | bytes 4718600 | tf_op jit(solution)/shard_map/ppermute | solution.py:502
  479.6 62.6 %collective-permute-start.50 = (bf16[192,4096]{1,0:T(8,128)(2,1)}, bf16[192,4096]{1,0:T(8,128)(2,1)}, u32[]{:S(2)}, u32[]{:S(2)}) collective-permute-start(bf16[192,4096]{1,0:T(8,128)(2,1)} %get-tuple-element.346), channel_id=1, source_target_pairs={{0,4},{12,8},{1,5},{13,9},{2,6},{14,10},{3,7},{15,11},{16,20},{28,... | collective-permute-start | bytes 4718600 | tf_op jit(solution)/shard_map/ppermute | solution.py:502
  485.6 65.5 %all-to-all-start.6 = ((bf16[4,96,1024]{2,1,0:T(8,128)(2,1)}), bf16[4,96,1024]{2,1,0:T(8,128)(2,1)}, u32[]{:S(2)}, u32[]{:S(2)}) async-start(bf16[4,96,1024]{2,1,0:T(8,128)(2,1)} %bitcast.88), calls=%async_computation.6 | async-start | bytes 1572864 | tf_op jit(solution)/shard_map/all_to_all | solution.py:29
  513.2 38.0 %collective-permute-start.47 = (bf16[256,768]{1,0:T(8,128)(2,1)}, bf16[256,768]{1,0:T(8,128)(2,1)S(1)}, u32[]{:S(2)}, u32[]{:S(2)}) collective-permute-start(bf16[256,768]{1,0:T(8,128)(2,1)} %get-tuple-element.318.refs_4_), channel_id=1, source_target_pairs={{0,2},{1,3},{2,0},{3,1},{4,6},{5,7},{6,4},{7,5},{8,10},{9,11},{10,... | collective-permute-start | bytes 1179656 | tf_op jit(solution)/shard_map/ppermute | solution.py:41
  524.7 36.9 %collective-permute-start.54 = (bf16[384,2304]{1,0:T(8,128)(2,1)}, bf16[384,2304]{1,0:T(8,128)(2,1)}, u32[]{:S(2)}, u32[]{:S(2)}) collective-permute-start(bf16[384,2304]{1,0:T(8,128)(2,1)} %convolution_convert_fusion.1), channel_id=1, source_target_pairs={{0,16},{16,0},{1,17},{17,1},{2,18},{18,2},{3,19},{19,3},{4,20},{20... | collective-permute-start | bytes 5308424 | tf_op jit(solution)/shard_map/ppermute | solution.py:25
  542.2 66.6 %collective-permute-start.52 = (bf16[192,4096]{1,0:T(8,128)(2,1)}, bf16[192,4096]{1,0:T(8,128)(2,1)}, u32[]{:S(2)}, u32[]{:S(2)}) collective-permute-start(bf16[192,4096]{1,0:T(8,128)(2,1)} %add_convert_fusion.13), channel_id=1, source_target_pairs={{4,8},{8,4},{5,9},{9,5},{6,10},{10,6},{7,11},{11,7},{20,24},{24,20... | collective-permute-start | bytes 4718600 | tf_op jit(solution)/shard_map/ppermute | solution.py:502
  544.0 64.8 %collective-permute-start.53 = (bf16[256,768]{1,0:T(8,128)(2,1)}, bf16[256,768]{1,0:T(8,128)(2,1)}, u32[]{:S(2)}, u32[]{:S(2)}) collective-permute-start(bf16[256,768]{1,0:T(8,128)(2,1)} %fusion.10), channel_id=1, source_target_pairs={{0,4},{12,8},{1,5},{13,9},{2,6},{14,10},{3,7},{15,11},{16,20},{28,... | collective-permute-start | bytes 1179656 | tf_op jit(solution)/shard_map/ppermute | solution.py:502
  554.8 77.1 %collective-permute-start.60 = (bf16[1024,768]{1,0:T(8,128)(2,1)}, bf16[1024,768]{1,0:T(8,128)(2,1)}, u32[]{:S(2)}, u32[]{:S(2)}) collective-permute-start(bf16[1024,768]{1,0:T(8,128)(2,1)} %add_convert_fusion.12), channel_id=1, source_target_pairs={{4,0},{8,12},{5,1},{9,13},{6,2},{10,14},{7,3},{11,15},{20,16},{24,... | collective-permute-start | bytes 4718600 | tf_op jit(solution)/shard_map/ppermute | solution.py:502
  559.8 73.4 %collective-permute-start.61 = (bf16[192,4096]{1,0:T(8,128)(2,1)}, bf16[192,4096]{1,0:T(8,128)(2,1)}, u32[]{:S(2)}, u32[]{:S(2)}) collective-permute-start(bf16[192,4096]{1,0:T(8,128)(2,1)} %add_convert_fusion.11), channel_id=1, source_target_pairs={{4,8},{8,4},{5,9},{9,5},{6,10},{10,6},{7,11},{11,7},{20,24},{24,20... | collective-permute-start | bytes 4718600 | tf_op jit(solution)/shard_map/ppermute | solution.py:502
  565.5 40.3 %all-to-all-start.7 = ((bf16[4,96,3200]{2,1,0:T(8,128)(2,1)}), bf16[4,96,3200]{2,1,0:T(8,128)(2,1)}, u32[]{:S(2)}, u32[]{:S(2)}) async-start(bf16[4,96,3200]{2,1,0:T(8,128)(2,1)} %pad_maximum_fusion.2), calls=%async_computation.7 | async-start | bytes 4915200 | tf_op jit(solution)/shard_map/all_to_all | solution.py:29
  631.9 51.6 %collective-permute-start.64 = (bf16[192,4096]{1,0:T(8,128)(2,1)}, bf16[192,4096]{1,0:T(8,128)(2,1)}, u32[]{:S(2)}, u32[]{:S(2)}) collective-permute-start(bf16[192,4096]{1,0:T(8,128)(2,1)} %add_convert_fusion.9), channel_id=1, source_target_pairs={{4,0},{8,12},{5,1},{9,13},{6,2},{10,14},{7,3},{11,15},{20,16},{24,... | collective-permute-start | bytes 4718600 | tf_op jit(solution)/shard_map/ppermute | solution.py:502
  633.2 42.6 %collective-permute-start.65 = (bf16[256,768]{1,0:T(8,128)(2,1)}, bf16[256,768]{1,0:T(8,128)(2,1)}, u32[]{:S(2)}, u32[]{:S(2)}) collective-permute-start(bf16[256,768]{1,0:T(8,128)(2,1)} %add_convert_fusion.33), channel_id=1, source_target_pairs={{4,8},{8,4},{5,9},{9,5},{6,10},{10,6},{7,11},{11,7},{20,24},{24,20... | collective-permute-start | bytes 1179656 | tf_op jit(solution)/shard_map/ppermute | solution.py:502
  634.6 42.5 %collective-permute-start.66 = (bf16[96,3200]{1,0:T(8,128)(2,1)}, bf16[96,3200]{1,0:T(8,128)(2,1)}, u32[]{:S(2)}, u32[]{:S(2)}) collective-permute-start(bf16[96,3200]{1,0:T(8,128)(2,1)} %reduce_sum.240), channel_id=1, source_target_pairs={{0,4},{12,8},{1,5},{13,9},{2,6},{14,10},{3,7},{15,11},{16,20},{28,... | collective-permute-start | bytes 1843208 | tf_op jit(solution)/shard_map/ppermute | solution.py:502
  675.8 47.0 %collective-permute-start.70 = (bf16[192,4096]{1,0:T(8,128)(2,1)}, bf16[192,4096]{1,0:T(8,128)(2,1)}, u32[]{:S(2)}, u32[]{:S(2)}) collective-permute-start(bf16[192,4096]{1,0:T(8,128)(2,1)} %add_convert_fusion.6), channel_id=1, source_target_pairs={{4,0},{8,12},{5,1},{9,13},{6,2},{10,14},{7,3},{11,15},{20,16},{24,... | collective-permute-start | bytes 4718600 | tf_op jit(solution)/shard_map/ppermute | solution.py:502
  677.1 45.7 %collective-permute-start.72 = (bf16[1024,768]{1,0:T(8,128)(2,1)}, bf16[1024,768]{1,0:T(8,128)(2,1)}, u32[]{:S(2)}, u32[]{:S(2)}) collective-permute-start(bf16[1024,768]{1,0:T(8,128)(2,1)} %add_convert_fusion.10), channel_id=1, source_target_pairs={{0,4},{12,8},{1,5},{13,9},{2,6},{14,10},{3,7},{15,11},{16,20},{28,... | collective-permute-start | bytes 4718600 | tf_op jit(solution)/shard_map/ppermute | solution.py:502
  688.5 34.3 %collective-permute-start.73 = (bf16[192,4096]{1,0:T(8,128)(2,1)}, bf16[192,4096]{1,0:T(8,128)(2,1)}, u32[]{:S(2)}, u32[]{:S(2)}) collective-permute-start(bf16[192,4096]{1,0:T(8,128)(2,1)} %broadcast_select_fusion.9), channel_id=1, source_target_pairs={{0,16},{1,17},{2,18},{3,19},{4,20},{5,21},{6,22},{7,23},{8,24},{9,... | collective-permute-start | bytes 4718600 | tf_op jit(solution)/shard_map/ppermute | solution.py:502
  703.4 74.3 %collective-permute-start.74 = (bf16[256,768]{1,0:T(8,128)(2,1)}, bf16[256,768]{1,0:T(8,128)(2,1)}, u32[]{:S(2)}, u32[]{:S(2)}) collective-permute-start(bf16[256,768]{1,0:T(8,128)(2,1)} %add_convert_fusion.32), channel_id=1, source_target_pairs={{4,0},{8,12},{5,1},{9,13},{6,2},{10,14},{7,3},{11,15},{20,16},{24,... | collective-permute-start | bytes 1179656 | tf_op jit(solution)/shard_map/ppermute | solution.py:502
  717.0 69.3 %collective-permute-start.76 = (bf16[192,4096]{1,0:T(8,128)(2,1)}, bf16[192,4096]{1,0:T(8,128)(2,1)}, u32[]{:S(2)}, u32[]{:S(2)}) collective-permute-start(bf16[192,4096]{1,0:T(8,128)(2,1)} %get-tuple-element.385), channel_id=1, source_target_pairs={{0,4},{12,8},{1,5},{13,9},{2,6},{14,10},{3,7},{15,11},{16,20},{28,... | collective-permute-start | bytes 4718600 | tf_op jit(solution)/shard_map/ppermute | solution.py:502
  724.3 47.8 %all-to-all-start.9 = ((bf16[4,256,576]{1,2,0:T(8,128)(2,1)}), bf16[4,256,576]{1,2,0:T(8,128)(2,1)S(1)}, u32[]{:S(2)}, u32[]{:S(2)}) async-start(bf16[4,256,576]{1,2,0:T(8,128)(2,1)} %copy.300), calls=%async_computation.9 | async-start | bytes 2359296 | tf_op jit(solution)/shard_map/all_to_all | solution.py:29
  729.8 56.5 %collective-permute-start.77 = (bf16[192,4096]{1,0:T(8,128)(2,1)S(1)}, bf16[192,4096]{1,0:T(8,128)(2,1)}, u32[]{:S(2)}, u32[]{:S(2)}) collective-permute-start(bf16[192,4096]{1,0:T(8,128)(2,1)S(1)} %broadcast_select_fusion.8), channel_id=1, source_target_pairs={{0,16},{1,17},{2,18},{3,19},{4,20},{5,21},{6,22},{7,23},{8,24},{9,... | collective-permute-start | bytes 4718600 | tf_op jit(solution)/shard_map/ppermute | solution.py:502
  732.5 47.0 %collective-permute-start.75 = (bf16[96,3200]{1,0:T(8,128)(2,1)S(1)}, bf16[96,3200]{1,0:T(8,128)(2,1)}, u32[]{:S(2)}, u32[]{:S(2)}) collective-permute-start(bf16[96,3200]{1,0:T(8,128)(2,1)S(1)} %add_convert_fusion.27), channel_id=1, source_target_pairs={{4,8},{8,4},{5,9},{9,5},{6,10},{10,6},{7,11},{11,7},{20,24},{24,20... | collective-permute-start | bytes 1843208 | tf_op jit(solution)/shard_map/ppermute | solution.py:502
  736.7 77.3 %collective-permute-start.83 = (bf16[384,1024]{1,0:T(8,128)(2,1)}, bf16[384,1024]{1,0:T(8,128)(2,1)}, u32[]{:S(2)}, u32[]{:S(2)}) collective-permute-start(bf16[384,1024]{1,0:T(8,128)(2,1)} %add_convert_fusion.21), channel_id=1, source_target_pairs={{4,0},{8,12},{5,1},{9,13},{6,2},{10,14},{7,3},{11,15},{20,16},{24,... | collective-permute-start | bytes 2359304 | tf_op jit(solution)/shard_map/ppermute | solution.py:502
  772.1 35.8 %all-to-all-start.10 = ((bf16[4,96,1024]{2,1,0:T(8,128)(2,1)}), bf16[4,96,1024]{2,1,0:T(8,128)(2,1)}, u32[]{:S(2)}, u32[]{:S(2)}) async-start(bf16[4,96,1024]{2,1,0:T(8,128)(2,1)} %bitcast.326), calls=%async_computation.10 | async-start | bytes 1572864 | tf_op jit(solution)/shard_map/all_to_all | solution.py:29
  777.7 37.5 %collective-permute-start.84 = (bf16[1024,768]{1,0:T(8,128)(2,1)}, bf16[1024,768]{1,0:T(8,128)(2,1)}, u32[]{:S(2)}, u32[]{:S(2)}) collective-permute-start(bf16[1024,768]{1,0:T(8,128)(2,1)} %add_convert_fusion.4), channel_id=1, source_target_pairs={{4,8},{8,4},{5,9},{9,5},{6,10},{10,6},{7,11},{11,7},{20,24},{24,20... | collective-permute-start | bytes 4718600 | tf_op jit(solution)/shard_map/ppermute | solution.py:502
  779.5 37.5 %collective-permute-start.85 = (bf16[192,4096]{1,0:T(8,128)(2,1)}, bf16[192,4096]{1,0:T(8,128)(2,1)}, u32[]{:S(2)}, u32[]{:S(2)}) collective-permute-start(bf16[192,4096]{1,0:T(8,128)(2,1)} %get-tuple-element.406), channel_id=1, source_target_pairs={{0,4},{12,8},{1,5},{13,9},{2,6},{14,10},{3,7},{15,11},{16,20},{28,... | collective-permute-start | bytes 4718600 | tf_op jit(solution)/shard_map/ppermute | solution.py:502
  803.6 80.8 %collective-permute-start.79 = (f32[256,768]{1,0:T(8,128)}, f32[256,768]{1,0:T(8,128)}, u32[]{:S(2)}, u32[]{:S(2)}) collective-permute-start(f32[256,768]{1,0:T(8,128)} %get-tuple-element.558), channel_id=1, source_target_pairs={{0,16},{16,0},{1,17},{17,1},{2,18},{18,2},{3,19},{19,3},{4,20},{20... | collective-permute-start | bytes 2359304 | tf_op jit(solution)/shard_map/ppermute | solution.py:25
  815.3 35.1 %collective-permute-start.81 = (bf16[192,4096]{1,0:T(8,128)(2,1)}, bf16[192,4096]{1,0:T(8,128)(2,1)}, u32[]{:S(2)}, u32[]{:S(2)}) collective-permute-start(bf16[192,4096]{1,0:T(8,128)(2,1)} %add_convert_fusion.5), channel_id=1, source_target_pairs={{4,8},{8,4},{5,9},{9,5},{6,10},{10,6},{7,11},{11,7},{20,24},{24,20... | collective-permute-start | bytes 4718600 | tf_op jit(solution)/shard_map/ppermute | solution.py:502
  841.3 36.5 %collective-permute-start.95 = (bf16[1024,768]{1,0:T(8,128)(2,1)}, bf16[1024,768]{1,0:T(8,128)(2,1)S(1)}, u32[]{:S(2)}, u32[]{:S(2)}) collective-permute-start(bf16[1024,768]{1,0:T(8,128)(2,1)} %add_convert_fusion.2), channel_id=1, source_target_pairs={{4,0},{8,12},{5,1},{9,13},{6,2},{10,14},{7,3},{11,15},{20,16},{24,... | collective-permute-start | bytes 4718600 | tf_op jit(solution)/shard_map/ppermute | solution.py:502
  842.6 35.2 %collective-permute-start.96 = (bf16[192,4096]{1,0:T(8,128)(2,1)}, bf16[192,4096]{1,0:T(8,128)(2,1)S(1)}, u32[]{:S(2)}, u32[]{:S(2)}) collective-permute-start(bf16[192,4096]{1,0:T(8,128)(2,1)} %add_convert_fusion.1), channel_id=1, source_target_pairs={{4,8},{8,4},{5,9},{9,5},{6,10},{10,6},{7,11},{11,7},{20,24},{24,20... | collective-permute-start | bytes 4718600 | tf_op jit(solution)/shard_map/ppermute | solution.py:502
  865.4 50.6 %collective-permute-start.92 = (bf16[192,4096]{1,0:T(8,128)(2,1)S(1)}, bf16[192,4096]{1,0:T(8,128)(2,1)S(1)}, u32[]{:S(2)}, u32[]{:S(2)}) collective-permute-start(bf16[192,4096]{1,0:T(8,128)(2,1)S(1)} %add_convert_fusion.3), channel_id=1, source_target_pairs={{4,0},{8,12},{5,1},{9,13},{6,2},{10,14},{7,3},{11,15},{20,16},{24,... | collective-permute-start | bytes 4718600 | tf_op jit(solution)/shard_map/ppermute | solution.py:502
  877.9 38.1 %collective-permute-start.99 = (bf16[1024,768]{1,0:T(8,128)(2,1)S(1)}, bf16[1024,768]{1,0:T(8,128)(2,1)S(1)}, u32[]{:S(2)}, u32[]{:S(2)}) collective-permute-start(bf16[1024,768]{1,0:T(8,128)(2,1)S(1)} %broadcast_select_fusion.10), channel_id=1, source_target_pairs={{16,0},{17,1},{18,2},{19,3},{20,4},{21,5},{22,6},{23,7},{24,8},{25... | collective-permute-start | bytes 4718600 | tf_op jit(solution)/shard_map/ppermute | solution.py:502
  903.0 42.2 %collective-permute-start.100 = (bf16[192,4096]{1,0:T(8,128)(2,1)S(1)}, bf16[192,4096]{1,0:T(8,128)(2,1)S(1)}, u32[]{:S(2)}, u32[]{:S(2)}) collective-permute-start(bf16[192,4096]{1,0:T(8,128)(2,1)S(1)} %add_convert_fusion), channel_id=1, source_target_pairs={{4,0},{8,12},{5,1},{9,13},{6,2},{10,14},{7,3},{11,15},{20,16},{24,... | collective-permute-start | bytes 4718600 | tf_op jit(solution)/shard_map/ppermute | solution.py:502
  920.9 36.0 %collective-permute-start.103 = (bf16[256,768]{1,0:T(8,128)(2,1)S(1)}, bf16[256,768]{1,0:T(8,128)(2,1)S(1)}, u32[]{:S(2)}, u32[]{:S(2)}) collective-permute-start(bf16[256,768]{1,0:T(8,128)(2,1)S(1)} %add_convert_fusion.30), channel_id=1, source_target_pairs={{4,0},{8,12},{5,1},{9,13},{6,2},{10,14},{7,3},{11,15},{20,16},{24,... | collective-permute-start | bytes 1179656 | tf_op jit(solution)/shard_map/ppermute | solution.py:502
  (198 other events, 2529.8 us)
Sparse Core Ops, SparseCore 0:
  129.3 49.0 all-gather.2

commit v2 on v1

--- a/solution.py
+++ b/solution.py
@@ -557,7 +557,7 @@
     return add_blocks(middle, parts), (scale, hidden, blocks, *out[:9])
 
 
-def mlp_backward(grad_blocks, middle, saved, context, weights, sums, ready):
+def mlp_backward(grad_blocks, middle, saved, context, weights, sums, ready, kernel_done):
     gain, w_small, w_sin, w_sdown, expert_weights, which = weights
     me, slot, info, capacity, experts = context
     scale, hidden, blocks, rows, gate, up, act, meta, ret, sg, su, sact = saved
@@ -565,7 +565,7 @@
     out = moe_backward(
         which, slot, info, meta, grad_blocks, ret, expert_weights, gate, up, sg, su, w_sin, w_sdown
     )
-    out = sums.step(out)
+    out = sums.step(kernel_done(out))
     dy, dg, du, dsg, dsu = out[:5]
     parts = scatter_blocks(out[5:])
     ready((rows, act, dy, dg, du), (blocks, sact, grad_blocks, dsg, dsu))
@@ -631,7 +631,10 @@
     small = (keep + swap_cores(send).astype(F32)).astype(BF)
     g_out = halves_by_member(mixed, dattn, core, members)
     g_qkv = halves_by_member(hidden_one, dqkv, core, members)
-    parts = a2a(jnp.concatenate([g_qkv, g_out, small], axis=2), EXP)
+    return jnp.concatenate([g_qkv, g_out, small], axis=2)
+
+
+def member_sum(parts):
     return jnp.sum(parts.astype(F32), axis=0).astype(BF)
 
 
@@ -719,8 +722,15 @@
 
     sums = LineSums()
 
-    def backward(section, grad_blocks, current, hidden, scale, heads, mixed, middle, saved, gain, w_qkv_s, w_out_s, mlp):
+    def backward(section, grad_blocks, current, hidden, scale, heads, mixed, middle, saved, gain, w_qkv_s, w_out_s, mlp, beside=None):
         shared = []
+
+        def kernel_done(out):
+            if beside is None:
+                return out
+            out, parts = lax.optimization_barrier((out, a2a(beside, EXP)))
+            sums.add(1 - section, 4, [member_sum(parts)])
+            return out
 
         def ready(terms, shared_terms):
             down, ein = expert_grads(terms, core)
@@ -728,7 +738,9 @@
             sums.add(section, 1, cut(ein, CHUNKS[1]))
             shared.append(shared_terms)
 
-        dmiddle, dgain_two, dlogits = mlp_backward(grad_blocks, middle, saved, context, mlp, sums, ready)
+        dmiddle, dgain_two, dlogits = mlp_backward(
+            grad_blocks, middle, saved, context, mlp, sums, ready, kernel_done
+        )
         dattn = dmiddle.astype(BF)
         dheads = to_heads(mm(dattn, w_out_s, 1, 1, out=BF), lanes, 1)
         g_sdown, g_sin = shared_grads(shared[0], core)
@@ -739,18 +751,19 @@
         dqkv = sums.step(to_tokens(dheads, lanes, 3))
         dinput, dgain_one = norm_backward(mm(dqkv, w_qkv_s, 1, 1), current, scale, gain)
         dense = (hidden, dqkv, mixed, dattn, saved[1], dlogits, (dgain_one, dgain_two))
-        sums.add(section, 4, [dense_grads(dense, core, members)])
-        return dmiddle + dinput
-
-    grad_1 = backward(
+        return dmiddle + dinput, dense_grads(dense, core, members)
+
+    grad_1, dense_1 = backward(
         1, grad_blocks, current_1, hidden_1, scale_1, heads_1, mixed_1, middle_1, saved_1, gains_1[0], qkv_1,
         w_out_1, mlp_1,
     )
-    grad_blocks = sums.step(gather_blocks(grad_1.astype(BF), members))
-    grad_0 = backward(
+    grad_blocks, dense_1 = lax.optimization_barrier((gather_blocks(grad_1.astype(BF), members), dense_1))
+    grad_blocks = sums.step(grad_blocks)
+    grad_0, dense_0 = backward(
         0, grad_blocks, current_0, hidden_0, scale_0, heads_0, mixed_0, middle_0, saved_0, gains_0[0], qkv_0,
-        w_out_0, mlp_0,
-    )
+        w_out_0, mlp_0, dense_1,
+    )
+    sums.add(0, 4, [member_sum(a2a(dense_0, EXP))])
     quarter = FF // members
 
     def by_columns(half):

time: 1020 us -> 1010 us (level)
    ppermute x48, waiting for transfers between devices: 101 us -> 88.1 us  [launch(): got = lax.ppermute(value, axis, pairs)]
    ppermute x21, waiting for transfers between devices: 48.7 us -> 59.3 us  [gather_blocks(): lax.ppermute(v, EXP, xor_pairs(members, k))]
  transfers between devices with their start and end apart: 124 -> 124, of which waited for: 30 -> 31; matrix products, arithmetic and copies ran while one was open for 28% -> 28% of each run, Pallas kernels for 10% -> 10%
where the time goes in v2:
time: 1010 us; the launch traced here: 1000 us
  waiting for transfers between devices  277 us (27%)
  starting transfers between devices  264 us (26%)
  other arithmetic  158 us (16%)
  Pallas kernels  124 us (12%)
  matrix products  82.1 us (8%)
  local copies, waits for them, and re-layouts  78.8 us (8%)
  between operations  19 us (2%)
    ppermute x48, starting transfers between devices, launch(): got = lax.ppermute(value, axis, pairs)  139 us
    all_to_all x12, waiting for transfers between devices, a2a(): return lax.all_to_all(v, axis, split_axis=0, concat_axis=0, tiled=True)  89.7 us
    ppermute x48, waiting for transfers between devices, launch(): got = lax.ppermute(value, axis, pairs)  88.1 us
    pallas_call x4, Pallas kernels, moe_call(): pl.pallas_call(kernel, out_shape=[jax.ShapeDtypeStruct(*shape) for shape...  86.6 us
    dot_general x40, matrix products, mm(): lax.dot_general(a, b, (((ca,), (cb,)), ((), ())), preferred_element_type=...  82.1 us
    ppermute x21, waiting for transfers between devices, gather_blocks(): lax.ppermute(v, EXP, xor_pairs(members, k))  59.3 us
    convert_element_type x24, other arithmetic, add_low(): return (a.astype(F32) + b.astype(F32)).astype(BF)  52.6 us
    all_to_all x12, starting transfers between devices, a2a(): return lax.all_to_all(v, axis, split_axis=0, concat_axis=0, tiled=True)  50.9 us
  transfers between devices with their start and end apart: 124, of which 31 were waited for; matrix products, arithmetic and copies ran while one was open for 28% of the time, Pallas kernels for 10%

profile of v2, /device:TPU:1, one launch (start us, length us, event | category | flops | bytes accessed | tf_op | source)
XLA Modules:
  0.0 1002.2 jit_solution(13447582860232182428)
XLA Ops:
  17.8 8.8 collective-permute-done.3
  26.6 10.3 %collective-permute-done.2 = bf16[96,2432]{1,0:T(8,128)(2,1)S(1)} collective-permute-done((bf16[96,2432]{1,0:T(8,128)(2,1)S(1)}, bf16[96,2432]{1,0:T(8,128)(2,1)S(1)}, u32[]{:S(2)}, u32[]{:S(2)}) %collective-permute-start.2) | collective-permute-done | bytes 466976 | tf_op jit(solution)/shard_map/ppermute | solution.py:41
  58.4 4.9 all-to-all-start
  79.6 9.3 collective-permute-done.14
  103.6 6.7 shard_map.213
  111.2 4.5 all-to-all-start.1
  143.1 14.5 %collective-permute-done.20.refs_7_ = bf16[256,768]{1,0:T(8,128)(2,1)} collective-permute-done((bf16[256,768]{1,0:T(8,128)(2,1)S(1)}, bf16[256,768]{1,0:T(8,128)(2,1)}, u32[]{:S(2)}, u32[]{:S(2)}) %collective-permute-start.20) | collective-permute-done | bytes 393248 | tf_op jit(solution)/shard_map/ppermute | solution.py:41
  157.6 20.4 %shard_map.214 = (bf16[512,768]{1,0:T(8,128)(2,1)}, bf16[512,2048]{1,0:T(8,128)(2,1)}, bf16[512,2048]{1,0:T(8,128)(2,1)}, bf16[512,2048]{1,0:T(8,128)(2,1)}, f32...) custom-call(s32[2]{0:T(128)} %pad_add_fusion.1.refs_0_, ...), custom_call_target="tpu_custom_call" | custom-call | flops 8858370048 | bytes 31457280 | tf_op jit(solution)/shard_map/pallas_call | solution.py:366
  183.5 9.2 collective-permute-done.25
  192.7 8.6 collective-permute-done.24
  215.1 4.6 all-to-all-start.2
  225.9 22.0 %all-to-all-done.2 = bf16[4,256,576]{1,2,0:T(8,128)(2,1)} async-done(((bf16[4,256,576]{1,2,0:T(8,128)(2,1)}), bf16[4,256,576]{1,2,0:T(8,128)(2,1)}, u32[]{:S(2)}, u32[]{:S(2)}) %all-to-all-start.2) | async-done | bytes 1179680 | tf_op jit(solution)/shard_map/all_to_all | solution.py:29
  249.6 6.6 shard_map.215
  289.1 8.1 collective-permute-done.32.refs_7_
  298.0 20.4 %shard_map.216 = (bf16[512,768]{1,0:T(8,128)(2,1)}, bf16[512,2048]{1,0:T(8,128)(2,1)}, bf16[512,2048]{1,0:T(8,128)(2,1)}, bf16[512,2048]{1,0:T(8,128)(2,1)}, f32...) custom-call(s32[2]{0:T(128)} %pad_add_fusion.2.refs_0_, ...), custom_call_target="tpu_custom_call" | custom-call | flops 8858370048 | bytes 31457280 | tf_op jit(solution)/shard_map/pallas_call | solution.py:366
  321.1 22.7 %shard_map.217 = (bf16[512,768]{1,0:T(8,128)(2,1)}, bf16[512,2048]{1,0:T(8,128)(2,1)}, bf16[512,2048]{1,0:T(8,128)(2,1)}, bf16[1024,512]{1,0:T(8,128)(2,1)}, bf1...) custom-call(s32[2]{0:T(128)} %pad_add_fusion.2.refs_0_, ...), custom_call_target="tpu_custom_call" | custom-call | flops 8858370048 | bytes 31457280 | tf_op jit(solution)/shard_map/pallas_call | solution.py:366
  381.9 9.2 collective-permute-start.36
  391.2 4.5 collective-permute-start.43
  415.1 19.9 %all-to-all-done.4 = bf16[4,256,192]{1,2,0:T(8,128)(2,1)} async-done(((bf16[4,256,192]{1,2,0:T(8,128)(2,1)}), bf16[4,256,192]{1,2,0:T(8,128)(2,1)}, u32[]{:S(2)}, u32[]{:S(2)}) %all-to-all-start.4) | async-done | bytes 393248 | tf_op jit(solution)/shard_map/all_to_all | solution.py:29
  436.2 12.1 %shard_map.218 = bf16[1024,576]{1,0:T(8,128)(2,1)S(1)} custom-call(s32[2]{0:T(128)S(1)} %slice_bitcast_fusion.1.ends_ref, bf16[1024,576]{1,0:T(8,128)(2,1)S(1)} %bitcast.272, bf16[1024,192]{1,0:T(8,128)(2,1)S(1)} %bitcast.277), custom_call_target="tpu_custom_call" | custom-call | flops 2013265920 | bytes 3145728 | tf_op jit(solution)/shard_map/pallas_call | solution.py:169
  451.7 4.5 all-to-all-start.5
  457.6 6.0 collective-permute-start.44
  480.5 5.2 all-to-all-done.5
  491.3 17.2 %collective-permute-done.44 = bf16[192,4096]{1,0:T(8,128)(2,1)} collective-permute-done((bf16[192,4096]{1,0:T(8,128)(2,1)}, bf16[192,4096]{1,0:T(8,128)(2,1)}, u32[]{:S(2)}, u32[]{:S(2)}) %collective-permute-start.44) | collective-permute-done | bytes 1572896 | tf_op jit(solution)/shard_map/ppermute | solution.py:502
  531.0 10.7 %collective-permute-done.47.refs_6_ = bf16[256,768]{1,0:T(8,128)(2,1)S(1)} collective-permute-done((bf16[256,768]{1,0:T(8,128)(2,1)}, bf16[256,768]{1,0:T(8,128)(2,1)S(1)}, u32[]{:S(2)}, u32[]{:S(2)}) %collective-permute-start.47) | collective-permute-done | bytes 393248 | tf_op jit(solution)/shard_map/ppermute | solution.py:41
  546.0 4.5 all-to-all-start.7
  564.9 23.1 %shard_map.219 = (bf16[512,768]{1,0:T(8,128)(2,1)}, bf16[512,2048]{1,0:T(8,128)(2,1)}, bf16[512,2048]{1,0:T(8,128)(2,1)}, bf16[1024,512]{1,0:T(8,128)(2,1)}, bf1...) custom-call(s32[2]{0:T(128)} %pad_add_fusion.1.refs_0_, ...), custom_call_target="tpu_custom_call" | custom-call | flops 8858370048 | bytes 31457280 | tf_op jit(solution)/shard_map/pallas_call | solution.py:366
  588.1 8.6 collective-permute-start.62
  626.0 6.5 collective-permute-start.66
  632.5 6.2 collective-permute-done.58
  668.4 6.4 collective-permute-start.72
  696.4 11.9 %shard_map.220 = bf16[1024,576]{1,0:T(8,128)(2,1)S(1)} custom-call(s32[2]{0:T(128)S(1)} %slice_bitcast_fusion.1.ends_ref, bf16[1024,576]{1,0:T(8,128)(2,1)S(1)} %bitcast.270, bf16[1024,192]{1,0:T(8,128)(2,1)S(1)} %bitcast.275), custom_call_target="tpu_custom_call" | custom-call | flops 2013265920 | bytes 3145728 | tf_op jit(solution)/shard_map/pallas_call | solution.py:169
  708.2 5.9 collective-permute-start.76
  732.3 31.1 %all-to-all-done.9 = bf16[4,256,576]{1,2,0:T(8,128)(2,1)S(1)} async-done(((bf16[4,256,576]{1,2,0:T(8,128)(2,1)}), bf16[4,256,576]{1,2,0:T(8,128)(2,1)S(1)}, u32[]{:S(2)}, u32[]{:S(2)}) %all-to-all-start.9) | async-done | bytes 1179680 | tf_op jit(solution)/shard_map/all_to_all | solution.py:29
  770.9 6.4 collective-permute-start.85
  808.4 7.0 collective-permute-start.82
  825.8 5.3 all-to-all-done.11
  834.6 6.6 collective-permute-start.97
  846.2 10.0 collective-permute-done.97
  857.5 11.5 %collective-permute-done.95 = bf16[1024,768]{1,0:T(8,128)(2,1)S(1)} collective-permute-done((bf16[1024,768]{1,0:T(8,128)(2,1)}, bf16[1024,768]{1,0:T(8,128)(2,1)S(1)}, u32[]{:S(2)}, u32[]{:S(2)}) %collective-permute-start.95) | collective-permute-done | bytes 1572896 | tf_op jit(solution)/shard_map/ppermute | solution.py:502
  869.2 6.5 collective-permute-start.99
  880.2 13.1 %collective-permute-start.94 = (bf16[96,3200]{1,0:T(8,128)(2,1)S(1)}, bf16[96,3200]{1,0:T(8,128)(2,1)S(1)}, u32[]{:S(2)}, u32[]{:S(2)}) collective-permute-start(bf16[96,3200]{1,0:T(8,128)(2,1)S(1)} %copy-done.44), channel_id=1, source_target_pairs={{0,4},{12,8},{1,5},{13,9},{2,6},{14,10},{3,7},{15,11},{16,20},{28,... | collective-permute-start | bytes 1843208 | tf_op jit(solution)/shard_map/ppermute | solution.py:502
  895.2 11.7 %collective-permute-done.94 = bf16[96,3200]{1,0:T(8,128)(2,1)S(1)} collective-permute-done((bf16[96,3200]{1,0:T(8,128)(2,1)S(1)}, bf16[96,3200]{1,0:T(8,128)(2,1)S(1)}, u32[]{:S(2)}, u32[]{:S(2)}) %collective-permute-start.94) | collective-permute-done | bytes 614432 | tf_op jit(solution)/shard_map/ppermute | solution.py:502
  919.8 16.6 %collective-permute-done.100 = bf16[192,4096]{1,0:T(8,128)(2,1)S(1)} collective-permute-done((bf16[192,4096]{1,0:T(8,128)(2,1)S(1)}, bf16[192,4096]{1,0:T(8,128)(2,1)S(1)}, u32[]{:S(2)}, u32[]{:S(2)}) %collective-permute-start.100) | collective-permute-done | bytes 1572896 | tf_op jit(solution)/shard_map/ppermute | solution.py:502
  936.6 6.5 collective-permute-start.105
  951.5 5.3 maximum_convert_fusion
  956.8 8.4 collective-permute-done.106
  972.4 12.6 %collective-permute-done.108 = bf16[96,3200]{1,0:T(8,128)(2,1)S(1)} collective-permute-done((bf16[96,3200]{1,0:T(8,128)(2,1)S(1)}, bf16[96,3200]{1,0:T(8,128)(2,1)S(1)}, u32[]{:S(2)}, u32[]{:S(2)}) %collective-permute-start.108) | collective-permute-done | bytes 614432 | tf_op jit(solution)/shard_map/ppermute | solution.py:502
  (769 shorter events, 480.6 us)
Async XLA Ops:
  17.7 139.8 %collective-permute-start.21 = (bf16[768,4096]{1,0:T(8,128)(2,1)}, bf16[768,4096]{1,0:T(8,128)(2,1)}, u32[]{:S(2)}, u32[]{:S(2)}) collective-permute-start(bf16[768,4096]{1,0:T(8,128)(2,1)} %bitcast.279), channel_id=1, source_target_pairs={{0,16},{16,0},{1,17},{17,1},{2,18},{18,2},{3,19},{19,3},{4,20},{20... | collective-permute-start | bytes 18874376 | tf_op jit(solution)/shard_map/ppermute | solution.py:25
  58.4 43.5 %all-to-all-start = ((bf16[4,256,576]{1,2,0:T(8,128)(2,1)}), bf16[4,256,576]{1,2,0:T(8,128)(2,1)}, u32[]{:S(2)}, u32[]{:S(2)}) async-start(bf16[4,256,576]{1,2,0:T(8,128)(2,1)} %bitcast.17), calls=%async_computation | async-start | bytes 2359296 | tf_op jit(solution)/shard_map/all_to_all | solution.py:29
  94.4 43.3 %collective-permute-start.22 = (bf16[2048,768]{1,0:T(8,128)(2,1)}, bf16[2048,768]{1,0:T(8,128)(2,1)}, u32[]{:S(2)}, u32[]{:S(2)}) collective-permute-start(bf16[2048,768]{1,0:T(8,128)(2,1)} %bitcast.52.refs_10_.refs_11_), channel_id=1, source_target_pairs={{0,16},{16,0},{1,17},{17,1},{2,18},{18,2},{3,19},{19,3},{4,20},{20... | collective-permute-start | bytes 9437192 | tf_op jit(solution)/shard_map/ppermute | solution.py:25
  115.8 62.5 %all-gather.3.cloned.1.call-start = ((), (), s32[]{:S(2)}) async-start(), calls=%async_computation.12 | async-start | bytes 3072000 | tf_op jit(solution)/shard_map/all_gather | solution.py:701
  215.1 32.7 %all-to-all-start.2 = ((bf16[4,256,576]{1,2,0:T(8,128)(2,1)}), bf16[4,256,576]{1,2,0:T(8,128)(2,1)}, u32[]{:S(2)}, u32[]{:S(2)}) async-start(bf16[4,256,576]{1,2,0:T(8,128)(2,1)} %bitcast.61), calls=%async_computation.2 | async-start | bytes 2359296 | tf_op jit(solution)/shard_map/all_to_all | solution.py:29
  318.4 50.3 %collective-permute-start.35 = (bf16[256,768]{1,0:T(8,128)(2,1)}, bf16[256,768]{1,0:T(8,128)(2,1)}, u32[]{:S(2)}, u32[]{:S(2)}) collective-permute-start(bf16[256,768]{1,0:T(8,128)(2,1)} %get-tuple-element.298), channel_id=1, source_target_pairs={{0,3},{1,2},{2,1},{3,0},{4,7},{5,6},{6,5},{7,4},{8,11},{9,10},{10,... | collective-permute-start | bytes 1179656 | tf_op jit(solution)/shard_map/ppermute | solution.py:46
  319.7 50.4 %collective-permute-start.34 = (bf16[256,768]{1,0:T(8,128)(2,1)}, bf16[256,768]{1,0:T(8,128)(2,1)}, u32[]{:S(2)}, u32[]{:S(2)}) collective-permute-start(bf16[256,768]{1,0:T(8,128)(2,1)} %get-tuple-element.297), channel_id=1, source_target_pairs={{0,2},{1,3},{2,0},{3,1},{4,6},{5,7},{6,4},{7,5},{8,10},{9,11},{10,... | collective-permute-start | bytes 1179656 | tf_op jit(solution)/shard_map/ppermute | solution.py:46
  321.0 49.2 %collective-permute-start.33 = (bf16[256,768]{1,0:T(8,128)(2,1)}, bf16[256,768]{1,0:T(8,128)(2,1)}, u32[]{:S(2)}, u32[]{:S(2)}) collective-permute-start(bf16[256,768]{1,0:T(8,128)(2,1)} %get-tuple-element.296), channel_id=1, source_target_pairs={{0,1},{1,0},{2,3},{3,2},{4,5},{5,4},{6,7},{7,6},{8,9},{9,8},{10,11... | collective-permute-start | bytes 1179656 | tf_op jit(solution)/shard_map/ppermute | solution.py:46
  374.0 33.3 %collective-permute-start.42 = (bf16[384,2048]{1,0:T(8,128)(2,1)}, bf16[384,2048]{1,0:T(8,128)(2,1)}, u32[]{:S(2)}, u32[]{:S(2)}) collective-permute-start(bf16[384,2048]{1,0:T(8,128)(2,1)} %convolution_convert_fusion.6), channel_id=1, source_target_pairs={{0,16},{16,0},{1,17},{17,1},{2,18},{18,2},{3,19},{19,3},{4,20},{20... | collective-permute-start | bytes 4718600 | tf_op jit(solution)/shard_map/ppermute | solution.py:25
  377.7 32.8 %collective-permute-start.41 = (bf16[384,2048]{1,0:T(8,128)(2,1)}, bf16[384,2048]{1,0:T(8,128)(2,1)}, u32[]{:S(2)}, u32[]{:S(2)}) collective-permute-start(bf16[384,2048]{1,0:T(8,128)(2,1)} %convolution_convert_fusion.7), channel_id=1, source_target_pairs={{0,16},{16,0},{1,17},{17,1},{2,18},{18,2},{3,19},{19,3},{4,20},{20... | collective-permute-start | bytes 4718600 | tf_op jit(solution)/shard_map/ppermute | solution.py:25
  381.7 84.9 %collective-permute-start.54 = (bf16[384,1024]{1,0:T(8,128)(2,1)}, bf16[384,1024]{1,0:T(8,128)(2,1)}, u32[]{:S(2)}, u32[]{:S(2)}) collective-permute-start(bf16[384,1024]{1,0:T(8,128)(2,1)} %convolution_convert_fusion.11), channel_id=1, source_target_pairs={{0,16},{16,0},{1,17},{17,1},{2,18},{18,2},{3,19},{19,3},{4,20},{20... | collective-permute-start | bytes 2359304 | tf_op jit(solution)/shard_map/ppermute | solution.py:25
  381.9 74.3 %collective-permute-start.36 = (bf16[256,768]{1,0:T(8,128)(2,1)}, bf16[256,768]{1,0:T(8,128)(2,1)}, u32[]{:S(2)}, u32[]{:S(2)}) collective-permute-start(bf16[256,768]{1,0:T(8,128)(2,1)} %get-tuple-element.596), channel_id=1, source_target_pairs={{0,16},{16,0},{1,17},{17,1},{2,18},{18,2},{3,19},{19,3},{4,20},{20... | collective-permute-start | bytes 1179656 | tf_op jit(solution)/shard_map/ppermute | solution.py:25
  391.2 58.1 %collective-permute-start.43 = (bf16[1024,768]{1,0:T(8,128)(2,1)}, bf16[1024,768]{1,0:T(8,128)(2,1)}, u32[]{:S(2)}, u32[]{:S(2)}) collective-permute-start(bf16[1024,768]{1,0:T(8,128)(2,1)} %add_convert_fusion.17), channel_id=1, source_target_pairs={{0,4},{12,8},{1,5},{13,9},{2,6},{14,10},{3,7},{15,11},{16,20},{28,... | collective-permute-start | bytes 4718600 | tf_op jit(solution)/shard_map/ppermute | solution.py:502
  402.9 32.1 %all-to-all-start.4 = ((bf16[4,256,192]{1,2,0:T(8,128)(2,1)}), bf16[4,256,192]{1,2,0:T(8,128)(2,1)}, u32[]{:S(2)}, u32[]{:S(2)}) async-start(bf16[4,256,192]{1,2,0:T(8,128)(2,1)} %bitcast.79), calls=%async_computation.4 | async-start | bytes 786432 | tf_op jit(solution)/shard_map/all_to_all | solution.py:29
  451.7 34.0 %all-to-all-start.5 = ((bf16[4,256,576]{1,2,0:T(8,128)(2,1)}), bf16[4,256,576]{1,2,0:T(8,128)(2,1)}, u32[]{:S(2)}, u32[]{:S(2)}) async-start(bf16[4,256,576]{1,2,0:T(8,128)(2,1)} %copy.290), calls=%async_computation.5 | async-start | bytes 2359296 | tf_op jit(solution)/shard_map/all_to_all | solution.py:29
  457.6 50.9 %collective-permute-start.44 = (bf16[192,4096]{1,0:T(8,128)(2,1)}, bf16[192,4096]{1,0:T(8,128)(2,1)}, u32[]{:S(2)}, u32[]{:S(2)}) collective-permute-start(bf16[192,4096]{1,0:T(8,128)(2,1)} %get-tuple-element.366), channel_id=1, source_target_pairs={{0,4},{12,8},{1,5},{13,9},{2,6},{14,10},{3,7},{15,11},{16,20},{28,... | collective-permute-start | bytes 4718600 | tf_op jit(solution)/shard_map/ppermute | solution.py:502
  476.3 69.7 %collective-permute-start.52 = (bf16[1024,768]{1,0:T(8,128)(2,1)}, bf16[1024,768]{1,0:T(8,128)(2,1)}, u32[]{:S(2)}, u32[]{:S(2)}) collective-permute-start(bf16[1024,768]{1,0:T(8,128)(2,1)} %add_convert_fusion.14), channel_id=1, source_target_pairs={{4,8},{8,4},{5,9},{9,5},{6,10},{10,6},{7,11},{11,7},{20,24},{24,20... | collective-permute-start | bytes 4718600 | tf_op jit(solution)/shard_map/ppermute | solution.py:502
  478.1 67.9 %collective-permute-start.53 = (bf16[192,4096]{1,0:T(8,128)(2,1)}, bf16[192,4096]{1,0:T(8,128)(2,1)}, u32[]{:S(2)}, u32[]{:S(2)}) collective-permute-start(bf16[192,4096]{1,0:T(8,128)(2,1)} %get-tuple-element.376), channel_id=1, source_target_pairs={{0,4},{12,8},{1,5},{13,9},{2,6},{14,10},{3,7},{15,11},{16,20},{28,... | collective-permute-start | bytes 4718600 | tf_op jit(solution)/shard_map/ppermute | solution.py:502
  485.7 60.3 %all-to-all-start.6 = ((bf16[4,96,1024]{2,1,0:T(8,128)(2,1)}), bf16[4,96,1024]{2,1,0:T(8,128)(2,1)}, u32[]{:S(2)}, u32[]{:S(2)}) async-start(bf16[4,96,1024]{2,1,0:T(8,128)(2,1)} %bitcast.327), calls=%async_computation.6 | async-start | bytes 1572864 | tf_op jit(solution)/shard_map/all_to_all | solution.py:29
  529.2 72.0 %collective-permute-start.55 = (bf16[192,4096]{1,0:T(8,128)(2,1)}, bf16[192,4096]{1,0:T(8,128)(2,1)}, u32[]{:S(2)}, u32[]{:S(2)}) collective-permute-start(bf16[192,4096]{1,0:T(8,128)(2,1)} %add_convert_fusion.13), channel_id=1, source_target_pairs={{4,8},{8,4},{5,9},{9,5},{6,10},{10,6},{7,11},{11,7},{20,24},{24,20... | collective-permute-start | bytes 4718600 | tf_op jit(solution)/shard_map/ppermute | solution.py:502
  541.8 59.4 %collective-permute-start.56 = (bf16[256,768]{1,0:T(8,128)(2,1)S(1)}, bf16[256,768]{1,0:T(8,128)(2,1)S(1)}, u32[]{:S(2)}, u32[]{:S(2)}) collective-permute-start(bf16[256,768]{1,0:T(8,128)(2,1)S(1)} %copy-done.59), channel_id=1, source_target_pairs={{0,4},{12,8},{1,5},{13,9},{2,6},{14,10},{3,7},{15,11},{16,20},{28,... | collective-permute-start | bytes 1179656 | tf_op jit(solution)/shard_map/ppermute | solution.py:502
  546.0 52.1 %all-to-all-start.7 = ((bf16[4,96,3200]{2,1,0:T(8,128)(2,1)}), bf16[4,96,3200]{2,1,0:T(8,128)(2,1)}, u32[]{:S(2)}, u32[]{:S(2)}) async-start(bf16[4,96,3200]{2,1,0:T(8,128)(2,1)} %pad_maximum_fusion.2), calls=%async_computation.7 | async-start | bytes 4915200 | tf_op jit(solution)/shard_map/all_to_all | solution.py:29
  554.0 69.3 %collective-permute-start.60 = (bf16[1024,768]{1,0:T(8,128)(2,1)}, bf16[1024,768]{1,0:T(8,128)(2,1)}, u32[]{:S(2)}, u32[]{:S(2)}) collective-permute-start(bf16[1024,768]{1,0:T(8,128)(2,1)} %add_convert_fusion.12), channel_id=1, source_target_pairs={{4,0},{8,12},{5,1},{9,13},{6,2},{10,14},{7,3},{11,15},{20,16},{24,... | collective-permute-start | bytes 4718600 | tf_op jit(solution)/shard_map/ppermute | solution.py:502
  558.8 65.7 %collective-permute-start.61 = (bf16[192,4096]{1,0:T(8,128)(2,1)}, bf16[192,4096]{1,0:T(8,128)(2,1)}, u32[]{:S(2)}, u32[]{:S(2)}) collective-permute-start(bf16[192,4096]{1,0:T(8,128)(2,1)} %add_convert_fusion.11), channel_id=1, source_target_pairs={{4,8},{8,4},{5,9},{9,5},{6,10},{10,6},{7,11},{11,7},{20,24},{24,20... | collective-permute-start | bytes 4718600 | tf_op jit(solution)/shard_map/ppermute | solution.py:502
  623.2 51.5 %collective-permute-start.64 = (bf16[192,4096]{1,0:T(8,128)(2,1)}, bf16[192,4096]{1,0:T(8,128)(2,1)}, u32[]{:S(2)}, u32[]{:S(2)}) collective-permute-start(bf16[192,4096]{1,0:T(8,128)(2,1)} %add_convert_fusion.9), channel_id=1, source_target_pairs={{4,0},{8,12},{5,1},{9,13},{6,2},{10,14},{7,3},{11,15},{20,16},{24,... | collective-permute-start | bytes 4718600 | tf_op jit(solution)/shard_map/ppermute | solution.py:502
  624.5 42.6 %collective-permute-start.65 = (bf16[256,768]{1,0:T(8,128)(2,1)}, bf16[256,768]{1,0:T(8,128)(2,1)}, u32[]{:S(2)}, u32[]{:S(2)}) collective-permute-start(bf16[256,768]{1,0:T(8,128)(2,1)} %add_convert_fusion.33), channel_id=1, source_target_pairs={{4,8},{8,4},{5,9},{9,5},{6,10},{10,6},{7,11},{11,7},{20,24},{24,20... | collective-permute-start | bytes 1179656 | tf_op jit(solution)/shard_map/ppermute | solution.py:502
  626.0 42.4 %collective-permute-start.66 = (bf16[96,3200]{1,0:T(8,128)(2,1)}, bf16[96,3200]{1,0:T(8,128)(2,1)}, u32[]{:S(2)}, u32[]{:S(2)}) collective-permute-start(bf16[96,3200]{1,0:T(8,128)(2,1)} %reduce_sum.240), channel_id=1, source_target_pairs={{0,4},{12,8},{1,5},{13,9},{2,6},{14,10},{3,7},{15,11},{16,20},{28,... | collective-permute-start | bytes 1843208 | tf_op jit(solution)/shard_map/ppermute | solution.py:502
  667.1 47.0 %collective-permute-start.70 = (bf16[192,4096]{1,0:T(8,128)(2,1)}, bf16[192,4096]{1,0:T(8,128)(2,1)}, u32[]{:S(2)}, u32[]{:S(2)}) collective-permute-start(bf16[192,4096]{1,0:T(8,128)(2,1)} %add_convert_fusion.6), channel_id=1, source_target_pairs={{4,0},{8,12},{5,1},{9,13},{6,2},{10,14},{7,3},{11,15},{20,16},{24,... | collective-permute-start | bytes 4718600 | tf_op jit(solution)/shard_map/ppermute | solution.py:502
  668.4 45.7 %collective-permute-start.72 = (bf16[1024,768]{1,0:T(8,128)(2,1)}, bf16[1024,768]{1,0:T(8,128)(2,1)}, u32[]{:S(2)}, u32[]{:S(2)}) collective-permute-start(bf16[1024,768]{1,0:T(8,128)(2,1)} %add_convert_fusion.10), channel_id=1, source_target_pairs={{0,4},{12,8},{1,5},{13,9},{2,6},{14,10},{3,7},{15,11},{16,20},{28,... | collective-permute-start | bytes 4718600 | tf_op jit(solution)/shard_map/ppermute | solution.py:502
  679.8 34.3 %collective-permute-start.73 = (bf16[192,4096]{1,0:T(8,128)(2,1)}, bf16[192,4096]{1,0:T(8,128)(2,1)}, u32[]{:S(2)}, u32[]{:S(2)}) collective-permute-start(bf16[192,4096]{1,0:T(8,128)(2,1)} %broadcast_select_fusion.9), channel_id=1, source_target_pairs={{0,16},{1,17},{2,18},{3,19},{4,20},{5,21},{6,22},{7,23},{8,24},{9,... | collective-permute-start | bytes 4718600 | tf_op jit(solution)/shard_map/ppermute | solution.py:502
  694.7 74.4 %collective-permute-start.74 = (bf16[256,768]{1,0:T(8,128)(2,1)}, bf16[256,768]{1,0:T(8,128)(2,1)}, u32[]{:S(2)}, u32[]{:S(2)}) collective-permute-start(bf16[256,768]{1,0:T(8,128)(2,1)} %add_convert_fusion.32), channel_id=1, source_target_pairs={{4,0},{8,12},{5,1},{9,13},{6,2},{10,14},{7,3},{11,15},{20,16},{24,... | collective-permute-start | bytes 1179656 | tf_op jit(solution)/shard_map/ppermute | solution.py:502
  708.2 69.1 %collective-permute-start.76 = (bf16[192,4096]{1,0:T(8,128)(2,1)}, bf16[192,4096]{1,0:T(8,128)(2,1)}, u32[]{:S(2)}, u32[]{:S(2)}) collective-permute-start(bf16[192,4096]{1,0:T(8,128)(2,1)} %get-tuple-element.415), channel_id=1, source_target_pairs={{0,4},{12,8},{1,5},{13,9},{2,6},{14,10},{3,7},{15,11},{16,20},{28,... | collective-permute-start | bytes 4718600 | tf_op jit(solution)/shard_map/ppermute | solution.py:502
  715.6 47.8 %all-to-all-start.9 = ((bf16[4,256,576]{1,2,0:T(8,128)(2,1)}), bf16[4,256,576]{1,2,0:T(8,128)(2,1)S(1)}, u32[]{:S(2)}, u32[]{:S(2)}) async-start(bf16[4,256,576]{1,2,0:T(8,128)(2,1)} %copy.300), calls=%async_computation.9 | async-start | bytes 2359296 | tf_op jit(solution)/shard_map/all_to_all | solution.py:29
  720.7 56.6 %collective-permute-start.77 = (bf16[192,4096]{1,0:T(8,128)(2,1)S(1)}, bf16[192,4096]{1,0:T(8,128)(2,1)}, u32[]{:S(2)}, u32[]{:S(2)}) collective-permute-start(bf16[192,4096]{1,0:T(8,128)(2,1)S(1)} %broadcast_select_fusion.8), channel_id=1, source_target_pairs={{0,16},{1,17},{2,18},{3,19},{4,20},{5,21},{6,22},{7,23},{8,24},{9,... | collective-permute-start | bytes 4718600 | tf_op jit(solution)/shard_map/ppermute | solution.py:502
  723.4 47.4 %collective-permute-start.75 = (bf16[96,3200]{1,0:T(8,128)(2,1)S(1)}, bf16[96,3200]{1,0:T(8,128)(2,1)}, u32[]{:S(2)}, u32[]{:S(2)}) collective-permute-start(bf16[96,3200]{1,0:T(8,128)(2,1)S(1)} %add_convert_fusion.27), channel_id=1, source_target_pairs={{4,8},{8,4},{5,9},{9,5},{6,10},{10,6},{7,11},{11,7},{20,24},{24,20... | collective-permute-start | bytes 1843208 | tf_op jit(solution)/shard_map/ppermute | solution.py:502
  727.8 77.4 %collective-permute-start.83 = (bf16[384,1024]{1,0:T(8,128)(2,1)}, bf16[384,1024]{1,0:T(8,128)(2,1)}, u32[]{:S(2)}, u32[]{:S(2)}) collective-permute-start(bf16[384,1024]{1,0:T(8,128)(2,1)} %add_convert_fusion.21), channel_id=1, source_target_pairs={{4,0},{8,12},{5,1},{9,13},{6,2},{10,14},{7,3},{11,15},{20,16},{24,... | collective-permute-start | bytes 2359304 | tf_op jit(solution)/shard_map/ppermute | solution.py:502
  763.4 35.7 %all-to-all-start.10 = ((bf16[4,96,1024]{2,1,0:T(8,128)(2,1)}), bf16[4,96,1024]{2,1,0:T(8,128)(2,1)}, u32[]{:S(2)}, u32[]{:S(2)}) async-start(bf16[4,96,1024]{2,1,0:T(8,128)(2,1)} %bitcast.326), calls=%async_computation.10 | async-start | bytes 1572864 | tf_op jit(solution)/shard_map/all_to_all | solution.py:29
  769.0 37.5 %collective-permute-start.84 = (bf16[1024,768]{1,0:T(8,128)(2,1)}, bf16[1024,768]{1,0:T(8,128)(2,1)}, u32[]{:S(2)}, u32[]{:S(2)}) collective-permute-start(bf16[1024,768]{1,0:T(8,128)(2,1)} %add_convert_fusion.4), channel_id=1, source_target_pairs={{4,8},{8,4},{5,9},{9,5},{6,10},{10,6},{7,11},{11,7},{20,24},{24,20... | collective-permute-start | bytes 4718600 | tf_op jit(solution)/shard_map/ppermute | solution.py:502
  770.9 37.5 %collective-permute-start.85 = (bf16[192,4096]{1,0:T(8,128)(2,1)}, bf16[192,4096]{1,0:T(8,128)(2,1)}, u32[]{:S(2)}, u32[]{:S(2)}) collective-permute-start(bf16[192,4096]{1,0:T(8,128)(2,1)} %get-tuple-element.436), channel_id=1, source_target_pairs={{0,4},{12,8},{1,5},{13,9},{2,6},{14,10},{3,7},{15,11},{16,20},{28,... | collective-permute-start | bytes 4718600 | tf_op jit(solution)/shard_map/ppermute | solution.py:502
  794.9 80.8 %collective-permute-start.79 = (f32[256,768]{1,0:T(8,128)}, f32[256,768]{1,0:T(8,128)}, u32[]{:S(2)}, u32[]{:S(2)}) collective-permute-start(f32[256,768]{1,0:T(8,128)} %get-tuple-element.588), channel_id=1, source_target_pairs={{0,16},{16,0},{1,17},{17,1},{2,18},{18,2},{3,19},{19,3},{4,20},{20... | collective-permute-start | bytes 2359304 | tf_op jit(solution)/shard_map/ppermute | solution.py:25
  799.1 32.0 %all-to-all-start.11 = ((bf16[4,96,3200]{2,1,0:T(8,128)(2,1)}), bf16[4,96,3200]{2,1,0:T(8,128)(2,1)S(1)}, u32[]{:S(2)}, u32[]{:S(2)}) async-start(bf16[4,96,3200]{2,1,0:T(8,128)(2,1)} %pad_maximum_fusion.3), calls=%async_computation.11 | async-start | bytes 4915200 | tf_op jit(solution)/shard_map/all_to_all | solution.py:29
  806.5 34.7 %collective-permute-start.81 = (bf16[192,4096]{1,0:T(8,128)(2,1)}, bf16[192,4096]{1,0:T(8,128)(2,1)}, u32[]{:S(2)}, u32[]{:S(2)}) collective-permute-start(bf16[192,4096]{1,0:T(8,128)(2,1)} %add_convert_fusion.5), channel_id=1, source_target_pairs={{4,8},{8,4},{5,9},{9,5},{6,10},{10,6},{7,11},{11,7},{20,24},{24,20... | collective-permute-start | bytes 4718600 | tf_op jit(solution)/shard_map/ppermute | solution.py:502
  832.5 36.5 %collective-permute-start.95 = (bf16[1024,768]{1,0:T(8,128)(2,1)}, bf16[1024,768]{1,0:T(8,128)(2,1)S(1)}, u32[]{:S(2)}, u32[]{:S(2)}) collective-permute-start(bf16[1024,768]{1,0:T(8,128)(2,1)} %add_convert_fusion.2), channel_id=1, source_target_pairs={{4,0},{8,12},{5,1},{9,13},{6,2},{10,14},{7,3},{11,15},{20,16},{24,... | collective-permute-start | bytes 4718600 | tf_op jit(solution)/shard_map/ppermute | solution.py:502
  833.8 35.2 %collective-permute-start.96 = (bf16[192,4096]{1,0:T(8,128)(2,1)}, bf16[192,4096]{1,0:T(8,128)(2,1)S(1)}, u32[]{:S(2)}, u32[]{:S(2)}) collective-permute-start(bf16[192,4096]{1,0:T(8,128)(2,1)} %add_convert_fusion.1), channel_id=1, source_target_pairs={{4,8},{8,4},{5,9},{9,5},{6,10},{10,6},{7,11},{11,7},{20,24},{24,20... | collective-permute-start | bytes 4718600 | tf_op jit(solution)/shard_map/ppermute | solution.py:502
  856.2 50.7 %collective-permute-start.92 = (bf16[192,4096]{1,0:T(8,128)(2,1)S(1)}, bf16[192,4096]{1,0:T(8,128)(2,1)S(1)}, u32[]{:S(2)}, u32[]{:S(2)}) collective-permute-start(bf16[192,4096]{1,0:T(8,128)(2,1)S(1)} %add_convert_fusion.3), channel_id=1, source_target_pairs={{4,0},{8,12},{5,1},{9,13},{6,2},{10,14},{7,3},{11,15},{20,16},{24,... | collective-permute-start | bytes 4718600 | tf_op jit(solution)/shard_map/ppermute | solution.py:502
  869.2 37.8 %collective-permute-start.99 = (bf16[1024,768]{1,0:T(8,128)(2,1)S(1)}, bf16[1024,768]{1,0:T(8,128)(2,1)S(1)}, u32[]{:S(2)}, u32[]{:S(2)}) collective-permute-start(bf16[1024,768]{1,0:T(8,128)(2,1)S(1)} %broadcast_select_fusion.10), channel_id=1, source_target_pairs={{16,0},{17,1},{18,2},{19,3},{20,4},{21,5},{22,6},{23,7},{24,8},{25... | collective-permute-start | bytes 4718600 | tf_op jit(solution)/shard_map/ppermute | solution.py:502
  893.9 42.5 %collective-permute-start.100 = (bf16[192,4096]{1,0:T(8,128)(2,1)S(1)}, bf16[192,4096]{1,0:T(8,128)(2,1)S(1)}, u32[]{:S(2)}, u32[]{:S(2)}) collective-permute-start(bf16[192,4096]{1,0:T(8,128)(2,1)S(1)} %add_convert_fusion), channel_id=1, source_target_pairs={{4,0},{8,12},{5,1},{9,13},{6,2},{10,14},{7,3},{11,15},{20,16},{24,... | collective-permute-start | bytes 4718600 | tf_op jit(solution)/shard_map/ppermute | solution.py:502
  911.8 36.3 %collective-permute-start.103 = (bf16[256,768]{1,0:T(8,128)(2,1)S(1)}, bf16[256,768]{1,0:T(8,128)(2,1)S(1)}, u32[]{:S(2)}, u32[]{:S(2)}) collective-permute-start(bf16[256,768]{1,0:T(8,128)(2,1)S(1)} %add_convert_fusion.30), channel_id=1, source_target_pairs={{4,0},{8,12},{5,1},{9,13},{6,2},{10,14},{7,3},{11,15},{20,16},{24,... | collective-permute-start | bytes 1179656 | tf_op jit(solution)/shard_map/ppermute | solution.py:502
  (201 other events, 2487.4 us)
Sparse Core Ops, SparseCore 0:
  129.2 49.0 all-gather.2

commit v3 on v2

--- a/solution.py
+++ b/solution.py
@@ -698,7 +698,7 @@
     gathered = []
 
     def land(out):
-        out, full = lax.optimization_barrier((out, lax.all_gather(after(later, middle_0), EXP)))
+        out, full = lax.optimization_barrier((out, lax.all_gather(after(later, heads_0), EXP)))
         gathered.append(full)
         return out
 

time: 1010 us -> 1000 us (0.990)
    unnamed x279 -> x281, local copies, waits for them, and re-layouts: 19 us -> 21.7 us
  transfers between devices with their start and end apart: 124 -> 124, of which waited for: 31 -> 28; matrix products, arithmetic and copies ran while one was open for 28% -> 29% of each run, Pallas kernels for 10% -> 10%
where the time goes in v3:
time: 1000 us; the launch traced here: 995 us
  waiting for transfers between devices  268 us (27%)
  starting transfers between devices  262 us (26%)
  other arithmetic  154 us (15%)
  Pallas kernels  124 us (12%)
  local copies, waits for them, and re-layouts  87.6 us (9%)
  matrix products  80 us (8%)
  between operations  19 us (2%)
    ppermute x48, starting transfers between devices, launch(): got = lax.ppermute(value, axis, pairs)  137 us
    ppermute x48, waiting for transfers between devices, launch(): got = lax.ppermute(value, axis, pairs)  86.8 us
    pallas_call x4, Pallas kernels, moe_call(): pl.pallas_call(kernel, out_shape=[jax.ShapeDtypeStruct(*shape) for shape...  86.6 us
    all_to_all x12, waiting for transfers between devices, a2a(): return lax.all_to_all(v, axis, split_axis=0, concat_axis=0, tiled=True)  85.4 us
    dot_general x40, matrix products, mm(): lax.dot_general(a, b, (((ca,), (cb,)), ((), ())), preferred_element_type=...  80 us
    ppermute x21, waiting for transfers between devices, gather_blocks(): lax.ppermute(v, EXP, xor_pairs(members, k))  62.6 us
    all_to_all x12, starting transfers between devices, a2a(): return lax.all_to_all(v, axis, split_axis=0, concat_axis=0, tiled=True)  54 us
    convert_element_type x24, other arithmetic, add_low(): return (a.astype(F32) + b.astype(F32)).astype(BF)  52.8 us
  transfers between devices with their start and end apart: 124, of which 28 were waited for; matrix products, arithmetic and copies ran while one was open for 29% of the time, Pallas kernels for 10%

profile of v3, /device:TPU:1, one launch (start us, length us, event | category | flops | bytes accessed | tf_op | source)
XLA Modules:
  0.0 994.7 jit_solution(5566233818324578855)
XLA Ops:
  17.7 8.9 collective-permute-done.3
  26.6 10.3 %collective-permute-done.2 = bf16[96,2432]{1,0:T(8,128)(2,1)S(1)} collective-permute-done((bf16[96,2432]{1,0:T(8,128)(2,1)S(1)}, bf16[96,2432]{1,0:T(8,128)(2,1)S(1)}, u32[]{:S(2)}, u32[]{:S(2)}) %collective-permute-start.2) | collective-permute-done | bytes 466976 | tf_op jit(solution)/shard_map/ppermute | solution.py:41
  54.4 4.7 all-to-all-start
  100.0 6.7 shard_map.213
  107.7 4.7 all-to-all-start.1
  118.8 4.8 all-to-all-done.1
  131.5 11.4 %collective-permute-done.18.refs_5_ = bf16[256,768]{1,0:T(8,128)(2,1)} collective-permute-done((bf16[256,768]{1,0:T(8,128)(2,1)S(1)}, bf16[256,768]{1,0:T(8,128)(2,1)}, u32[]{:S(2)}, u32[]{:S(2)}) %collective-permute-start.18) | collective-permute-done | bytes 393248 | tf_op jit(solution)/shard_map/ppermute | solution.py:41
  142.9 9.3 collective-permute-done.20.refs_7_
  152.3 20.4 %shard_map.214 = (bf16[512,768]{1,0:T(8,128)(2,1)}, bf16[512,2048]{1,0:T(8,128)(2,1)}, bf16[512,2048]{1,0:T(8,128)(2,1)}, bf16[512,2048]{1,0:T(8,128)(2,1)}, f32...) custom-call(s32[2]{0:T(128)} %pad_add_fusion.1.refs_0_, ...), custom_call_target="tpu_custom_call" | custom-call | flops 8858370048 | bytes 31457280 | tf_op jit(solution)/shard_map/pallas_call | solution.py:366
  176.5 9.2 collective-permute-done.25
  185.7 7.5 collective-permute-done.24
  213.8 22.4 %all-to-all-done.2 = bf16[4,256,576]{1,2,0:T(8,128)(2,1)} async-done(((bf16[4,256,576]{1,2,0:T(8,128)(2,1)}), bf16[4,256,576]{1,2,0:T(8,128)(2,1)}, u32[]{:S(2)}, u32[]{:S(2)}) %all-to-all-start.2) | async-done | bytes 1179680 | tf_op jit(solution)/shard_map/all_to_all | solution.py:29
  237.9 6.7 shard_map.215
  278.6 8.4 collective-permute-done.32.refs_7_
  287.8 20.4 %shard_map.216 = (bf16[512,768]{1,0:T(8,128)(2,1)}, bf16[512,2048]{1,0:T(8,128)(2,1)}, bf16[512,2048]{1,0:T(8,128)(2,1)}, bf16[512,2048]{1,0:T(8,128)(2,1)}, f32...) custom-call(s32[2]{0:T(128)} %pad_add_fusion.2.refs_0_, ...), custom_call_target="tpu_custom_call" | custom-call | flops 8858370048 | bytes 31457280 | tf_op jit(solution)/shard_map/pallas_call | solution.py:366
  310.9 22.8 %shard_map.217 = (bf16[512,768]{1,0:T(8,128)(2,1)}, bf16[512,2048]{1,0:T(8,128)(2,1)}, bf16[512,2048]{1,0:T(8,128)(2,1)}, bf16[1024,512]{1,0:T(8,128)(2,1)}, bf1...) custom-call(s32[2]{0:T(128)} %pad_add_fusion.2.refs_0_, ...), custom_call_target="tpu_custom_call" | custom-call | flops 8858370048 | bytes 31457280 | tf_op jit(solution)/shard_map/pallas_call | solution.py:366
  372.1 6.2 collective-permute-done.39
  403.3 17.3 %all-to-all-done.4 = bf16[4,256,192]{1,2,0:T(8,128)(2,1)} async-done(((bf16[4,256,192]{1,2,0:T(8,128)(2,1)}), bf16[4,256,192]{1,2,0:T(8,128)(2,1)}, u32[]{:S(2)}, u32[]{:S(2)}) %all-to-all-start.4) | async-done | bytes 393248 | tf_op jit(solution)/shard_map/all_to_all | solution.py:29
  421.8 12.2 %shard_map.218 = bf16[1024,576]{1,0:T(8,128)(2,1)S(1)} custom-call(s32[2]{0:T(128)S(1)} %slice_bitcast_fusion.1.ends_ref, bf16[1024,576]{1,0:T(8,128)(2,1)S(1)} %bitcast.272, bf16[1024,192]{1,0:T(8,128)(2,1)S(1)} %bitcast.277), custom_call_target="tpu_custom_call" | custom-call | flops 2013265920 | bytes 3145728 | tf_op jit(solution)/shard_map/pallas_call | solution.py:169
  443.1 5.9 collective-permute-start.44
  470.9 6.1 all-to-all-start.6
  478.4 13.9 %collective-permute-done.44 = bf16[192,4096]{1,0:T(8,128)(2,1)} collective-permute-done((bf16[192,4096]{1,0:T(8,128)(2,1)}, bf16[192,4096]{1,0:T(8,128)(2,1)}, u32[]{:S(2)}, u32[]{:S(2)}) %collective-permute-start.44) | collective-permute-done | bytes 1572896 | tf_op jit(solution)/shard_map/ppermute | solution.py:502
  497.5 6.6 collective-permute-start.49
  520.6 11.9 %collective-permute-done.47.refs_6_ = bf16[256,768]{1,0:T(8,128)(2,1)S(1)} collective-permute-done((bf16[256,768]{1,0:T(8,128)(2,1)S(1)}, bf16[256,768]{1,0:T(8,128)(2,1)S(1)}, u32[]{:S(2)}, u32[]{:S(2)}) %collective-permute-start.47) | collective-permute-done | bytes 393248 | tf_op jit(solution)/shard_map/ppermute | solution.py:41
  536.8 4.5 all-to-all-start.7
  554.7 23.1 %shard_map.219 = (bf16[512,768]{1,0:T(8,128)(2,1)}, bf16[512,2048]{1,0:T(8,128)(2,1)}, bf16[512,2048]{1,0:T(8,128)(2,1)}, bf16[1024,512]{1,0:T(8,128)(2,1)}, bf1...) custom-call(s32[2]{0:T(128)} %pad_add_fusion.1.refs_0_, ...), custom_call_target="tpu_custom_call" | custom-call | flops 8858370048 | bytes 31457280 | tf_op jit(solution)/shard_map/pallas_call | solution.py:366
  577.8 8.7 collective-permute-start.62
  616.0 6.5 collective-permute-start.66
  622.5 4.9 collective-permute-done.58
  659.4 6.3 collective-permute-start.72
  686.2 11.9 %shard_map.220 = bf16[1024,576]{1,0:T(8,128)(2,1)S(1)} custom-call(s32[2]{0:T(128)S(1)} %slice_bitcast_fusion.1.ends_ref, bf16[1024,576]{1,0:T(8,128)(2,1)S(1)} %bitcast.270, bf16[1024,192]{1,0:T(8,128)(2,1)S(1)} %bitcast.275), custom_call_target="tpu_custom_call" | custom-call | flops 2013265920 | bytes 3145728 | tf_op jit(solution)/shard_map/pallas_call | solution.py:169
  698.1 5.8 collective-permute-start.76
  723.9 29.4 %all-to-all-done.9 = bf16[4,256,576]{1,2,0:T(8,128)(2,1)S(1)} async-done(((bf16[4,256,576]{1,2,0:T(8,128)(2,1)}), bf16[4,256,576]{1,2,0:T(8,128)(2,1)S(1)}, u32[]{:S(2)}, u32[]{:S(2)}) %all-to-all-start.9) | async-done | bytes 1179680 | tf_op jit(solution)/shard_map/all_to_all | solution.py:29
  759.6 6.4 collective-permute-start.85
  787.1 4.5 all-to-all-start.11
  797.1 6.2 collective-permute-start.82
  812.6 7.6 all-to-all-done.11
  824.4 5.8 collective-permute-start.97
  835.3 10.0 %collective-permute-done.97 = bf16[384,1024]{1,0:T(8,128)(2,1)S(1)} collective-permute-done((bf16[384,1024]{1,0:T(8,128)(2,1)}, bf16[384,1024]{1,0:T(8,128)(2,1)S(1)}, u32[]{:S(2)}, u32[]{:S(2)}) %collective-permute-start.97) | collective-permute-done | bytes 786464 | tf_op jit(solution)/shard_map/ppermute | solution.py:502
  846.6 12.0 %collective-permute-done.95 = bf16[1024,768]{1,0:T(8,128)(2,1)S(1)} collective-permute-done((bf16[1024,768]{1,0:T(8,128)(2,1)S(1)}, bf16[1024,768]{1,0:T(8,128)(2,1)S(1)}, u32[]{:S(2)}, u32[]{:S(2)}) %collective-permute-start.95) | collective-permute-done | bytes 1572896 | tf_op jit(solution)/shard_map/ppermute | solution.py:502
  858.9 6.4 collective-permute-start.99
  869.7 11.5 %collective-permute-start.94 = (bf16[96,3200]{1,0:T(8,128)(2,1)S(1)}, bf16[96,3200]{1,0:T(8,128)(2,1)S(1)}, u32[]{:S(2)}, u32[]{:S(2)}) collective-permute-start(bf16[96,3200]{1,0:T(8,128)(2,1)S(1)} %reduce_sum.248), channel_id=1, source_target_pairs={{0,4},{12,8},{1,5},{13,9},{2,6},{14,10},{3,7},{15,11},{16,20},{28,... | collective-permute-start | bytes 1843208 | tf_op jit(solution)/shard_map/ppermute | solution.py:502
  883.1 11.7 %collective-permute-done.94 = bf16[96,3200]{1,0:T(8,128)(2,1)S(1)} collective-permute-done((bf16[96,3200]{1,0:T(8,128)(2,1)S(1)}, bf16[96,3200]{1,0:T(8,128)(2,1)S(1)}, u32[]{:S(2)}, u32[]{:S(2)}) %collective-permute-start.94) | collective-permute-done | bytes 614432 | tf_op jit(solution)/shard_map/ppermute | solution.py:502
  909.0 17.1 %collective-permute-done.100 = bf16[192,4096]{1,0:T(8,128)(2,1)S(1)} collective-permute-done((bf16[192,4096]{1,0:T(8,128)(2,1)S(1)}, bf16[192,4096]{1,0:T(8,128)(2,1)S(1)}, u32[]{:S(2)}, u32[]{:S(2)}) %collective-permute-start.100) | collective-permute-done | bytes 1572896 | tf_op jit(solution)/shard_map/ppermute | solution.py:502
  926.2 6.4 collective-permute-start.105
  941.1 5.3 maximum_convert_fusion
  946.4 8.4 collective-permute-done.106
  961.0 13.6 %collective-permute-done.108 = bf16[96,3200]{1,0:T(8,128)(2,1)S(1)} collective-permute-done((bf16[96,3200]{1,0:T(8,128)(2,1)S(1)}, bf16[96,3200]{1,0:T(8,128)(2,1)S(1)}, u32[]{:S(2)}, u32[]{:S(2)}) %collective-permute-start.108) | collective-permute-done | bytes 614432 | tf_op jit(solution)/shard_map/ppermute | solution.py:502
  (771 shorter events, 482.8 us)
Async XLA Ops:
  17.7 134.6 %collective-permute-start.21 = (bf16[768,4096]{1,0:T(8,128)(2,1)}, bf16[768,4096]{1,0:T(8,128)(2,1)}, u32[]{:S(2)}, u32[]{:S(2)}) collective-permute-start(bf16[768,4096]{1,0:T(8,128)(2,1)} %bitcast.279), channel_id=1, source_target_pairs={{0,16},{16,0},{1,17},{17,1},{2,18},{18,2},{3,19},{19,3},{4,20},{20... | collective-permute-start | bytes 18874376 | tf_op jit(solution)/shard_map/ppermute | solution.py:25
  54.4 41.8 %all-to-all-start = ((bf16[4,256,576]{1,2,0:T(8,128)(2,1)}), bf16[4,256,576]{1,2,0:T(8,128)(2,1)S(1)}, u32[]{:S(2)}, u32[]{:S(2)}) async-start(bf16[4,256,576]{1,2,0:T(8,128)(2,1)} %bitcast.17), calls=%async_computation | async-start | bytes 2359296 | tf_op jit(solution)/shard_map/all_to_all | solution.py:29
  59.2 113.5 %all-gather.3.cloned.1.call-start = ((), (), s32[]{:S(2)}) async-start(), calls=%async_computation.12 | async-start | bytes 3072000 | tf_op jit(solution)/shard_map/all_gather | solution.py:701
  80.5 51.0 %collective-permute-start.22 = (bf16[2048,768]{1,0:T(8,128)(2,1)}, bf16[2048,768]{1,0:T(8,128)(2,1)}, u32[]{:S(2)}, u32[]{:S(2)}) collective-permute-start(bf16[2048,768]{1,0:T(8,128)(2,1)} %bitcast.288), channel_id=1, source_target_pairs={{0,16},{16,0},{1,17},{17,1},{2,18},{18,2},{3,19},{19,3},{4,20},{20... | collective-permute-start | bytes 9437192 | tf_op jit(solution)/shard_map/ppermute | solution.py:25
  203.7 32.5 %all-to-all-start.2 = ((bf16[4,256,576]{1,2,0:T(8,128)(2,1)}), bf16[4,256,576]{1,2,0:T(8,128)(2,1)}, u32[]{:S(2)}, u32[]{:S(2)}) async-start(bf16[4,256,576]{1,2,0:T(8,128)(2,1)} %bitcast.61), calls=%async_computation.2 | async-start | bytes 2359296 | tf_op jit(solution)/shard_map/all_to_all | solution.py:29
  308.2 50.4 %collective-permute-start.35 = (bf16[256,768]{1,0:T(8,128)(2,1)}, bf16[256,768]{1,0:T(8,128)(2,1)}, u32[]{:S(2)}, u32[]{:S(2)}) collective-permute-start(bf16[256,768]{1,0:T(8,128)(2,1)} %get-tuple-element.298), channel_id=1, source_target_pairs={{0,3},{1,2},{2,1},{3,0},{4,7},{5,6},{6,5},{7,4},{8,11},{9,10},{10,... | collective-permute-start | bytes 1179656 | tf_op jit(solution)/shard_map/ppermute | solution.py:46
  309.5 49.1 %collective-permute-start.34 = (bf16[256,768]{1,0:T(8,128)(2,1)}, bf16[256,768]{1,0:T(8,128)(2,1)}, u32[]{:S(2)}, u32[]{:S(2)}) collective-permute-start(bf16[256,768]{1,0:T(8,128)(2,1)} %get-tuple-element.297), channel_id=1, source_target_pairs={{0,2},{1,3},{2,0},{3,1},{4,6},{5,7},{6,4},{7,5},{8,10},{9,11},{10,... | collective-permute-start | bytes 1179656 | tf_op jit(solution)/shard_map/ppermute | solution.py:46
  309.8 50.3 %collective-permute-start.33 = (bf16[256,768]{1,0:T(8,128)(2,1)}, bf16[256,768]{1,0:T(8,128)(2,1)}, u32[]{:S(2)}, u32[]{:S(2)}) collective-permute-start(bf16[256,768]{1,0:T(8,128)(2,1)} %get-tuple-element.296), channel_id=1, source_target_pairs={{0,1},{1,0},{2,3},{3,2},{4,5},{5,4},{6,7},{7,6},{8,9},{9,8},{10,11... | collective-permute-start | bytes 1179656 | tf_op jit(solution)/shard_map/ppermute | solution.py:46
  363.8 31.7 %collective-permute-start.42 = (bf16[384,2048]{1,0:T(8,128)(2,1)}, bf16[384,2048]{1,0:T(8,128)(2,1)}, u32[]{:S(2)}, u32[]{:S(2)}) collective-permute-start(bf16[384,2048]{1,0:T(8,128)(2,1)} %convolution_convert_fusion.6), channel_id=1, source_target_pairs={{0,16},{16,0},{1,17},{17,1},{2,18},{18,2},{3,19},{19,3},{4,20},{20... | collective-permute-start | bytes 4718600 | tf_op jit(solution)/shard_map/ppermute | solution.py:25
  367.6 31.2 %collective-permute-start.41 = (bf16[384,2048]{1,0:T(8,128)(2,1)}, bf16[384,2048]{1,0:T(8,128)(2,1)}, u32[]{:S(2)}, u32[]{:S(2)}) collective-permute-start(bf16[384,2048]{1,0:T(8,128)(2,1)} %convolution_convert_fusion.7), channel_id=1, source_target_pairs={{0,16},{16,0},{1,17},{17,1},{2,18},{18,2},{3,19},{19,3},{4,20},{20... | collective-permute-start | bytes 4718600 | tf_op jit(solution)/shard_map/ppermute | solution.py:25
  371.6 82.5 %collective-permute-start.54 = (bf16[384,1024]{1,0:T(8,128)(2,1)}, bf16[384,1024]{1,0:T(8,128)(2,1)}, u32[]{:S(2)}, u32[]{:S(2)}) collective-permute-start(bf16[384,1024]{1,0:T(8,128)(2,1)} %convolution_convert_fusion.11), channel_id=1, source_target_pairs={{0,16},{16,0},{1,17},{17,1},{2,18},{18,2},{3,19},{19,3},{4,20},{20... | collective-permute-start | bytes 2359304 | tf_op jit(solution)/shard_map/ppermute | solution.py:25
  371.8 70.1 %collective-permute-start.36 = (bf16[256,768]{1,0:T(8,128)(2,1)}, bf16[256,768]{1,0:T(8,128)(2,1)}, u32[]{:S(2)}, u32[]{:S(2)}) collective-permute-start(bf16[256,768]{1,0:T(8,128)(2,1)} %get-tuple-element.596), channel_id=1, source_target_pairs={{0,16},{16,0},{1,17},{17,1},{2,18},{18,2},{3,19},{19,3},{4,20},{20... | collective-permute-start | bytes 1179656 | tf_op jit(solution)/shard_map/ppermute | solution.py:25
  378.4 56.7 %collective-permute-start.43 = (bf16[1024,768]{1,0:T(8,128)(2,1)}, bf16[1024,768]{1,0:T(8,128)(2,1)}, u32[]{:S(2)}, u32[]{:S(2)}) collective-permute-start(bf16[1024,768]{1,0:T(8,128)(2,1)} %add_convert_fusion.17), channel_id=1, source_target_pairs={{0,4},{12,8},{1,5},{13,9},{2,6},{14,10},{3,7},{15,11},{16,20},{28,... | collective-permute-start | bytes 4718600 | tf_op jit(solution)/shard_map/ppermute | solution.py:502
  437.5 33.4 %all-to-all-start.5 = ((bf16[4,256,576]{1,2,0:T(8,128)(2,1)}), bf16[4,256,576]{1,2,0:T(8,128)(2,1)}, u32[]{:S(2)}, u32[]{:S(2)}) async-start(bf16[4,256,576]{1,2,0:T(8,128)(2,1)} %copy.290), calls=%async_computation.5 | async-start | bytes 2359296 | tf_op jit(solution)/shard_map/all_to_all | solution.py:29
  443.1 49.1 %collective-permute-start.44 = (bf16[192,4096]{1,0:T(8,128)(2,1)}, bf16[192,4096]{1,0:T(8,128)(2,1)}, u32[]{:S(2)}, u32[]{:S(2)}) collective-permute-start(bf16[192,4096]{1,0:T(8,128)(2,1)} %get-tuple-element.366), channel_id=1, source_target_pairs={{0,4},{12,8},{1,5},{13,9},{2,6},{14,10},{3,7},{15,11},{16,20},{28,... | collective-permute-start | bytes 4718600 | tf_op jit(solution)/shard_map/ppermute | solution.py:502
  465.1 71.7 %collective-permute-start.52 = (bf16[1024,768]{1,0:T(8,128)(2,1)}, bf16[1024,768]{1,0:T(8,128)(2,1)}, u32[]{:S(2)}, u32[]{:S(2)}) collective-permute-start(bf16[1024,768]{1,0:T(8,128)(2,1)} %add_convert_fusion.14), channel_id=1, source_target_pairs={{4,8},{8,4},{5,9},{9,5},{6,10},{10,6},{7,11},{11,7},{20,24},{24,20... | collective-permute-start | bytes 4718600 | tf_op jit(solution)/shard_map/ppermute | solution.py:502
  467.0 69.8 %collective-permute-start.53 = (bf16[192,4096]{1,0:T(8,128)(2,1)}, bf16[192,4096]{1,0:T(8,128)(2,1)}, u32[]{:S(2)}, u32[]{:S(2)}) collective-permute-start(bf16[192,4096]{1,0:T(8,128)(2,1)} %get-tuple-element.376), channel_id=1, source_target_pairs={{0,4},{12,8},{1,5},{13,9},{2,6},{14,10},{3,7},{15,11},{16,20},{28,... | collective-permute-start | bytes 4718600 | tf_op jit(solution)/shard_map/ppermute | solution.py:502
  470.9 65.8 %all-to-all-start.6 = ((bf16[4,96,1024]{2,1,0:T(8,128)(2,1)}), bf16[4,96,1024]{2,1,0:T(8,128)(2,1)}, u32[]{:S(2)}, u32[]{:S(2)}) async-start(bf16[4,96,1024]{2,1,0:T(8,128)(2,1)} %bitcast.100), calls=%async_computation.6 | async-start | bytes 1572864 | tf_op jit(solution)/shard_map/all_to_all | solution.py:29
  518.8 71.3 %collective-permute-start.55 = (bf16[192,4096]{1,0:T(8,128)(2,1)}, bf16[192,4096]{1,0:T(8,128)(2,1)}, u32[]{:S(2)}, u32[]{:S(2)}) collective-permute-start(bf16[192,4096]{1,0:T(8,128)(2,1)} %add_convert_fusion.13), channel_id=1, source_target_pairs={{4,8},{8,4},{5,9},{9,5},{6,10},{10,6},{7,11},{11,7},{20,24},{24,20... | collective-permute-start | bytes 4718600 | tf_op jit(solution)/shard_map/ppermute | solution.py:502
  532.5 57.5 %collective-permute-start.56 = (bf16[256,768]{1,0:T(8,128)(2,1)}, bf16[256,768]{1,0:T(8,128)(2,1)S(1)}, u32[]{:S(2)}, u32[]{:S(2)}) collective-permute-start(bf16[256,768]{1,0:T(8,128)(2,1)} %fusion.10), channel_id=1, source_target_pairs={{0,4},{12,8},{1,5},{13,9},{2,6},{14,10},{3,7},{15,11},{16,20},{28,... | collective-permute-start | bytes 1179656 | tf_op jit(solution)/shard_map/ppermute | solution.py:502
  536.8 51.1 %all-to-all-start.7 = ((bf16[4,96,3200]{2,1,0:T(8,128)(2,1)}), bf16[4,96,3200]{2,1,0:T(8,128)(2,1)}, u32[]{:S(2)}, u32[]{:S(2)}) async-start(bf16[4,96,3200]{2,1,0:T(8,128)(2,1)} %pad_maximum_fusion.2), calls=%async_computation.7 | async-start | bytes 4915200 | tf_op jit(solution)/shard_map/all_to_all | solution.py:29
  544.7 68.5 %collective-permute-start.60 = (bf16[1024,768]{1,0:T(8,128)(2,1)}, bf16[1024,768]{1,0:T(8,128)(2,1)}, u32[]{:S(2)}, u32[]{:S(2)}) collective-permute-start(bf16[1024,768]{1,0:T(8,128)(2,1)} %add_convert_fusion.12), channel_id=1, source_target_pairs={{4,0},{8,12},{5,1},{9,13},{6,2},{10,14},{7,3},{11,15},{20,16},{24,... | collective-permute-start | bytes 4718600 | tf_op jit(solution)/shard_map/ppermute | solution.py:502
  549.6 65.0 %collective-permute-start.61 = (bf16[192,4096]{1,0:T(8,128)(2,1)}, bf16[192,4096]{1,0:T(8,128)(2,1)}, u32[]{:S(2)}, u32[]{:S(2)}) collective-permute-start(bf16[192,4096]{1,0:T(8,128)(2,1)} %add_convert_fusion.11), channel_id=1, source_target_pairs={{4,8},{8,4},{5,9},{9,5},{6,10},{10,6},{7,11},{11,7},{20,24},{24,20... | collective-permute-start | bytes 4718600 | tf_op jit(solution)/shard_map/ppermute | solution.py:502
  613.3 52.4 %collective-permute-start.64 = (bf16[192,4096]{1,0:T(8,128)(2,1)}, bf16[192,4096]{1,0:T(8,128)(2,1)}, u32[]{:S(2)}, u32[]{:S(2)}) collective-permute-start(bf16[192,4096]{1,0:T(8,128)(2,1)} %add_convert_fusion.9), channel_id=1, source_target_pairs={{4,0},{8,12},{5,1},{9,13},{6,2},{10,14},{7,3},{11,15},{20,16},{24,... | collective-permute-start | bytes 4718600 | tf_op jit(solution)/shard_map/ppermute | solution.py:502
  614.6 43.6 %collective-permute-start.65 = (bf16[256,768]{1,0:T(8,128)(2,1)}, bf16[256,768]{1,0:T(8,128)(2,1)}, u32[]{:S(2)}, u32[]{:S(2)}) collective-permute-start(bf16[256,768]{1,0:T(8,128)(2,1)} %add_convert_fusion.33), channel_id=1, source_target_pairs={{4,8},{8,4},{5,9},{9,5},{6,10},{10,6},{7,11},{11,7},{20,24},{24,20... | collective-permute-start | bytes 1179656 | tf_op jit(solution)/shard_map/ppermute | solution.py:502
  616.0 43.4 %collective-permute-start.66 = (bf16[96,3200]{1,0:T(8,128)(2,1)S(1)}, bf16[96,3200]{1,0:T(8,128)(2,1)}, u32[]{:S(2)}, u32[]{:S(2)}) collective-permute-start(bf16[96,3200]{1,0:T(8,128)(2,1)S(1)} %reduce_sum.240), channel_id=1, source_target_pairs={{0,4},{12,8},{1,5},{13,9},{2,6},{14,10},{3,7},{15,11},{16,20},{28,... | collective-permute-start | bytes 1843208 | tf_op jit(solution)/shard_map/ppermute | solution.py:502
  640.9 31.2 %collective-permute-start.87 = (bf16[384,1024]{1,0:T(8,128)(2,1)}, bf16[384,1024]{1,0:T(8,128)(2,1)}, u32[]{:S(2)}, u32[]{:S(2)}) collective-permute-start(bf16[384,1024]{1,0:T(8,128)(2,1)} %convolution_convert_fusion.10), channel_id=1, source_target_pairs={{0,16},{16,0},{1,17},{17,1},{2,18},{18,2},{3,19},{19,3},{4,20},{20... | collective-permute-start | bytes 2359304 | tf_op jit(solution)/shard_map/ppermute | solution.py:25
  658.1 45.9 %collective-permute-start.70 = (bf16[192,4096]{1,0:T(8,128)(2,1)}, bf16[192,4096]{1,0:T(8,128)(2,1)}, u32[]{:S(2)}, u32[]{:S(2)}) collective-permute-start(bf16[192,4096]{1,0:T(8,128)(2,1)} %add_convert_fusion.6), channel_id=1, source_target_pairs={{4,0},{8,12},{5,1},{9,13},{6,2},{10,14},{7,3},{11,15},{20,16},{24,... | collective-permute-start | bytes 4718600 | tf_op jit(solution)/shard_map/ppermute | solution.py:502
  659.4 44.5 %collective-permute-start.72 = (bf16[1024,768]{1,0:T(8,128)(2,1)}, bf16[1024,768]{1,0:T(8,128)(2,1)}, u32[]{:S(2)}, u32[]{:S(2)}) collective-permute-start(bf16[1024,768]{1,0:T(8,128)(2,1)} %add_convert_fusion.10), channel_id=1, source_target_pairs={{0,4},{12,8},{1,5},{13,9},{2,6},{14,10},{3,7},{15,11},{16,20},{28,... | collective-permute-start | bytes 4718600 | tf_op jit(solution)/shard_map/ppermute | solution.py:502
  670.8 33.2 %collective-permute-start.73 = (bf16[192,4096]{1,0:T(8,128)(2,1)}, bf16[192,4096]{1,0:T(8,128)(2,1)}, u32[]{:S(2)}, u32[]{:S(2)}) collective-permute-start(bf16[192,4096]{1,0:T(8,128)(2,1)} %broadcast_select_fusion.9), channel_id=1, source_target_pairs={{0,16},{1,17},{2,18},{3,19},{4,20},{5,21},{6,22},{7,23},{8,24},{9,... | collective-permute-start | bytes 4718600 | tf_op jit(solution)/shard_map/ppermute | solution.py:502
  684.5 73.0 %collective-permute-start.74 = (bf16[256,768]{1,0:T(8,128)(2,1)}, bf16[256,768]{1,0:T(8,128)(2,1)}, u32[]{:S(2)}, u32[]{:S(2)}) collective-permute-start(bf16[256,768]{1,0:T(8,128)(2,1)} %add_convert_fusion.32), channel_id=1, source_target_pairs={{4,0},{8,12},{5,1},{9,13},{6,2},{10,14},{7,3},{11,15},{20,16},{24,... | collective-permute-start | bytes 1179656 | tf_op jit(solution)/shard_map/ppermute | solution.py:502
  698.1 67.8 %collective-permute-start.76 = (bf16[192,4096]{1,0:T(8,128)(2,1)}, bf16[192,4096]{1,0:T(8,128)(2,1)}, u32[]{:S(2)}, u32[]{:S(2)}) collective-permute-start(bf16[192,4096]{1,0:T(8,128)(2,1)} %get-tuple-element.415), channel_id=1, source_target_pairs={{0,4},{12,8},{1,5},{13,9},{2,6},{14,10},{3,7},{15,11},{16,20},{28,... | collective-permute-start | bytes 4718600 | tf_op jit(solution)/shard_map/ppermute | solution.py:502
  705.4 47.8 %all-to-all-start.9 = ((bf16[4,256,576]{1,2,0:T(8,128)(2,1)}), bf16[4,256,576]{1,2,0:T(8,128)(2,1)S(1)}, u32[]{:S(2)}, u32[]{:S(2)}) async-start(bf16[4,256,576]{1,2,0:T(8,128)(2,1)} %copy.300), calls=%async_computation.9 | async-start | bytes 2359296 | tf_op jit(solution)/shard_map/all_to_all | solution.py:29
  711.9 54.1 %collective-permute-start.77 = (bf16[192,4096]{1,0:T(8,128)(2,1)}, bf16[192,4096]{1,0:T(8,128)(2,1)}, u32[]{:S(2)}, u32[]{:S(2)}) collective-permute-start(bf16[192,4096]{1,0:T(8,128)(2,1)} %broadcast_select_fusion.8), channel_id=1, source_target_pairs={{0,16},{1,17},{2,18},{3,19},{4,20},{5,21},{6,22},{7,23},{8,24},{9,... | collective-permute-start | bytes 4718600 | tf_op jit(solution)/shard_map/ppermute | solution.py:502
  715.2 44.4 %collective-permute-start.75 = (bf16[96,3200]{1,0:T(8,128)(2,1)}, bf16[96,3200]{1,0:T(8,128)(2,1)}, u32[]{:S(2)}, u32[]{:S(2)}) collective-permute-start(bf16[96,3200]{1,0:T(8,128)(2,1)} %add_convert_fusion.27), channel_id=1, source_target_pairs={{4,8},{8,4},{5,9},{9,5},{6,10},{10,6},{7,11},{11,7},{20,24},{24,20... | collective-permute-start | bytes 1843208 | tf_op jit(solution)/shard_map/ppermute | solution.py:502
  719.4 74.5 %collective-permute-start.83 = (bf16[384,1024]{1,0:T(8,128)(2,1)}, bf16[384,1024]{1,0:T(8,128)(2,1)}, u32[]{:S(2)}, u32[]{:S(2)}) collective-permute-start(bf16[384,1024]{1,0:T(8,128)(2,1)} %add_convert_fusion.21), channel_id=1, source_target_pairs={{4,0},{8,12},{5,1},{9,13},{6,2},{10,14},{7,3},{11,15},{20,16},{24,... | collective-permute-start | bytes 2359304 | tf_op jit(solution)/shard_map/ppermute | solution.py:502
  753.2 33.9 %all-to-all-start.10 = ((bf16[4,96,1024]{2,1,0:T(8,128)(2,1)}), bf16[4,96,1024]{2,1,0:T(8,128)(2,1)}, u32[]{:S(2)}, u32[]{:S(2)}) async-start(bf16[4,96,1024]{2,1,0:T(8,128)(2,1)} %bitcast.339), calls=%async_computation.10 | async-start | bytes 1572864 | tf_op jit(solution)/shard_map/all_to_all | solution.py:29
  757.5 37.7 %collective-permute-start.84 = (bf16[1024,768]{1,0:T(8,128)(2,1)}, bf16[1024,768]{1,0:T(8,128)(2,1)}, u32[]{:S(2)}, u32[]{:S(2)}) collective-permute-start(bf16[1024,768]{1,0:T(8,128)(2,1)} %add_convert_fusion.4), channel_id=1, source_target_pairs={{4,8},{8,4},{5,9},{9,5},{6,10},{10,6},{7,11},{11,7},{20,24},{24,20... | collective-permute-start | bytes 4718600 | tf_op jit(solution)/shard_map/ppermute | solution.py:502
  759.6 37.5 %collective-permute-start.85 = (bf16[192,4096]{1,0:T(8,128)(2,1)}, bf16[192,4096]{1,0:T(8,128)(2,1)}, u32[]{:S(2)}, u32[]{:S(2)}) collective-permute-start(bf16[192,4096]{1,0:T(8,128)(2,1)} %get-tuple-element.436), channel_id=1, source_target_pairs={{0,4},{12,8},{1,5},{13,9},{2,6},{14,10},{3,7},{15,11},{16,20},{28,... | collective-permute-start | bytes 4718600 | tf_op jit(solution)/shard_map/ppermute | solution.py:502
  782.8 82.4 %collective-permute-start.79 = (f32[256,768]{1,0:T(8,128)}, f32[256,768]{1,0:T(8,128)}, u32[]{:S(2)}, u32[]{:S(2)}) collective-permute-start(f32[256,768]{1,0:T(8,128)} %get-tuple-element.588), channel_id=1, source_target_pairs={{0,16},{16,0},{1,17},{17,1},{2,18},{18,2},{3,19},{19,3},{4,20},{20... | collective-permute-start | bytes 2359304 | tf_op jit(solution)/shard_map/ppermute | solution.py:25
  787.1 33.1 %all-to-all-start.11 = ((bf16[4,96,3200]{2,1,0:T(8,128)(2,1)}), bf16[4,96,3200]{2,1,0:T(8,128)(2,1)}, u32[]{:S(2)}, u32[]{:S(2)}) async-start(bf16[4,96,3200]{2,1,0:T(8,128)(2,1)} %pad_maximum_fusion.3), calls=%async_computation.11 | async-start | bytes 4915200 | tf_op jit(solution)/shard_map/all_to_all | solution.py:29
  795.2 35.0 %collective-permute-start.81 = (bf16[192,4096]{1,0:T(8,128)(2,1)}, bf16[192,4096]{1,0:T(8,128)(2,1)}, u32[]{:S(2)}, u32[]{:S(2)}) collective-permute-start(bf16[192,4096]{1,0:T(8,128)(2,1)} %add_convert_fusion.5), channel_id=1, source_target_pairs={{4,8},{8,4},{5,9},{9,5},{6,10},{10,6},{7,11},{11,7},{20,24},{24,20... | collective-permute-start | bytes 4718600 | tf_op jit(solution)/shard_map/ppermute | solution.py:502
  822.3 36.3 %collective-permute-start.95 = (bf16[1024,768]{1,0:T(8,128)(2,1)S(1)}, bf16[1024,768]{1,0:T(8,128)(2,1)S(1)}, u32[]{:S(2)}, u32[]{:S(2)}) collective-permute-start(bf16[1024,768]{1,0:T(8,128)(2,1)S(1)} %add_convert_fusion.2), channel_id=1, source_target_pairs={{4,0},{8,12},{5,1},{9,13},{6,2},{10,14},{7,3},{11,15},{20,16},{24,... | collective-permute-start | bytes 4718600 | tf_op jit(solution)/shard_map/ppermute | solution.py:502
  823.6 35.0 %collective-permute-start.96 = (bf16[192,4096]{1,0:T(8,128)(2,1)}, bf16[192,4096]{1,0:T(8,128)(2,1)S(1)}, u32[]{:S(2)}, u32[]{:S(2)}) collective-permute-start(bf16[192,4096]{1,0:T(8,128)(2,1)} %add_convert_fusion.1), channel_id=1, source_target_pairs={{4,8},{8,4},{5,9},{9,5},{6,10},{10,6},{7,11},{11,7},{20,24},{24,20... | collective-permute-start | bytes 4718600 | tf_op jit(solution)/shard_map/ppermute | solution.py:502
  845.3 49.4 %collective-permute-start.92 = (bf16[192,4096]{1,0:T(8,128)(2,1)S(1)}, bf16[192,4096]{1,0:T(8,128)(2,1)S(1)}, u32[]{:S(2)}, u32[]{:S(2)}) collective-permute-start(bf16[192,4096]{1,0:T(8,128)(2,1)S(1)} %add_convert_fusion.3), channel_id=1, source_target_pairs={{4,0},{8,12},{5,1},{9,13},{6,2},{10,14},{7,3},{11,15},{20,16},{24,... | collective-permute-start | bytes 4718600 | tf_op jit(solution)/shard_map/ppermute | solution.py:502
  858.9 35.9 %collective-permute-start.99 = (bf16[1024,768]{1,0:T(8,128)(2,1)S(1)}, bf16[1024,768]{1,0:T(8,128)(2,1)S(1)}, u32[]{:S(2)}, u32[]{:S(2)}) collective-permute-start(bf16[1024,768]{1,0:T(8,128)(2,1)S(1)} %broadcast_select_fusion.10), channel_id=1, source_target_pairs={{16,0},{17,1},{18,2},{19,3},{20,4},{21,5},{22,6},{23,7},{24,8},{25... | collective-permute-start | bytes 4718600 | tf_op jit(solution)/shard_map/ppermute | solution.py:502
  881.7 44.3 %collective-permute-start.100 = (bf16[192,4096]{1,0:T(8,128)(2,1)S(1)}, bf16[192,4096]{1,0:T(8,128)(2,1)S(1)}, u32[]{:S(2)}, u32[]{:S(2)}) collective-permute-start(bf16[192,4096]{1,0:T(8,128)(2,1)S(1)} %add_convert_fusion), channel_id=1, source_target_pairs={{4,0},{8,12},{5,1},{9,13},{6,2},{10,14},{7,3},{11,15},{20,16},{24,... | collective-permute-start | bytes 4718600 | tf_op jit(solution)/shard_map/ppermute | solution.py:502
  901.1 36.2 %collective-permute-start.103 = (bf16[256,768]{1,0:T(8,128)(2,1)S(1)}, bf16[256,768]{1,0:T(8,128)(2,1)S(1)}, u32[]{:S(2)}, u32[]{:S(2)}) collective-permute-start(bf16[256,768]{1,0:T(8,128)(2,1)S(1)} %add_convert_fusion.30), channel_id=1, source_target_pairs={{4,0},{8,12},{5,1},{9,13},{6,2},{10,14},{7,3},{11,15},{20,16},{24,... | collective-permute-start | bytes 1179656 | tf_op jit(solution)/shard_map/ppermute | solution.py:502
  (202 other events, 2523.2 us)
Sparse Core Ops, SparseCore 0:
  97.1 43.4 all-gather.2

commit v4 on v3

--- a/solution.py
+++ b/solution.py
@@ -156,7 +156,7 @@
         out_shape=jax.ShapeDtypeStruct((pack, per * HEAD), BF),
         in_specs=[pl.BlockSpec(memory_space=pltpu.SMEM), vmem()],
         out_specs=vmem(),
-        compiler_params=pltpu.CompilerParams(vmem_limit_bytes=32 << 20),
+        compiler_params=pltpu.CompilerParams(vmem_limit_bytes=16 << 20),
         cost_estimate=pl.CostEstimate(
             flops=4 * per * pack * pack * HEAD, bytes_accessed=8 * pack * columns // 3, transcendentals=per * pack * pack
         ),
@@ -172,7 +172,7 @@
         in_specs=[pl.BlockSpec(memory_space=pltpu.SMEM), vmem(), vmem()],
         out_specs=vmem(),
         scratch_shapes=[pltpu.VMEM((per, pack, HEAD), F32)] * 2,
-        compiler_params=pltpu.CompilerParams(vmem_limit_bytes=32 << 20),
+        compiler_params=pltpu.CompilerParams(vmem_limit_bytes=16 << 20),
         cost_estimate=pl.CostEstimate(
             flops=10 * per * pack * pack * HEAD, bytes_accessed=16 * pack * columns // 3, transcendentals=per * pack * pack
         ),
@@ -686,7 +686,7 @@
     expert_weights = ((w.w_ein, w.w_edown), (swap_cores(w.w_ein), swap_cores(w.w_edown)))
     which = [jnp.stack([me, (core == s).astype(I32)]) for s in range(2)]
     heads_0 = to_heads(projected, lanes, 3)
-    heads_0, slot, info, w_out_0 = lax.optimization_barrier((heads_0, slot, info, w_out_0))
+    heads_0, slot, info = lax.optimization_barrier((heads_0, slot, info))
     context = (me, slot, info, capacity, experts)
     later = jnp.concatenate([w.first_shares[1], w.out_shares[1]], axis=1)
     mixed_0, shared = lax.optimization_barrier((attention_forward(ends, heads_0, tokens), shared))

time: 1000 us -> 1010 us (1.010)
    unnamed x281 -> x283, local copies, waits for them, and re-layouts: 21.7 us -> 18.9 us
  transfers between devices with their start and end apart: 124 -> 124, of which waited for: 28 -> 28; matrix products, arithmetic and copies ran while one was open for 29% -> 28% of each run, Pallas kernels for 10% -> 10%
where the time goes in v4:
time: 1010 us; the launch traced here: 996 us
  waiting for transfers between devices  275 us (27%)
  starting transfers between devices  261 us (26%)
  other arithmetic  154 us (15%)
  Pallas kernels  124 us (12%)
  local copies, waits for them, and re-layouts  83.3 us (8%)
  matrix products  79.9 us (8%)
  between operations  19 us (2%)
    ppermute x48, starting transfers between devices, launch(): got = lax.ppermute(value, axis, pairs)  138 us
    ppermute x48, waiting for transfers between devices, launch(): got = lax.ppermute(value, axis, pairs)  90.1 us
    all_to_all x12, waiting for transfers between devices, a2a(): return lax.all_to_all(v, axis, split_axis=0, concat_axis=0, tiled=True)  88.9 us
    pallas_call x4, Pallas kernels, moe_call(): pl.pallas_call(kernel, out_shape=[jax.ShapeDtypeStruct(*shape) for shape...  86.5 us
    dot_general x40, matrix products, mm(): lax.dot_general(a, b, (((ca,), (cb,)), ((), ())), preferred_element_type=...  79.9 us
    ppermute x21, waiting for transfers between devices, gather_blocks(): lax.ppermute(v, EXP, xor_pairs(members, k))  58.8 us
    convert_element_type x24, other arithmetic, add_low(): return (a.astype(F32) + b.astype(F32)).astype(BF)  52.9 us
    all_to_all x12, starting transfers between devices, a2a(): return lax.all_to_all(v, axis, split_axis=0, concat_axis=0, tiled=True)  52.2 us
  transfers between devices with their start and end apart: 124, of which 28 were waited for; matrix products, arithmetic and copies ran while one was open for 28% of the time, Pallas kernels for 10%

profile of v4, /device:TPU:1, one launch (start us, length us, event | category | flops | bytes accessed | tf_op | source)
XLA Modules:
  0.0 995.9 jit_solution(5644935678260178488)
XLA Ops:
  17.7 8.9 collective-permute-done.3
  27.9 9.0 collective-permute-done.2
  54.4 4.6 all-to-all-start
  76.2 10.1 %collective-permute-done.9 = bf16[192,1024]{1,0:T(8,128)(2,1)} collective-permute-done((bf16[192,1024]{1,0:T(8,128)(2,1)}, bf16[192,1024]{1,0:T(8,128)(2,1)}, u32[]{:S(2)}, u32[]{:S(2)}) %collective-permute-start.9) | collective-permute-done | bytes 393248 | tf_op jit(solution)/shard_map/ppermute | solution.py:46
  103.3 6.6 shard_map.213
  110.9 4.8 all-to-all-start.1
  122.1 4.8 all-to-all-done.1
  134.9 9.0 collective-permute-done.18.refs_5_
  143.9 9.3 collective-permute-done.20.refs_7_
  153.2 20.4 %shard_map.214 = (bf16[512,768]{1,0:T(8,128)(2,1)}, bf16[512,2048]{1,0:T(8,128)(2,1)}, bf16[512,2048]{1,0:T(8,128)(2,1)}, bf16[512,2048]{1,0:T(8,128)(2,1)}, f32...) custom-call(s32[2]{0:T(128)} %pad_add_fusion.1.refs_0_, ...), custom_call_target="tpu_custom_call" | custom-call | flops 8858370048 | bytes 31457280 | tf_op jit(solution)/shard_map/pallas_call | solution.py:366
  177.4 9.2 collective-permute-done.25
  186.6 7.5 collective-permute-done.24
  214.8 22.3 %all-to-all-done.2 = bf16[4,256,576]{1,2,0:T(8,128)(2,1)} async-done(((bf16[4,256,576]{1,2,0:T(8,128)(2,1)}), bf16[4,256,576]{1,2,0:T(8,128)(2,1)}, u32[]{:S(2)}, u32[]{:S(2)}) %all-to-all-start.2) | async-done | bytes 1179680 | tf_op jit(solution)/shard_map/all_to_all | solution.py:29
  238.9 6.7 shard_map.215
  279.6 8.4 collective-permute-done.32.refs_7_
  288.8 20.4 %shard_map.216 = (bf16[512,768]{1,0:T(8,128)(2,1)}, bf16[512,2048]{1,0:T(8,128)(2,1)}, bf16[512,2048]{1,0:T(8,128)(2,1)}, bf16[512,2048]{1,0:T(8,128)(2,1)}, f32...) custom-call(s32[2]{0:T(128)} %pad_add_fusion.2.refs_0_, ...), custom_call_target="tpu_custom_call" | custom-call | flops 8858370048 | bytes 31457280 | tf_op jit(solution)/shard_map/pallas_call | solution.py:366
  312.0 22.6 %shard_map.217 = (bf16[512,768]{1,0:T(8,128)(2,1)}, bf16[512,2048]{1,0:T(8,128)(2,1)}, bf16[512,2048]{1,0:T(8,128)(2,1)}, bf16[1024,512]{1,0:T(8,128)(2,1)}, bf1...) custom-call(s32[2]{0:T(128)} %pad_add_fusion.2.refs_0_, ...), custom_call_target="tpu_custom_call" | custom-call | flops 8858370048 | bytes 31457280 | tf_op jit(solution)/shard_map/pallas_call | solution.py:366
  338.4 4.5 collective-permute-start.40
  372.8 7.9 collective-permute-start.36
  405.7 18.9 %all-to-all-done.4 = bf16[4,256,192]{1,2,0:T(8,128)(2,1)} async-done(((bf16[4,256,192]{1,2,0:T(8,128)(2,1)}), bf16[4,256,192]{1,2,0:T(8,128)(2,1)}, u32[]{:S(2)}, u32[]{:S(2)}) %all-to-all-start.4) | async-done | bytes 393248 | tf_op jit(solution)/shard_map/all_to_all | solution.py:29
  425.8 12.2 %shard_map.218 = bf16[1024,576]{1,0:T(8,128)(2,1)S(1)} custom-call(s32[2]{0:T(128)S(1)} %slice_bitcast_fusion.1.ends_ref, bf16[1024,576]{1,0:T(8,128)(2,1)S(1)} %bitcast.272, bf16[1024,192]{1,0:T(8,128)(2,1)S(1)} %bitcast.277), custom_call_target="tpu_custom_call" | custom-call | flops 2013265920 | bytes 3145728 | tf_op jit(solution)/shard_map/pallas_call | solution.py:169
  447.2 6.1 collective-permute-start.44
  481.0 17.2 %collective-permute-done.44 = bf16[192,4096]{1,0:T(8,128)(2,1)} collective-permute-done((bf16[192,4096]{1,0:T(8,128)(2,1)}, bf16[192,4096]{1,0:T(8,128)(2,1)}, u32[]{:S(2)}, u32[]{:S(2)}) %collective-permute-start.44) | collective-permute-done | bytes 1572896 | tf_op jit(solution)/shard_map/ppermute | solution.py:502
  521.6 11.8 %collective-permute-done.47.refs_6_ = bf16[256,768]{1,0:T(8,128)(2,1)S(1)} collective-permute-done((bf16[256,768]{1,0:T(8,128)(2,1)S(1)}, bf16[256,768]{1,0:T(8,128)(2,1)S(1)}, u32[]{:S(2)}, u32[]{:S(2)}) %collective-permute-start.47) | collective-permute-done | bytes 393248 | tf_op jit(solution)/shard_map/ppermute | solution.py:41
  537.8 4.6 all-to-all-start.7
  555.7 23.1 %shard_map.219 = (bf16[512,768]{1,0:T(8,128)(2,1)}, bf16[512,2048]{1,0:T(8,128)(2,1)}, bf16[512,2048]{1,0:T(8,128)(2,1)}, bf16[1024,512]{1,0:T(8,128)(2,1)}, bf1...) custom-call(s32[2]{0:T(128)} %pad_add_fusion.1.refs_0_, ...), custom_call_target="tpu_custom_call" | custom-call | flops 8858370048 | bytes 31457280 | tf_op jit(solution)/shard_map/pallas_call | solution.py:366
  578.8 8.7 collective-permute-start.62
  617.0 6.5 collective-permute-start.66
  623.5 4.9 collective-permute-done.58
  660.4 6.3 collective-permute-start.72
  687.3 11.9 %shard_map.220 = bf16[1024,576]{1,0:T(8,128)(2,1)S(1)} custom-call(s32[2]{0:T(128)S(1)} %slice_bitcast_fusion.1.ends_ref, bf16[1024,576]{1,0:T(8,128)(2,1)S(1)} %bitcast.270, bf16[1024,192]{1,0:T(8,128)(2,1)S(1)} %bitcast.275), custom_call_target="tpu_custom_call" | custom-call | flops 2013265920 | bytes 3145728 | tf_op jit(solution)/shard_map/pallas_call | solution.py:169
  699.2 6.0 collective-permute-start.76
  725.1 29.2 %all-to-all-done.9 = bf16[4,256,576]{1,2,0:T(8,128)(2,1)S(1)} async-done(((bf16[4,256,576]{1,2,0:T(8,128)(2,1)}), bf16[4,256,576]{1,2,0:T(8,128)(2,1)S(1)}, u32[]{:S(2)}, u32[]{:S(2)}) %all-to-all-start.9) | async-done | bytes 1179680 | tf_op jit(solution)/shard_map/all_to_all | solution.py:29
  760.6 6.5 collective-permute-start.85
  788.3 4.5 all-to-all-start.11
  798.3 6.1 collective-permute-start.82
  813.8 7.6 all-to-all-done.11
  825.5 5.8 collective-permute-start.97
  836.3 10.0 %collective-permute-done.97 = bf16[384,1024]{1,0:T(8,128)(2,1)S(1)} collective-permute-done((bf16[384,1024]{1,0:T(8,128)(2,1)}, bf16[384,1024]{1,0:T(8,128)(2,1)S(1)}, u32[]{:S(2)}, u32[]{:S(2)}) %collective-permute-start.97) | collective-permute-done | bytes 786464 | tf_op jit(solution)/shard_map/ppermute | solution.py:502
  847.6 12.1 %collective-permute-done.95 = bf16[1024,768]{1,0:T(8,128)(2,1)S(1)} collective-permute-done((bf16[1024,768]{1,0:T(8,128)(2,1)S(1)}, bf16[1024,768]{1,0:T(8,128)(2,1)S(1)}, u32[]{:S(2)}, u32[]{:S(2)}) %collective-permute-start.95) | collective-permute-done | bytes 1572896 | tf_op jit(solution)/shard_map/ppermute | solution.py:502
  859.9 6.5 collective-permute-start.99
  870.8 11.4 %collective-permute-start.94 = (bf16[96,3200]{1,0:T(8,128)(2,1)S(1)}, bf16[96,3200]{1,0:T(8,128)(2,1)S(1)}, u32[]{:S(2)}, u32[]{:S(2)}) collective-permute-start(bf16[96,3200]{1,0:T(8,128)(2,1)S(1)} %reduce_sum.248), channel_id=1, source_target_pairs={{0,4},{12,8},{1,5},{13,9},{2,6},{14,10},{3,7},{15,11},{16,20},{28,... | collective-permute-start | bytes 1843208 | tf_op jit(solution)/shard_map/ppermute | solution.py:502
  884.1 11.7 %collective-permute-done.94 = bf16[96,3200]{1,0:T(8,128)(2,1)S(1)} collective-permute-done((bf16[96,3200]{1,0:T(8,128)(2,1)S(1)}, bf16[96,3200]{1,0:T(8,128)(2,1)S(1)}, u32[]{:S(2)}, u32[]{:S(2)}) %collective-permute-start.94) | collective-permute-done | bytes 614432 | tf_op jit(solution)/shard_map/ppermute | solution.py:502
  910.1 17.0 %collective-permute-done.100 = bf16[192,4096]{1,0:T(8,128)(2,1)S(1)} collective-permute-done((bf16[192,4096]{1,0:T(8,128)(2,1)S(1)}, bf16[192,4096]{1,0:T(8,128)(2,1)S(1)}, u32[]{:S(2)}, u32[]{:S(2)}) %collective-permute-start.100) | collective-permute-done | bytes 1572896 | tf_op jit(solution)/shard_map/ppermute | solution.py:502
  927.3 6.5 collective-permute-start.105
  942.2 5.3 maximum_convert_fusion
  947.5 8.4 collective-permute-done.106
  962.1 13.6 %collective-permute-done.108 = bf16[96,3200]{1,0:T(8,128)(2,1)S(1)} collective-permute-done((bf16[96,3200]{1,0:T(8,128)(2,1)S(1)}, bf16[96,3200]{1,0:T(8,128)(2,1)S(1)}, u32[]{:S(2)}, u32[]{:S(2)}) %collective-permute-start.108) | collective-permute-done | bytes 614432 | tf_op jit(solution)/shard_map/ppermute | solution.py:502
  (773 shorter events, 479.6 us)
Async XLA Ops:
  17.7 135.5 %collective-permute-start.21 = (bf16[768,4096]{1,0:T(8,128)(2,1)}, bf16[768,4096]{1,0:T(8,128)(2,1)}, u32[]{:S(2)}, u32[]{:S(2)}) collective-permute-start(bf16[768,4096]{1,0:T(8,128)(2,1)} %bitcast.279), channel_id=1, source_target_pairs={{0,16},{16,0},{1,17},{17,1},{2,18},{18,2},{3,19},{19,3},{4,20},{20... | collective-permute-start | bytes 18874376 | tf_op jit(solution)/shard_map/ppermute | solution.py:25
  26.6 108.3 %collective-permute-start.22 = (bf16[2048,768]{1,0:T(8,128)(2,1)}, bf16[2048,768]{1,0:T(8,128)(2,1)}, u32[]{:S(2)}, u32[]{:S(2)}) collective-permute-start(bf16[2048,768]{1,0:T(8,128)(2,1)} %bitcast.288), channel_id=1, source_target_pairs={{0,16},{16,0},{1,17},{17,1},{2,18},{18,2},{3,19},{19,3},{4,20},{20... | collective-permute-start | bytes 9437192 | tf_op jit(solution)/shard_map/ppermute | solution.py:25
  54.4 42.6 %all-to-all-start = ((bf16[4,256,576]{1,2,0:T(8,128)(2,1)}), bf16[4,256,576]{1,2,0:T(8,128)(2,1)S(1)}, u32[]{:S(2)}, u32[]{:S(2)}) async-start(bf16[4,256,576]{1,2,0:T(8,128)(2,1)} %bitcast.17), calls=%async_computation | async-start | bytes 2359296 | tf_op jit(solution)/shard_map/all_to_all | solution.py:29
  59.0 114.6 %all-gather.3.cloned.1.call-start = ((), (), s32[]{:S(2)}) async-start(), calls=%async_computation.12 | async-start | bytes 3072000 | tf_op jit(solution)/shard_map/all_gather | solution.py:701
  204.6 32.6 %all-to-all-start.2 = ((bf16[4,256,576]{1,2,0:T(8,128)(2,1)}), bf16[4,256,576]{1,2,0:T(8,128)(2,1)}, u32[]{:S(2)}, u32[]{:S(2)}) async-start(bf16[4,256,576]{1,2,0:T(8,128)(2,1)} %bitcast.61), calls=%async_computation.2 | async-start | bytes 2359296 | tf_op jit(solution)/shard_map/all_to_all | solution.py:29
  309.2 50.3 %collective-permute-start.35 = (bf16[256,768]{1,0:T(8,128)(2,1)}, bf16[256,768]{1,0:T(8,128)(2,1)}, u32[]{:S(2)}, u32[]{:S(2)}) collective-permute-start(bf16[256,768]{1,0:T(8,128)(2,1)} %get-tuple-element.296), channel_id=1, source_target_pairs={{0,3},{1,2},{2,1},{3,0},{4,7},{5,6},{6,5},{7,4},{8,11},{9,10},{10,... | collective-permute-start | bytes 1179656 | tf_op jit(solution)/shard_map/ppermute | solution.py:46
  310.5 49.1 %collective-permute-start.34 = (bf16[256,768]{1,0:T(8,128)(2,1)}, bf16[256,768]{1,0:T(8,128)(2,1)}, u32[]{:S(2)}, u32[]{:S(2)}) collective-permute-start(bf16[256,768]{1,0:T(8,128)(2,1)} %get-tuple-element.295), channel_id=1, source_target_pairs={{0,2},{1,3},{2,0},{3,1},{4,6},{5,7},{6,4},{7,5},{8,10},{9,11},{10,... | collective-permute-start | bytes 1179656 | tf_op jit(solution)/shard_map/ppermute | solution.py:46
  310.8 50.3 %collective-permute-start.33 = (bf16[256,768]{1,0:T(8,128)(2,1)}, bf16[256,768]{1,0:T(8,128)(2,1)}, u32[]{:S(2)}, u32[]{:S(2)}) collective-permute-start(bf16[256,768]{1,0:T(8,128)(2,1)} %get-tuple-element.294), channel_id=1, source_target_pairs={{0,1},{1,0},{2,3},{3,2},{4,5},{5,4},{6,7},{7,6},{8,9},{9,8},{10,11... | collective-permute-start | bytes 1179656 | tf_op jit(solution)/shard_map/ppermute | solution.py:46
  364.8 33.1 %collective-permute-start.42 = (bf16[384,2048]{1,0:T(8,128)(2,1)}, bf16[384,2048]{1,0:T(8,128)(2,1)}, u32[]{:S(2)}, u32[]{:S(2)}) collective-permute-start(bf16[384,2048]{1,0:T(8,128)(2,1)} %convolution_convert_fusion.6), channel_id=1, source_target_pairs={{0,16},{16,0},{1,17},{17,1},{2,18},{18,2},{3,19},{19,3},{4,20},{20... | collective-permute-start | bytes 4718600 | tf_op jit(solution)/shard_map/ppermute | solution.py:25
  368.6 32.6 %collective-permute-start.41 = (bf16[384,2048]{1,0:T(8,128)(2,1)}, bf16[384,2048]{1,0:T(8,128)(2,1)}, u32[]{:S(2)}, u32[]{:S(2)}) collective-permute-start(bf16[384,2048]{1,0:T(8,128)(2,1)} %convolution_convert_fusion.7), channel_id=1, source_target_pairs={{0,16},{16,0},{1,17},{17,1},{2,18},{18,2},{3,19},{19,3},{4,20},{20... | collective-permute-start | bytes 4718600 | tf_op jit(solution)/shard_map/ppermute | solution.py:25
  372.6 83.9 %collective-permute-start.54 = (bf16[384,1024]{1,0:T(8,128)(2,1)}, bf16[384,1024]{1,0:T(8,128)(2,1)}, u32[]{:S(2)}, u32[]{:S(2)}) collective-permute-start(bf16[384,1024]{1,0:T(8,128)(2,1)} %convolution_convert_fusion.11), channel_id=1, source_target_pairs={{0,16},{16,0},{1,17},{17,1},{2,18},{18,2},{3,19},{19,3},{4,20},{20... | collective-permute-start | bytes 2359304 | tf_op jit(solution)/shard_map/ppermute | solution.py:25
  372.8 73.2 %collective-permute-start.36 = (bf16[256,768]{1,0:T(8,128)(2,1)}, bf16[256,768]{1,0:T(8,128)(2,1)}, u32[]{:S(2)}, u32[]{:S(2)}) collective-permute-start(bf16[256,768]{1,0:T(8,128)(2,1)} %get-tuple-element.594), channel_id=1, source_target_pairs={{0,16},{16,0},{1,17},{17,1},{2,18},{18,2},{3,19},{19,3},{4,20},{20... | collective-permute-start | bytes 1179656 | tf_op jit(solution)/shard_map/ppermute | solution.py:25
  380.8 58.3 %collective-permute-start.43 = (bf16[1024,768]{1,0:T(8,128)(2,1)}, bf16[1024,768]{1,0:T(8,128)(2,1)}, u32[]{:S(2)}, u32[]{:S(2)}) collective-permute-start(bf16[1024,768]{1,0:T(8,128)(2,1)} %add_convert_fusion.17), channel_id=1, source_target_pairs={{0,4},{12,8},{1,5},{13,9},{2,6},{14,10},{3,7},{15,11},{16,20},{28,... | collective-permute-start | bytes 4718600 | tf_op jit(solution)/shard_map/ppermute | solution.py:502
  441.5 34.0 %all-to-all-start.5 = ((bf16[4,256,576]{1,2,0:T(8,128)(2,1)}), bf16[4,256,576]{1,2,0:T(8,128)(2,1)}, u32[]{:S(2)}, u32[]{:S(2)}) async-start(bf16[4,256,576]{1,2,0:T(8,128)(2,1)} %copy.290), calls=%async_computation.5 | async-start | bytes 2359296 | tf_op jit(solution)/shard_map/all_to_all | solution.py:29
  447.2 51.0 %collective-permute-start.44 = (bf16[192,4096]{1,0:T(8,128)(2,1)}, bf16[192,4096]{1,0:T(8,128)(2,1)}, u32[]{:S(2)}, u32[]{:S(2)}) collective-permute-start(bf16[192,4096]{1,0:T(8,128)(2,1)} %get-tuple-element.364), channel_id=1, source_target_pairs={{0,4},{12,8},{1,5},{13,9},{2,6},{14,10},{3,7},{15,11},{16,20},{28,... | collective-permute-start | bytes 4718600 | tf_op jit(solution)/shard_map/ppermute | solution.py:502
  467.5 70.2 %collective-permute-start.52 = (bf16[1024,768]{1,0:T(8,128)(2,1)}, bf16[1024,768]{1,0:T(8,128)(2,1)}, u32[]{:S(2)}, u32[]{:S(2)}) collective-permute-start(bf16[1024,768]{1,0:T(8,128)(2,1)} %add_convert_fusion.14), channel_id=1, source_target_pairs={{4,8},{8,4},{5,9},{9,5},{6,10},{10,6},{7,11},{11,7},{20,24},{24,20... | collective-permute-start | bytes 4718600 | tf_op jit(solution)/shard_map/ppermute | solution.py:502
  469.3 68.4 %collective-permute-start.53 = (bf16[192,4096]{1,0:T(8,128)(2,1)}, bf16[192,4096]{1,0:T(8,128)(2,1)}, u32[]{:S(2)}, u32[]{:S(2)}) collective-permute-start(bf16[192,4096]{1,0:T(8,128)(2,1)} %get-tuple-element.374), channel_id=1, source_target_pairs={{0,4},{12,8},{1,5},{13,9},{2,6},{14,10},{3,7},{15,11},{16,20},{28,... | collective-permute-start | bytes 4718600 | tf_op jit(solution)/shard_map/ppermute | solution.py:502
  475.5 62.3 %all-to-all-start.6 = ((bf16[4,96,1024]{2,1,0:T(8,128)(2,1)}), bf16[4,96,1024]{2,1,0:T(8,128)(2,1)}, u32[]{:S(2)}, u32[]{:S(2)}) async-start(bf16[4,96,1024]{2,1,0:T(8,128)(2,1)} %bitcast.100), calls=%async_computation.6 | async-start | bytes 1572864 | tf_op jit(solution)/shard_map/all_to_all | solution.py:29
  519.8 71.2 %collective-permute-start.55 = (bf16[192,4096]{1,0:T(8,128)(2,1)}, bf16[192,4096]{1,0:T(8,128)(2,1)}, u32[]{:S(2)}, u32[]{:S(2)}) collective-permute-start(bf16[192,4096]{1,0:T(8,128)(2,1)} %add_convert_fusion.13), channel_id=1, source_target_pairs={{4,8},{8,4},{5,9},{9,5},{6,10},{10,6},{7,11},{11,7},{20,24},{24,20... | collective-permute-start | bytes 4718600 | tf_op jit(solution)/shard_map/ppermute | solution.py:502
  533.5 57.5 %collective-permute-start.56 = (bf16[256,768]{1,0:T(8,128)(2,1)}, bf16[256,768]{1,0:T(8,128)(2,1)S(1)}, u32[]{:S(2)}, u32[]{:S(2)}) collective-permute-start(bf16[256,768]{1,0:T(8,128)(2,1)} %fusion.10), channel_id=1, source_target_pairs={{0,4},{12,8},{1,5},{13,9},{2,6},{14,10},{3,7},{15,11},{16,20},{28,... | collective-permute-start | bytes 1179656 | tf_op jit(solution)/shard_map/ppermute | solution.py:502
  537.8 51.1 %all-to-all-start.7 = ((bf16[4,96,3200]{2,1,0:T(8,128)(2,1)}), bf16[4,96,3200]{2,1,0:T(8,128)(2,1)}, u32[]{:S(2)}, u32[]{:S(2)}) async-start(bf16[4,96,3200]{2,1,0:T(8,128)(2,1)} %pad_maximum_fusion.2), calls=%async_computation.7 | async-start | bytes 4915200 | tf_op jit(solution)/shard_map/all_to_all | solution.py:29
  545.7 68.5 %collective-permute-start.60 = (bf16[1024,768]{1,0:T(8,128)(2,1)}, bf16[1024,768]{1,0:T(8,128)(2,1)}, u32[]{:S(2)}, u32[]{:S(2)}) collective-permute-start(bf16[1024,768]{1,0:T(8,128)(2,1)} %add_convert_fusion.12), channel_id=1, source_target_pairs={{4,0},{8,12},{5,1},{9,13},{6,2},{10,14},{7,3},{11,15},{20,16},{24,... | collective-permute-start | bytes 4718600 | tf_op jit(solution)/shard_map/ppermute | solution.py:502
  550.6 64.9 %collective-permute-start.61 = (bf16[192,4096]{1,0:T(8,128)(2,1)}, bf16[192,4096]{1,0:T(8,128)(2,1)}, u32[]{:S(2)}, u32[]{:S(2)}) collective-permute-start(bf16[192,4096]{1,0:T(8,128)(2,1)} %add_convert_fusion.11), channel_id=1, source_target_pairs={{4,8},{8,4},{5,9},{9,5},{6,10},{10,6},{7,11},{11,7},{20,24},{24,20... | collective-permute-start | bytes 4718600 | tf_op jit(solution)/shard_map/ppermute | solution.py:502
  614.2 52.5 %collective-permute-start.64 = (bf16[192,4096]{1,0:T(8,128)(2,1)}, bf16[192,4096]{1,0:T(8,128)(2,1)}, u32[]{:S(2)}, u32[]{:S(2)}) collective-permute-start(bf16[192,4096]{1,0:T(8,128)(2,1)} %add_convert_fusion.9), channel_id=1, source_target_pairs={{4,0},{8,12},{5,1},{9,13},{6,2},{10,14},{7,3},{11,15},{20,16},{24,... | collective-permute-start | bytes 4718600 | tf_op jit(solution)/shard_map/ppermute | solution.py:502
  615.5 43.6 %collective-permute-start.65 = (bf16[256,768]{1,0:T(8,128)(2,1)}, bf16[256,768]{1,0:T(8,128)(2,1)}, u32[]{:S(2)}, u32[]{:S(2)}) collective-permute-start(bf16[256,768]{1,0:T(8,128)(2,1)} %add_convert_fusion.33), channel_id=1, source_target_pairs={{4,8},{8,4},{5,9},{9,5},{6,10},{10,6},{7,11},{11,7},{20,24},{24,20... | collective-permute-start | bytes 1179656 | tf_op jit(solution)/shard_map/ppermute | solution.py:502
  617.0 43.4 %collective-permute-start.66 = (bf16[96,3200]{1,0:T(8,128)(2,1)S(1)}, bf16[96,3200]{1,0:T(8,128)(2,1)}, u32[]{:S(2)}, u32[]{:S(2)}) collective-permute-start(bf16[96,3200]{1,0:T(8,128)(2,1)S(1)} %reduce_sum.240), channel_id=1, source_target_pairs={{0,4},{12,8},{1,5},{13,9},{2,6},{14,10},{3,7},{15,11},{16,20},{28,... | collective-permute-start | bytes 1843208 | tf_op jit(solution)/shard_map/ppermute | solution.py:502
  641.8 31.3 %collective-permute-start.87 = (bf16[384,1024]{1,0:T(8,128)(2,1)}, bf16[384,1024]{1,0:T(8,128)(2,1)}, u32[]{:S(2)}, u32[]{:S(2)}) collective-permute-start(bf16[384,1024]{1,0:T(8,128)(2,1)} %convolution_convert_fusion.10), channel_id=1, source_target_pairs={{0,16},{16,0},{1,17},{17,1},{2,18},{18,2},{3,19},{19,3},{4,20},{20... | collective-permute-start | bytes 2359304 | tf_op jit(solution)/shard_map/ppermute | solution.py:25
  659.1 46.0 %collective-permute-start.70 = (bf16[192,4096]{1,0:T(8,128)(2,1)}, bf16[192,4096]{1,0:T(8,128)(2,1)}, u32[]{:S(2)}, u32[]{:S(2)}) collective-permute-start(bf16[192,4096]{1,0:T(8,128)(2,1)} %add_convert_fusion.6), channel_id=1, source_target_pairs={{4,0},{8,12},{5,1},{9,13},{6,2},{10,14},{7,3},{11,15},{20,16},{24,... | collective-permute-start | bytes 4718600 | tf_op jit(solution)/shard_map/ppermute | solution.py:502
  660.4 44.7 %collective-permute-start.72 = (bf16[1024,768]{1,0:T(8,128)(2,1)}, bf16[1024,768]{1,0:T(8,128)(2,1)}, u32[]{:S(2)}, u32[]{:S(2)}) collective-permute-start(bf16[1024,768]{1,0:T(8,128)(2,1)} %add_convert_fusion.10), channel_id=1, source_target_pairs={{0,4},{12,8},{1,5},{13,9},{2,6},{14,10},{3,7},{15,11},{16,20},{28,... | collective-permute-start | bytes 4718600 | tf_op jit(solution)/shard_map/ppermute | solution.py:502
  671.8 33.3 %collective-permute-start.73 = (bf16[192,4096]{1,0:T(8,128)(2,1)}, bf16[192,4096]{1,0:T(8,128)(2,1)}, u32[]{:S(2)}, u32[]{:S(2)}) collective-permute-start(bf16[192,4096]{1,0:T(8,128)(2,1)} %broadcast_select_fusion.9), channel_id=1, source_target_pairs={{0,16},{1,17},{2,18},{3,19},{4,20},{5,21},{6,22},{7,23},{8,24},{9,... | collective-permute-start | bytes 4718600 | tf_op jit(solution)/shard_map/ppermute | solution.py:502
  685.6 73.0 %collective-permute-start.74 = (bf16[256,768]{1,0:T(8,128)(2,1)}, bf16[256,768]{1,0:T(8,128)(2,1)}, u32[]{:S(2)}, u32[]{:S(2)}) collective-permute-start(bf16[256,768]{1,0:T(8,128)(2,1)} %add_convert_fusion.32), channel_id=1, source_target_pairs={{4,0},{8,12},{5,1},{9,13},{6,2},{10,14},{7,3},{11,15},{20,16},{24,... | collective-permute-start | bytes 1179656 | tf_op jit(solution)/shard_map/ppermute | solution.py:502
  699.2 67.9 %collective-permute-start.76 = (bf16[192,4096]{1,0:T(8,128)(2,1)}, bf16[192,4096]{1,0:T(8,128)(2,1)}, u32[]{:S(2)}, u32[]{:S(2)}) collective-permute-start(bf16[192,4096]{1,0:T(8,128)(2,1)} %get-tuple-element.413), channel_id=1, source_target_pairs={{0,4},{12,8},{1,5},{13,9},{2,6},{14,10},{3,7},{15,11},{16,20},{28,... | collective-permute-start | bytes 4718600 | tf_op jit(solution)/shard_map/ppermute | solution.py:502
  706.6 47.7 %all-to-all-start.9 = ((bf16[4,256,576]{1,2,0:T(8,128)(2,1)}), bf16[4,256,576]{1,2,0:T(8,128)(2,1)S(1)}, u32[]{:S(2)}, u32[]{:S(2)}) async-start(bf16[4,256,576]{1,2,0:T(8,128)(2,1)} %copy.300), calls=%async_computation.9 | async-start | bytes 2359296 | tf_op jit(solution)/shard_map/all_to_all | solution.py:29
  713.1 54.1 %collective-permute-start.77 = (bf16[192,4096]{1,0:T(8,128)(2,1)}, bf16[192,4096]{1,0:T(8,128)(2,1)}, u32[]{:S(2)}, u32[]{:S(2)}) collective-permute-start(bf16[192,4096]{1,0:T(8,128)(2,1)} %broadcast_select_fusion.8), channel_id=1, source_target_pairs={{0,16},{1,17},{2,18},{3,19},{4,20},{5,21},{6,22},{7,23},{8,24},{9,... | collective-permute-start | bytes 4718600 | tf_op jit(solution)/shard_map/ppermute | solution.py:502
  716.4 44.2 %collective-permute-start.75 = (bf16[96,3200]{1,0:T(8,128)(2,1)}, bf16[96,3200]{1,0:T(8,128)(2,1)}, u32[]{:S(2)}, u32[]{:S(2)}) collective-permute-start(bf16[96,3200]{1,0:T(8,128)(2,1)} %add_convert_fusion.27), channel_id=1, source_target_pairs={{4,8},{8,4},{5,9},{9,5},{6,10},{10,6},{7,11},{11,7},{20,24},{24,20... | collective-permute-start | bytes 1843208 | tf_op jit(solution)/shard_map/ppermute | solution.py:502
  720.7 74.5 %collective-permute-start.83 = (bf16[384,1024]{1,0:T(8,128)(2,1)}, bf16[384,1024]{1,0:T(8,128)(2,1)}, u32[]{:S(2)}, u32[]{:S(2)}) collective-permute-start(bf16[384,1024]{1,0:T(8,128)(2,1)} %add_convert_fusion.21), channel_id=1, source_target_pairs={{4,0},{8,12},{5,1},{9,13},{6,2},{10,14},{7,3},{11,15},{20,16},{24,... | collective-permute-start | bytes 2359304 | tf_op jit(solution)/shard_map/ppermute | solution.py:502
  754.3 34.0 %all-to-all-start.10 = ((bf16[4,96,1024]{2,1,0:T(8,128)(2,1)}), bf16[4,96,1024]{2,1,0:T(8,128)(2,1)}, u32[]{:S(2)}, u32[]{:S(2)}) async-start(bf16[4,96,1024]{2,1,0:T(8,128)(2,1)} %bitcast.339), calls=%async_computation.10 | async-start | bytes 1572864 | tf_op jit(solution)/shard_map/all_to_all | solution.py:29
  758.6 37.8 %collective-permute-start.84 = (bf16[1024,768]{1,0:T(8,128)(2,1)}, bf16[1024,768]{1,0:T(8,128)(2,1)}, u32[]{:S(2)}, u32[]{:S(2)}) collective-permute-start(bf16[1024,768]{1,0:T(8,128)(2,1)} %add_convert_fusion.4), channel_id=1, source_target_pairs={{4,8},{8,4},{5,9},{9,5},{6,10},{10,6},{7,11},{11,7},{20,24},{24,20... | collective-permute-start | bytes 4718600 | tf_op jit(solution)/shard_map/ppermute | solution.py:502
  760.6 37.7 %collective-permute-start.85 = (bf16[192,4096]{1,0:T(8,128)(2,1)}, bf16[192,4096]{1,0:T(8,128)(2,1)}, u32[]{:S(2)}, u32[]{:S(2)}) collective-permute-start(bf16[192,4096]{1,0:T(8,128)(2,1)} %get-tuple-element.434), channel_id=1, source_target_pairs={{0,4},{12,8},{1,5},{13,9},{2,6},{14,10},{3,7},{15,11},{16,20},{28,... | collective-permute-start | bytes 4718600 | tf_op jit(solution)/shard_map/ppermute | solution.py:502
  784.0 82.4 %collective-permute-start.79 = (f32[256,768]{1,0:T(8,128)}, f32[256,768]{1,0:T(8,128)}, u32[]{:S(2)}, u32[]{:S(2)}) collective-permute-start(f32[256,768]{1,0:T(8,128)} %get-tuple-element.586), channel_id=1, source_target_pairs={{0,16},{16,0},{1,17},{17,1},{2,18},{18,2},{3,19},{19,3},{4,20},{20... | collective-permute-start | bytes 2359304 | tf_op jit(solution)/shard_map/ppermute | solution.py:25
  788.3 33.0 %all-to-all-start.11 = ((bf16[4,96,3200]{2,1,0:T(8,128)(2,1)}), bf16[4,96,3200]{2,1,0:T(8,128)(2,1)}, u32[]{:S(2)}, u32[]{:S(2)}) async-start(bf16[4,96,3200]{2,1,0:T(8,128)(2,1)} %pad_maximum_fusion.3), calls=%async_computation.11 | async-start | bytes 4915200 | tf_op jit(solution)/shard_map/all_to_all | solution.py:29
  796.4 34.9 %collective-permute-start.81 = (bf16[192,4096]{1,0:T(8,128)(2,1)}, bf16[192,4096]{1,0:T(8,128)(2,1)}, u32[]{:S(2)}, u32[]{:S(2)}) collective-permute-start(bf16[192,4096]{1,0:T(8,128)(2,1)} %add_convert_fusion.5), channel_id=1, source_target_pairs={{4,8},{8,4},{5,9},{9,5},{6,10},{10,6},{7,11},{11,7},{20,24},{24,20... | collective-permute-start | bytes 4718600 | tf_op jit(solution)/shard_map/ppermute | solution.py:502
  823.4 36.3 %collective-permute-start.95 = (bf16[1024,768]{1,0:T(8,128)(2,1)S(1)}, bf16[1024,768]{1,0:T(8,128)(2,1)S(1)}, u32[]{:S(2)}, u32[]{:S(2)}) collective-permute-start(bf16[1024,768]{1,0:T(8,128)(2,1)S(1)} %add_convert_fusion.2), channel_id=1, source_target_pairs={{4,0},{8,12},{5,1},{9,13},{6,2},{10,14},{7,3},{11,15},{20,16},{24,... | collective-permute-start | bytes 4718600 | tf_op jit(solution)/shard_map/ppermute | solution.py:502
  824.7 35.0 %collective-permute-start.96 = (bf16[192,4096]{1,0:T(8,128)(2,1)}, bf16[192,4096]{1,0:T(8,128)(2,1)S(1)}, u32[]{:S(2)}, u32[]{:S(2)}) collective-permute-start(bf16[192,4096]{1,0:T(8,128)(2,1)} %add_convert_fusion.1), channel_id=1, source_target_pairs={{4,8},{8,4},{5,9},{9,5},{6,10},{10,6},{7,11},{11,7},{20,24},{24,20... | collective-permute-start | bytes 4718600 | tf_op jit(solution)/shard_map/ppermute | solution.py:502
  846.3 49.5 %collective-permute-start.92 = (bf16[192,4096]{1,0:T(8,128)(2,1)S(1)}, bf16[192,4096]{1,0:T(8,128)(2,1)S(1)}, u32[]{:S(2)}, u32[]{:S(2)}) collective-permute-start(bf16[192,4096]{1,0:T(8,128)(2,1)S(1)} %add_convert_fusion.3), channel_id=1, source_target_pairs={{4,0},{8,12},{5,1},{9,13},{6,2},{10,14},{7,3},{11,15},{20,16},{24,... | collective-permute-start | bytes 4718600 | tf_op jit(solution)/shard_map/ppermute | solution.py:502
  859.9 35.9 %collective-permute-start.99 = (bf16[1024,768]{1,0:T(8,128)(2,1)S(1)}, bf16[1024,768]{1,0:T(8,128)(2,1)S(1)}, u32[]{:S(2)}, u32[]{:S(2)}) collective-permute-start(bf16[1024,768]{1,0:T(8,128)(2,1)S(1)} %broadcast_select_fusion.10), channel_id=1, source_target_pairs={{16,0},{17,1},{18,2},{19,3},{20,4},{21,5},{22,6},{23,7},{24,8},{25... | collective-permute-start | bytes 4718600 | tf_op jit(solution)/shard_map/ppermute | solution.py:502
  882.8 44.3 %collective-permute-start.100 = (bf16[192,4096]{1,0:T(8,128)(2,1)S(1)}, bf16[192,4096]{1,0:T(8,128)(2,1)S(1)}, u32[]{:S(2)}, u32[]{:S(2)}) collective-permute-start(bf16[192,4096]{1,0:T(8,128)(2,1)S(1)} %add_convert_fusion), channel_id=1, source_target_pairs={{4,0},{8,12},{5,1},{9,13},{6,2},{10,14},{7,3},{11,15},{20,16},{24,... | collective-permute-start | bytes 4718600 | tf_op jit(solution)/shard_map/ppermute | solution.py:502
  902.3 36.2 %collective-permute-start.103 = (bf16[256,768]{1,0:T(8,128)(2,1)S(1)}, bf16[256,768]{1,0:T(8,128)(2,1)S(1)}, u32[]{:S(2)}, u32[]{:S(2)}) collective-permute-start(bf16[256,768]{1,0:T(8,128)(2,1)S(1)} %add_convert_fusion.30), channel_id=1, source_target_pairs={{4,0},{8,12},{5,1},{9,13},{6,2},{10,14},{7,3},{11,15},{20,16},{24,... | collective-permute-start | bytes 1179656 | tf_op jit(solution)/shard_map/ppermute | solution.py:502
  (203 other events, 2514.6 us)
Sparse Core Ops, SparseCore 0:
  97.9 41.2 all-gather.2
